TPU v7x, 32 devices: a whole 2x2x4 slice. The times are simulated.
32 devices in a mesh: dp: 2 (over core), expert: 16 (over z, y, x).
Axes of the slice: x: 2, y: 2, z: 4, core: 2. Of those that a mesh axis runs over, the one named last changes fastest.
Arguments:
- tokens: bfloat16 [2048, 3072], P('expert'), may hold values from -6 to 6
- cotangent: bfloat16 [2048, 3072], P('expert'), may hold values from -6 to 6
- routes: int32 [2048, 2], P('expert'), may hold values from 0 to 15, as said below
- gate_values: float32 [2048, 2], P('expert'), may hold values from 0.1 to 0.9
- weights: bfloat16 [2, 24576, 3, 2, 512], P(None, 'expert', None, 'dp'), may hold values from -0.15625 to 0.15625
Outputs:
- layer_out: bfloat16 [2048, 3072], P('expert')
- input_grad: bfloat16 [2048, 3072], P('expert')
- gate_grad: float32 [2048, 2], P('expert')
- weight_grad: bfloat16 [16, 3072, 3, 2, 512], P('expert', None, None, 'dp')
Inputs may be any that keep to these rules, and one draw needn't show every extreme that they name: `routes`: within the rows of one device, the first id of a token is below 8 and the second is 8 or more, no id appears more than 20 times, and for each of the two columns one id, the same for every device, appears exactly 20 times in the rows of every device.
All inputs are finite; a program needn't handle non-finite values.
Results may differ from a plain program's by a relative error of at most 0.0072.
Values may be sent and summed in bfloat16 or wider, within the bound.
No kernel may reach another device: no remote copies, remote signals or barrier semaphores. Data moves between devices by JAX's collectives and lax.ppermute only.
A program may use at most 128 MiB of HBM per device.

v0:
```python
import functools

import jax
import jax.numpy as jnp
import numpy as np
from jax import lax
from jax.experimental import pallas as pl
from jax.experimental.pallas import tpu as pltpu
from jax.sharding import PartitionSpec as P

F32 = jnp.float32
BF16 = jnp.bfloat16
CHUNKS = 2
VMEM_LIMIT = 40 * 1024 * 1024


def dot(left, right, left_dim, right_dim):
    return lax.dot_general(
        left, right, (((left_dim,), (right_dim,)), ((), ())), preferred_element_type=F32
    )


def params():
    return pltpu.CompilerParams(vmem_limit_bytes=VMEM_LIMIT)


def cost(macs, moved):
    return pl.CostEstimate(flops=2 * macs, bytes_accessed=moved, transcendentals=0)


def iota(shape, dim):
    return lax.broadcasted_iota(jnp.int32, shape, dim)


def split_index(index, size, count):
    whole = jnp.floor((index.astype(F32) + 0.5) * (1.0 / size)).astype(jnp.int32)
    return whole, index - whole * size


def dispatch_kernel(dims, chunk, ids, routes, gates, tokens, cotangent, sent, picks, scales):
    subs, groups, per_chunk, cap, block = dims
    token_count = routes.shape[1]

    @pl.when(pl.program_id(0) == 0)
    def _():
        route = [routes[k : k + 1, :] for k in range(2)]
        gate = [gates[k : k + 1, :] for k in range(2)]
        sub = iota((subs, token_count), 0)
        hits = [(route[k] == sub).astype(F32) for k in range(2)]
        earlier = (iota((token_count,) * 2, 0) < iota((token_count,) * 2, 1)).astype(BF16)
        before = dot((hits[0] + hits[1]).astype(BF16), earlier, 1, 0)
        slot = [jnp.sum(hits[k] * before, axis=0, keepdims=True) for k in range(2)]
        slot[1] = slot[1] + (route[0] == route[1]).astype(F32)
        row = iota((block, token_count), 0)
        row = jnp.where(row >= block // 2, row - block // 2, row)
        local = jnp.zeros_like(row)
        for i in range(1, per_chunk):
            local = local + (row >= i * cap).astype(jnp.int32)
        place = (row - local * cap).astype(F32)
        for e in range(subs // groups):
            wanted = local + (e * groups + chunk * per_chunk)
            match = [(route[k] == wanted) & (slot[k] == place) for k in range(2)]
            scale = jnp.where(match[0], gate[0], 0.0) + jnp.where(match[1], gate[1], 0.0)
            scales[e * block : (e + 1) * block, :] = jnp.broadcast_to(
                jnp.sum(scale, axis=1, keepdims=True), scale.shape
            )
            picks[e * block : (e + 1) * block, :] = (
                match[0].astype(F32) + match[1].astype(F32)
            ).astype(BF16)

    rows = picks[...]
    chosen = dot(rows, tokens[...], 1, 0)
    graded = dot(rows, cotangent[...], 1, 0) * scales[:, :1]
    for e in range(subs // groups):
        part = slice(e * block, (e + 1) * block)
        first = iota((block, 1), 0) < block // 2
        sent[e] = jnp.where(first, chosen[part], graded[part]).astype(BF16)


def quarter(value, groups, width):
    rows = value.shape[0]
    if width % 128 == 0:
        return value, pl.BlockSpec((rows, width), lambda p, ids: (0, 2 * p + ids[0]))
    own = lax.dynamic_index_in_dim(
        value.reshape(rows, groups, 2, width), lax.axis_index("dp"), 2, keepdims=False
    )
    return own.transpose(1, 0, 2), pl.BlockSpec((None, rows, width), lambda p, ids: (p, 0, 0))


def dispatch(dims, chunk, width, ids, routes, gates, tokens, cotangent):
    subs, groups, per_chunk, cap, block = dims
    experts = subs // groups
    token_count = routes.shape[1]
    whole = lambda shape: pl.BlockSpec(shape, lambda p, ids: (0,) * len(shape))
    tokens, tokens_spec = tokens
    cotangent, cotangent_spec = cotangent
    return pl.pallas_call(
        functools.partial(dispatch_kernel, dims, chunk),
        out_shape=jax.ShapeDtypeStruct((experts, groups, block, width), BF16),
        grid_spec=pltpu.PrefetchScalarGridSpec(
            num_scalar_prefetch=1,
            grid=(groups,),
            in_specs=[whole(routes.shape), whole(gates.shape), tokens_spec, cotangent_spec],
            out_specs=pl.BlockSpec((experts, None, block, width), lambda p, ids: (0, p, 0, 0)),
            scratch_shapes=[
                pltpu.VMEM((experts * block, token_count), BF16),
                pltpu.VMEM((experts * block, token_count), F32),
            ],
        ),
        compiler_params=params(),
        cost_estimate=cost(
            2 * experts * block * token_count * width * groups,
            2 * (2 * token_count + experts * block) * width * groups,
        ),
        name=f"dispatch_{chunk}",
    )(ids, routes, gates, tokens, cotangent)


def partial_kernel(dims, ids, own, other, weights, *rest):
    subs, groups, per_chunk, cap, block = dims
    features, partial, held = rest[-3:]
    q = ids[0]
    width = own.shape[1]
    kind = pl.program_id(0)
    sources = subs
    rows = sources * cap

    @pl.when(kind == 0)
    def _():
        source, place = split_index(iota((rows, 1), 0), cap, sources)
        lane = iota((rows, sources * block), 1)
        for half in range(2):
            for i in range(per_chunk):
                target = source * block + (half * per_chunk + i) * cap + place
                chooser = (lane == target).astype(F32).astype(BF16)
                for side, received in enumerate((own, other)):
                    unpacked = dot(chooser, received[...], 1, 0).astype(BF16)
                    held[i, side, half] = unpacked
                    features[i, side, half] = unpacked

    half = jnp.where(kind == 2, 1, 0)
    for i in range(per_chunk):
        total = dot(
            held[i, 0, half], weights[i, pl.ds(pl.multiple_of(q * width, 64), width), :], 1, 0
        )
        total += dot(
            held[i, 1, half], weights[i, pl.ds(pl.multiple_of((1 - q) * width, 64), width), :], 1, 0
        )
        partial[i] = total.astype(BF16)


def partial_products(dims, chunk, ids, own, other, weights, features):
    subs, groups, per_chunk, cap, block = dims
    rows = subs * cap
    width = own.shape[1]
    depth, units = weights.shape[2:]
    whole = lambda shape: pl.BlockSpec(shape, lambda m, ids: (0,) * len(shape))
    feature_shape = (groups, 2, 2, rows, width)
    in_specs = [
        whole(own.shape),
        whole(other.shape),
        pl.BlockSpec((per_chunk, None, depth, units), lambda m, ids: (chunk, m, 0, 0)),
    ]
    operands = [ids, own, other, weights]
    aliases = {}
    if features is not None:
        in_specs.append(pl.BlockSpec(memory_space=pl.ANY))
        operands.append(features)
        aliases = {4: 0}
    return pl.pallas_call(
        functools.partial(partial_kernel, dims),
        out_shape=(
            jax.ShapeDtypeStruct(feature_shape, BF16),
            jax.ShapeDtypeStruct((per_chunk, rows, 3 * units), BF16),
        ),
        grid_spec=pltpu.PrefetchScalarGridSpec(
            num_scalar_prefetch=1,
            grid=(3,),
            in_specs=in_specs,
            out_specs=(
                pl.BlockSpec((per_chunk, 2, 2, rows, width), lambda m, ids: (chunk, 0, 0, 0, 0)),
                pl.BlockSpec((per_chunk, rows, units), lambda m, ids: (0, 0, m)),
            ),
            scratch_shapes=[pltpu.VMEM((per_chunk, 2, 2, rows, width), BF16)],
        ),
        input_output_aliases=aliases,
        compiler_params=params(),
        cost_estimate=cost(
            per_chunk * rows * (3 * depth * units + 4 * subs * block * width),
            2 * per_chunk * (3 * depth * units + 8 * rows * width + 3 * rows * units),
        ),
        name=f"partial_{chunk}",
    )(*operands)


def output_kernel(dims, ids, mine, theirs, weights, *rest):
    per_chunk = dims[2]
    acts, own, other, held = rest[-4:]
    units = weights.shape[3]
    rows = mine.shape[1]
    step = pl.program_id(0)

    @pl.when(step == 0)
    def _():
        for i in range(per_chunk):
            total = lambda m: mine[i, :, m * units : (m + 1) * units].astype(F32) + theirs[
                i, :, m * units : (m + 1) * units
            ].astype(F32)
            gate, up, grad = total(0), total(1), total(2)
            sigmoid = jax.nn.sigmoid(gate)
            active = gate * sigmoid
            values = (
                (grad * up * sigmoid * (1.0 + gate * (1.0 - sigmoid))).astype(BF16),
                (grad * active).astype(BF16),
                (active * up).astype(BF16),
            )
            for m in range(3):
                held[i, m] = values[m]
                acts[i, :, m * units : (m + 1) * units] = values[m]

    def emit(target):
        for i in range(per_chunk):
            target[0, i] = dot(held[i, 2], weights[i, 2], 1, 1).astype(BF16)
            target[1, i] = (
                dot(held[i, 0], weights[i, 0], 1, 1) + dot(held[i, 1], weights[i, 1], 1, 1)
            ).astype(BF16)

    pl.when(step == 0)(lambda: emit(other))
    pl.when(step == 1)(lambda: emit(own))


def output_products(dims, chunk, ids, mine, theirs, weights, acts):
    subs, groups, per_chunk, cap, block = dims
    rows = subs * cap
    depth, units = weights.shape[2:]
    width = depth // 2
    whole = lambda shape: pl.BlockSpec(shape, lambda s, ids: (0,) * len(shape))
    in_specs = [
        whole(mine.shape),
        whole(theirs.shape),
        pl.BlockSpec(
            (per_chunk, 3, width, units),
            lambda s, ids: (chunk, 0, jnp.where(s == 0, 1 - ids[0], ids[0]), 0),
        ),
    ]
    operands = [ids, mine, theirs, weights]
    aliases = {}
    if acts is not None:
        in_specs.append(pl.BlockSpec(memory_space=pl.ANY))
        operands.append(acts)
        aliases = {4: 0}
    out = jax.ShapeDtypeStruct((2, per_chunk, rows, width), BF16)
    return pl.pallas_call(
        functools.partial(output_kernel, dims),
        out_shape=(jax.ShapeDtypeStruct((groups, rows, 3 * units), BF16), out, out),
        grid_spec=pltpu.PrefetchScalarGridSpec(
            num_scalar_prefetch=1,
            grid=(2,),
            in_specs=in_specs,
            out_specs=(
                pl.BlockSpec((per_chunk, rows, 3 * units), lambda s, ids: (chunk, 0, 0)),
                whole(out.shape),
                whole(out.shape),
            ),
            scratch_shapes=[pltpu.VMEM((per_chunk, 3, rows, units), BF16)],
        ),
        input_output_aliases=aliases,
        compiler_params=params(),
        cost_estimate=cost(
            per_chunk * rows * 3 * depth * units,
            2 * per_chunk * (3 * depth * units + 2 * rows * depth + 9 * rows * units),
        ),
        name=f"output_{chunk}",
    )(*operands)


def pack_kernel(dims, own, arrived, packed):
    subs, groups, per_chunk, cap, block = dims
    rows = own.shape[2]
    source, place = split_index(iota((subs * block, 1), 0), block, subs)
    lane = iota((subs * block, rows), 1)
    total = None
    for half in range(2):
        for i in range(per_chunk):
            start = (half * per_chunk + i) * cap
            inside = (place >= start) & (place < start + cap)
            target = jnp.where(inside, source * cap + place - start, -1)
            chooser = (lane == target).astype(F32).astype(BF16)
            summed = (own[half, i].astype(F32) + arrived[half, i].astype(F32)).astype(BF16)
            term = dot(chooser, summed, 1, 0)
            total = term if total is None else total + term
    packed[...] = total.astype(BF16)


def pack(dims, chunk, own, arrived):
    subs, groups, per_chunk, cap, block = dims
    rows = subs * cap
    width = own.shape[3]
    columns = 256 if width % 256 == 0 else width
    spec = pl.BlockSpec((2, per_chunk, rows, columns), lambda c: (0, 0, 0, c))
    return pl.pallas_call(
        functools.partial(pack_kernel, dims),
        out_shape=jax.ShapeDtypeStruct((subs * block, width), BF16),
        grid=(width // columns,),
        in_specs=[spec, spec],
        out_specs=pl.BlockSpec((subs * block, columns), lambda c: (0, c)),
        compiler_params=params(),
        cost_estimate=cost(
            subs * block * 2 * per_chunk * rows * width, 6 * subs * block * width
        ),
        name=f"pack_{chunk}",
    )(own, arrived)


def chooser_kernel(dims, ids, routes, marks, *choosers):
    subs, groups, per_chunk, cap, block = dims
    token_count = routes.shape[0]
    p = pl.program_id(0)
    route = [routes[:, k : k + 1] for k in range(2)]
    sub = iota((token_count, subs), 1)
    hits = [(route[k] == sub).astype(F32) for k in range(2)]
    earlier = (iota((token_count,) * 2, 1) < iota((token_count,) * 2, 0)).astype(BF16)
    before = dot(earlier, (hits[0] + hits[1]).astype(BF16), 1, 0)
    slot = [jnp.sum(hits[k] * before, axis=1, keepdims=True) for k in range(2)]
    slot[1] = slot[1] + (route[0] == route[1]).astype(F32)
    slot = [value.astype(jnp.int32) for value in slot]
    for chunk in range(CHUNKS):
        wanted = marks[0:1, :] + chunk * per_chunk
        place, half, holder = marks[1:2, :], marks[2:3, :], marks[3:4, :]
        match = [
            ((route[k] == wanted) & (slot[k] == place) & (holder == p)).astype(F32)
            for k in range(2)
        ]
        first = (half == 0).astype(F32)
        second = (half == 1).astype(F32)
        choosers[chunk][0:token_count, :] = (match[0] * first).astype(BF16)
        choosers[chunk][token_count : 2 * token_count, :] = (match[1] * first).astype(BF16)
        choosers[chunk][2 * token_count :, :] = ((match[0] + match[1]) * second).astype(BF16)


def return_choosers(dims, ids, routes):
    subs, groups, per_chunk, cap, block = dims
    token_count = routes.shape[0]
    row = np.arange(subs * block)
    device, inner = row // block, row % block
    half, inner = inner // (per_chunk * cap), inner % (per_chunk * cap)
    local, place = inner // cap, inner % cap
    marks = np.zeros((8, subs * block), np.int32)
    marks[0] = device // groups * groups + local
    marks[1] = place
    marks[2] = half
    marks[3] = device % groups
    whole = lambda shape: pl.BlockSpec(shape, lambda p, ids: (0,) * len(shape))
    shape = jax.ShapeDtypeStruct((groups, 3 * token_count, subs * block), BF16)
    spec = pl.BlockSpec((None, 3 * token_count, subs * block), lambda p, ids: (p, 0, 0))
    return pl.pallas_call(
        functools.partial(chooser_kernel, dims),
        out_shape=(shape,) * CHUNKS,
        grid_spec=pltpu.PrefetchScalarGridSpec(
            num_scalar_prefetch=1,
            grid=(groups,),
            in_specs=[whole(routes.shape), whole(marks.shape)],
            out_specs=(spec,) * CHUNKS,
        ),
        compiler_params=params(),
        cost_estimate=cost(0, 2 * CHUNKS * groups * 3 * token_count * subs * block),
        name="choosers",
    )(ids, routes, jnp.asarray(marks))


def combine_kernel(ids, gates, cotangent, *rest):
    choosers = rest[:CHUNKS]
    returned = rest[CHUNKS : 2 * CHUNKS]
    combined, gate_grad = rest[2 * CHUNKS :]
    token_count = gates.shape[0]
    p = pl.program_id(0)
    total = dot(choosers[0][...], returned[0][...], 1, 0)
    for chunk in range(1, CHUNKS):
        total += dot(choosers[chunk][...], returned[chunk][...], 1, 0)
    picked = [total[k * token_count : (k + 1) * token_count] for k in range(3)]
    combined[0] = (gates[:, 0:1] * picked[0] + gates[:, 1:2] * picked[1]).astype(BF16)
    combined[1] = picked[2].astype(BF16)
    grads = cotangent[...].astype(F32)
    lane = iota((token_count, 128), 1)
    term = jnp.where(lane == 0, jnp.sum(grads * picked[0], axis=1, keepdims=True), 0.0)
    term += jnp.where(lane == 1, jnp.sum(grads * picked[1], axis=1, keepdims=True), 0.0)

    @pl.when(p == 0)
    def _():
        gate_grad[...] = term

    @pl.when(p > 0)
    def _():
        gate_grad[...] += term


def combine(dims, width, ids, gates, cotangent, choosers, returned):
    subs, groups, per_chunk, cap, block = dims
    token_count = gates.shape[0]
    cotangent, cotangent_spec = cotangent
    whole = lambda shape: pl.BlockSpec(shape, lambda p, ids: (0,) * len(shape))
    chooser_spec = pl.BlockSpec((None, 3 * token_count, subs * block), lambda p, ids: (p, 0, 0))
    return pl.pallas_call(
        combine_kernel,
        out_shape=(
            jax.ShapeDtypeStruct((2, groups, token_count, width), BF16),
            jax.ShapeDtypeStruct((token_count, 128), F32),
        ),
        grid_spec=pltpu.PrefetchScalarGridSpec(
            num_scalar_prefetch=1,
            grid=(groups,),
            in_specs=[whole(gates.shape), cotangent_spec]
            + [chooser_spec] * CHUNKS
            + [whole(returned[0].shape)] * CHUNKS,
            out_specs=(
                pl.BlockSpec((2, None, token_count, width), lambda p, ids: (0, p, 0, 0)),
                whole((token_count, 128)),
            ),
        ),
        compiler_params=params(),
        cost_estimate=cost(
            CHUNKS * groups * 3 * token_count * subs * block * width,
            2 * CHUNKS * subs * block * (width + 3 * groups * token_count),
        ),
        name="combine",
    )(ids, gates, cotangent, *choosers, *returned)


def merge_kernel(ids, own, other, layer_out, input_grad):
    side = pl.program_id(1)

    @pl.when(side == 0)
    def _():
        layer_out[...] = own[0]
        input_grad[...] = own[1]

    @pl.when(side == 1)
    def _():
        layer_out[...] = other[0]
        input_grad[...] = other[1]


def merge(ids, own, other):
    _, groups, token_count, width = own.shape
    model_width = 2 * groups * width
    if width % 128:
        q = lax.axis_index("dp")
        pair = jnp.stack([jnp.where(q == 0, own, other), jnp.where(q == 0, other, own)], axis=2)
        pair = pair.transpose(0, 3, 1, 2, 4).reshape(2, token_count, model_width)
        return pair[0], pair[1]
    in_spec = pl.BlockSpec((2, None, token_count, width), lambda p, s, ids: (0, p, 0, 0))
    out_spec = pl.BlockSpec(
        (token_count, width), lambda p, s, ids: (0, 2 * p + jnp.where(s == 0, ids[0], 1 - ids[0]))
    )
    shape = jax.ShapeDtypeStruct((token_count, model_width), BF16)
    return pl.pallas_call(
        merge_kernel,
        out_shape=(shape, shape),
        grid_spec=pltpu.PrefetchScalarGridSpec(
            num_scalar_prefetch=1,
            grid=(groups, 2),
            in_specs=[in_spec, in_spec],
            out_specs=(out_spec, out_spec),
        ),
        compiler_params=params(),
        cost_estimate=cost(0, 8 * token_count * model_width),
        name="merge",
    )(ids, own, other)


def weight_grad_kernel(count, ids, acts, *rest):
    features, grads = rest[:-1], rest[-1]
    units = acts.shape[1] // 3
    step = pl.program_id(0)
    for index in range(count):

        @pl.when(step == index)
        def _(index=index):
            both = dot(features[index][0], acts[:, : 2 * units], 0, 0).astype(BF16)
            grads[0] = both[:, :units]
            grads[1] = both[:, units:]
            grads[2] = dot(features[index][1], acts[:, 2 * units :], 0, 0).astype(BF16)


def weight_grads(ids, acts, features, far):
    groups, _, _, rows, width = features.shape
    units = acts.shape[2] // 3
    operands = [features, features]
    specs = [
        pl.BlockSpec((None, None, 2, rows, width), lambda s, ids: (ids[1], 0, 0, 0, 0)),
        pl.BlockSpec((None, None, 2, rows, width), lambda s, ids: (ids[1], 1, 0, 0, 0)),
    ]
    for own, other in far:
        operands += [own, other]
        specs += [pl.BlockSpec(own.shape, lambda s, ids: (0, 0, 0))] * 2
    steps = len(operands)

    def target(s, ids):
        holder = ids[1] ^ (s // 2)
        side = jnp.where(s % 2 == 0, ids[0], 1 - ids[0])
        return 0, 2 * holder + side, 0

    return pl.pallas_call(
        functools.partial(weight_grad_kernel, steps),
        out_shape=jax.ShapeDtypeStruct((3, steps * width, units), BF16),
        grid_spec=pltpu.PrefetchScalarGridSpec(
            num_scalar_prefetch=1,
            grid=(steps,),
            in_specs=[pl.BlockSpec((None, rows, 3 * units), lambda s, ids: (ids[1], 0, 0))]
            + specs,
            out_specs=pl.BlockSpec((3, width, units), target),
        ),
        compiler_params=params(),
        cost_estimate=cost(
            3 * rows * steps * width * units, 6 * steps * width * units + 4 * steps * rows * width
        ),
        name="weight_grads",
    )(ids, acts, *operands)


def swap_cores(value):
    return lax.ppermute(value, "dp", [(0, 1), (1, 0)])


def swap_holders(value, mask):
    size = lax.axis_size("expert")
    return lax.ppermute(value, "expert", [(source, source ^ mask) for source in range(size)])


def shards(tokens, cotangent, routes, gate_values, weights):
    groups, depth = weights.shape[:2]
    token_count, top_count = routes.shape
    subs = lax.axis_size("expert")
    cap = 5 * token_count * top_count // (4 * subs)
    per_chunk = groups // CHUNKS
    block = 2 * per_chunk * cap
    width = depth // 2
    dims = (subs, groups, per_chunk, cap, block)
    core = lax.axis_index("dp")
    holder = lax.axis_index("expert") % groups
    ids = jnp.stack([core, holder]).astype(jnp.int32)
    weights = weights[:, :, :, 0, :].transpose(0, 2, 1, 3)
    own_tokens = quarter(tokens, groups, width)
    own_cotangent = quarter(cotangent, groups, width)

    def exchange(rows):
        blocks = rows.reshape(subs, block, width)
        moved = lax.all_to_all(blocks, "expert", split_axis=0, concat_axis=0, tiled=True)
        return moved.reshape(subs * block, width)

    sent = [
        dispatch(dims, c, width, ids, routes.T, gate_values.T, own_tokens, own_cotangent)
        for c in range(CHUNKS)
    ]
    choosers = return_choosers(dims, ids, routes)
    arrived = [exchange(value) for value in sent]
    features = acts = None
    partials = []
    for c in range(CHUNKS):
        features, partial = partial_products(
            dims, c, ids, arrived[c], swap_cores(arrived[c]), weights, features
        )
        partials.append(partial)
    returned = []
    for c in range(CHUNKS):
        mine, mask = partials[c], 1
        while mask < groups // 2:
            mine = (mine.astype(F32) + swap_holders(mine, mask).astype(F32)).astype(BF16)
            mask *= 2
        acts, own, other = output_products(
            dims, c, ids, mine, swap_holders(mine, mask), weights, acts
        )
        returned.append(exchange(pack(dims, c, own, swap_cores(other))))
    far = []
    for mask in range(1, groups):
        near = swap_holders(
            lax.dynamic_index_in_dim(features, holder ^ mask, 0, keepdims=False)[0], mask
        )
        far.append((near, swap_cores(near)))
    weight_grad = weight_grads(ids, acts, features, far)
    combined, gate_part = combine(
        dims, width, ids, gate_values, own_cotangent, choosers, returned
    )
    layer_out, input_grad = merge(ids, combined, swap_cores(combined))
    gate_grad = (gate_part + swap_cores(gate_part))[:, :top_count]
    weight_grad = weight_grad.transpose(1, 0, 2).reshape(1, groups * depth, 3, 1, -1)
    return layer_out, input_grad, gate_grad, weight_grad


def solution(mesh):
    in_specs = (
        P("expert", None),
        P("expert", None),
        P("expert", None),
        P("expert", None),
        P(None, "expert", None, "dp", None),
    )
    out_specs = (
        P("expert", None),
        P("expert", None),
        P("expert", None),
        P("expert", None, None, "dp", None),
    )
    return jax.shard_map(shards, mesh=mesh, in_specs=in_specs, out_specs=out_specs, check_vma=False)
```

profile of v0, /device:TPU:17, one launch (start us, length us, event | category | flops | bytes accessed | tf_op | source)
XLA Modules:
  0.0 208.2 jit_solution(8176783741405179732)
XLA Ops:
  4.4 2.5 %dispatch_0.1 = bf16[8,2,40,768]{3,2,1,0:T(8,128)(2,1)} custom-call(s32[2]{0:T(128)S(1)} %pad_add_fusion.ids, s32[2,128]{1,0:T(2,128)S(1)} %bitcast.26, f32[2,128]{1,0:T(2,128)S(1)} %bitcast.28, bf16[128,3072]{1,0:T(8,128)(2,1)S(1)} %copy-done.4, bf16[128,3072]{1,0:T(8,128)(2,1)S(1)} %copy-done.6), custom_call_target="tpu_custom_call" | custom-call | flops 251658240 | bytes 1769472 | tf_op jit(solution)/shard_map/dispatch_0/pallas_call | solution.py:97
  6.9 6.5 %all-to-all-start = ((bf16[16,40,768]{2,1,0:T(8,128)(2,1)}), bf16[16,40,768]{2,1,0:T(8,128)(2,1)S(1)}, u32[]{:S(2)}, u32[]{:S(2)}) async-start(bf16[16,40,768]{2,1,0:T(8,128)(2,1)} %bitcast.4), calls=%async_computation | async-start | bytes 1966080 | tf_op jit(solution)/shard_map/all_to_all | solution.py:548
  13.5 2.6 %dispatch_1.1 = bf16[8,2,40,768]{3,2,1,0:T(8,128)(2,1)} custom-call(s32[2]{0:T(128)S(1)} %pad_add_fusion.ids, s32[2,128]{1,0:T(2,128)S(1)} %bitcast.27, f32[2,128]{1,0:T(2,128)S(1)} %bitcast.29, bf16[128,3072]{1,0:T(8,128)(2,1)S(1)} %copy-done.5, bf16[128,3072]{1,0:T(8,128)(2,1)S(1)} %copy-done.7), custom_call_target="tpu_custom_call" | custom-call | flops 251658240 | bytes 1769472 | tf_op jit(solution)/shard_map/dispatch_1/pallas_call | solution.py:97
  16.1 20.0 %all-to-all-done = bf16[16,40,768]{2,1,0:T(8,128)(2,1)S(1)} async-done(((bf16[16,40,768]{2,1,0:T(8,128)(2,1)}), bf16[16,40,768]{2,1,0:T(8,128)(2,1)S(1)}, u32[]{:S(2)}, u32[]{:S(2)}) %all-to-all-start) | async-done | bytes 983072 | tf_op jit(solution)/shard_map/all_to_all | solution.py:548
  36.0 4.9 %all-to-all-start.2 = ((bf16[16,40,768]{2,1,0:T(8,128)(2,1)}), bf16[16,40,768]{2,1,0:T(8,128)(2,1)S(1)}, u32[]{:S(2)}, u32[]{:S(2)}) async-start(bf16[16,40,768]{2,1,0:T(8,128)(2,1)} %bitcast.10), calls=%async_computation.2 | async-start | bytes 1966080 | tf_op jit(solution)/shard_map/all_to_all | solution.py:548
  40.9 2.6 %collective-permute-start = (bf16[640,768]{1,0:T(8,128)(2,1)S(1)}, bf16[640,768]{1,0:T(8,128)(2,1)S(1)}, u32[]{:S(2)}, u32[]{:S(2)}) collective-permute-start(bf16[640,768]{1,0:T(8,128)(2,1)S(1)} %bitcast.24), channel_id=1, source_target_pairs={{0,16},{16,0},{1,17},{17,1},{2,18},{18,2},{3,19},{19,3},{4,20},{20... | collective-permute-start | bytes 2949128 | tf_op jit(solution)/shard_map/ppermute | solution.py:522
  43.6 2.2 %collective-permute-done.other = bf16[640,768]{1,0:T(8,128)(2,1)S(1)} collective-permute-done((bf16[640,768]{1,0:T(8,128)(2,1)S(1)}, bf16[640,768]{1,0:T(8,128)(2,1)S(1)}, u32[]{:S(2)}, u32[]{:S(2)}) %collective-permute-start) | collective-permute-done | bytes 983072 | tf_op jit(solution)/shard_map/ppermute | solution.py:522
  45.7 6.4 %partial_0.1 = (bf16[2,2,2,320,768]{4,3,2,1,0:T(8,128)(2,1)S(1)}, bf16[1,320,1536]{2,1,0:T(8,128)(2,1)S(1)}) custom-call(s32[2]{0:T(128)S(1)} %pad_add_fusion.ids, bf16[640,768]{1,0:T(8,128)(2,1)S(1)} %bitcast.25, bf16[640,768]{1,0:T(8,128)(2,1)S(1)} %collective-permute-done.other, bf16[2,3,1536,512]{3,2,1,0:T(8,128)(2,1)} %bitcast.30), custom_call_target="tpu_custom_call" | custom-call | flops 2768240640 | bytes 9633792 | tf_op jit(solution)/shard_map/partial_0/pallas_call | solution.py:170
  56.3 7.5 %all-to-all-done.2 = bf16[16,40,768]{2,1,0:T(8,128)(2,1)S(1)} async-done(((bf16[16,40,768]{2,1,0:T(8,128)(2,1)}), bf16[16,40,768]{2,1,0:T(8,128)(2,1)S(1)}, u32[]{:S(2)}, u32[]{:S(2)}) %all-to-all-start.2) | async-done | bytes 983072 | tf_op jit(solution)/shard_map/all_to_all | solution.py:548
  65.3 17.4 %collective-permute-done.1.theirs = bf16[1,320,1536]{2,1,0:T(8,128)(2,1)S(1)} collective-permute-done((bf16[1,320,1536]{2,1,0:T(8,128)(2,1)S(1)}, bf16[1,320,1536]{2,1,0:T(8,128)(2,1)S(1)}, u32[]{:S(2)}, u32[]{:S(2)}) %collective-permute-start.1) | collective-permute-done | bytes 983072 | tf_op jit(solution)/shard_map/ppermute | solution.py:527
  86.0 4.4 %output_0.1 = (bf16[2,320,1536]{2,1,0:T(8,128)(2,1)S(1)}, bf16[2,1,320,768]{3,2,1,0:T(8,128)(2,1)S(1)}, bf16[2,1,320,768]{3,2,1,0:T(8,128)(2,1)S(1)}) custom-call(s32[2]{0:T(128)S(1)} %pad_add_fusion.ids, bf16[1,320,1536]{2,1,0:T(8,128)(2,1)S(1)} %copy-done.10, bf16[1,320,1536]{2,1,0:T(8,128)(2,1)S(1)} %copy-done.12, bf16[2,3,1536,512]{3,2,1,0:T(8,128)(2,1)} %bitcast.31), custom_call_target="tpu_custom_call" | custom-call | flops 1509949440 | bytes 9633792 | tf_op jit(solution)/shard_map/output_0/pallas_call | solution.py:253
  91.0 7.3 %partial_1.1 = (bf16[2,2,2,320,768]{4,3,2,1,0:T(8,128)(2,1)S(1)}, bf16[1,320,1536]{2,1,0:T(8,128)(2,1)}) custom-call(s32[2]{0:T(128)S(1)} %pad_add_fusion.ids, bf16[640,768]{1,0:T(8,128)(2,1)S(1)} %bitcast.23, bf16[640,768]{1,0:T(8,128)(2,1)S(1)} %collective-permute-done.3.other, ...), custom_call_target="tpu_custom_call", output_to_operand_aliasing={{0}: (4, {})} | custom-call | flops 2768240640 | bytes 9633792 | tf_op jit(solution)/shard_map/partial_1/pallas_call | solution.py:170
  98.3 1.9 copy-done.2
  100.4 2.9 %pack_0.1 = bf16[640,768]{1,0:T(8,128)(2,1)} custom-call(bf16[2,1,320,768]{3,2,1,0:T(8,128)(2,1)S(1)} %get-tuple-element.23.own, bf16[2,1,320,768]{3,2,1,0:T(8,128)(2,1)S(1)} %collective-permute-done.2.arrived), custom_call_target="tpu_custom_call" | custom-call | flops 629145600 | bytes 2949120 | tf_op jit(solution)/shard_map/pack_0/pallas_call | solution.py:301
  103.3 5.5 %all-to-all-start.1 = ((bf16[16,40,768]{2,1,0:T(8,128)(2,1)}), bf16[16,40,768]{2,1,0:T(8,128)(2,1)}, u32[]{:S(2)}, u32[]{:S(2)}) async-start(bf16[16,40,768]{2,1,0:T(8,128)(2,1)} %bitcast.8), calls=%async_computation.1 | async-start | bytes 1966080 | tf_op jit(solution)/shard_map/all_to_all | solution.py:548
  108.8 22.8 %collective-permute-done.4.theirs = bf16[1,320,1536]{2,1,0:T(8,128)(2,1)S(1)} collective-permute-done((bf16[1,320,1536]{2,1,0:T(8,128)(2,1)}, bf16[1,320,1536]{2,1,0:T(8,128)(2,1)S(1)}, u32[]{:S(2)}, u32[]{:S(2)}) %collective-permute-start.4) | collective-permute-done | bytes 983072 | tf_op jit(solution)/shard_map/ppermute | solution.py:527
  131.6 4.6 %output_1.1 = (bf16[2,320,1536]{2,1,0:T(8,128)(2,1)S(1)}, bf16[2,1,320,768]{3,2,1,0:T(8,128)(2,1)S(1)}, bf16[2,1,320,768]{3,2,1,0:T(8,128)(2,1)S(1)}) custom-call(s32[2]{0:T(128)S(1)} %pad_add_fusion.ids, bf16[1,320,1536]{2,1,0:T(8,128)(2,1)} %get-tuple-element.26.mine, ...), custom_call_target="tpu_custom_call", output_to_operand_aliasing={{0}: (4, {})} | custom-call | flops 1509949440 | bytes 9633792 | tf_op jit(solution)/shard_map/output_1/pallas_call | solution.py:253
  137.6 2.2 %collective-permute-done.5.arrived = bf16[2,1,320,768]{3,2,1,0:T(8,128)(2,1)S(1)} collective-permute-done((bf16[2,1,320,768]{3,2,1,0:T(8,128)(2,1)S(1)}, bf16[2,1,320,768]{3,2,1,0:T(8,128)(2,1)S(1)}, u32[]{:S(2)}, u32[]{:S(2)}) %collective-permute-start.5) | collective-permute-done | bytes 983072 | tf_op jit(solution)/shard_map/ppermute | solution.py:522
  139.8 2.9 %pack_1.1 = bf16[640,768]{1,0:T(8,128)(2,1)} custom-call(bf16[2,1,320,768]{3,2,1,0:T(8,128)(2,1)S(1)} %get-tuple-element.28.own, bf16[2,1,320,768]{3,2,1,0:T(8,128)(2,1)S(1)} %collective-permute-done.5.arrived), custom_call_target="tpu_custom_call" | custom-call | flops 629145600 | bytes 2949120 | tf_op jit(solution)/shard_map/pack_1/pallas_call | solution.py:301
  142.7 5.2 %all-to-all-start.3 = ((bf16[16,40,768]{2,1,0:T(8,128)(2,1)}), bf16[16,40,768]{2,1,0:T(8,128)(2,1)}, u32[]{:S(2)}, u32[]{:S(2)}) async-start(bf16[16,40,768]{2,1,0:T(8,128)(2,1)} %bitcast.13), calls=%async_computation.3 | async-start | bytes 1966080 | tf_op jit(solution)/shard_map/all_to_all | solution.py:548
  150.4 30.7 %collective-permute-done.8.rest_2_ = bf16[2,320,768]{2,1,0:T(8,128)(2,1)} collective-permute-done((bf16[2,320,768]{2,1,0:T(8,128)(2,1)S(1)}, bf16[2,320,768]{2,1,0:T(8,128)(2,1)}, u32[]{:S(2)}, u32[]{:S(2)}) %collective-permute-start.8) | collective-permute-done | bytes 983072 | tf_op jit(solution)/shard_map/ppermute | solution.py:527
  190.8 4.5 %combine.1 = (bf16[2,2,128,768]{3,2,1,0:T(8,128)(2,1)S(1)}, f32[128,128]{1,0:T(8,128)S(1)}) custom-call(s32[2]{0:T(128)S(1)} %pad_add_fusion.ids, f32[128,2]{1,0:T(8,128)S(1)} %copy-done.13, bf16[128,3072]{1,0:T(8,128)(2,1)S(1)} %copy-done.8, bf16[2,384,640]{2,1,0:T(8,128)(2,1)S(1)} %copy-done.20, bf16[2,384,640]{2,1,0:T(8,128)(2,1)S(1)} %copy-done.22, ...), custom_call_target="tpu_custom_call" | custom-call | flops 1509949440 | bytes 3932160 | tf_op jit(solution)/shard_map/combine/pallas_call | solution.py:403
  195.9 9.3 %weight_grads.1 = bf16[3,3072,512]{2,1,0:T(8,128)(2,1)} custom-call(s32[2]{0:T(128)S(1)} %pad_add_fusion.ids, bf16[2,320,1536]{2,1,0:T(8,128)(2,1)S(1)} %get-tuple-element.34.acts, bf16[2,2,2,320,768]{4,3,2,1,0:T(8,128)(2,1)S(1)} %copy-done.3, bf16[2,2,2,320,768]{4,3,2,1,0:T(8,128)(2,1)S(1)} %copy-done.3, ...), custom_call_target="tpu_custom_call" | custom-call | flops 3019898880 | bytes 13369344 | tf_op jit(solution)/shard_map/weight_grads/pallas_call | solution.py:503
  205.9 2.3 %merge.1 = (bf16[128,3072]{1,0:T(8,128)(2,1)}, bf16[128,3072]{1,0:T(8,128)(2,1)}) custom-call(s32[2]{0:T(128)S(1)} %pad_add_fusion.ids, bf16[2,2,128,768]{3,2,1,0:T(8,128)(2,1)S(1)} %get-tuple-element.30.own, bf16[2,2,128,768]{3,2,1,0:T(8,128)(2,1)S(1)} %collective-permute-done.6.other), custom_call_target="tpu_custom_call" | custom-call | bytes 3145728 | tf_op jit(solution)/shard_map/merge/pallas_call | solution.py:456
  (68 shorter events, 28.2 us)
Async XLA Ops:
  0.6 12.8 %copy-start.16 = (s32[128,2]{0,1:T(2,128)S(1)}, s32[128,2]{0,1:T(2,128)}, u32[]{:S(2)}) copy-start(s32[128,2]{0,1:T(2,128)} %param.8) | copy-start | bytes 3076
  4.4 9.1 %copy-start.5 = (bf16[128,3072]{1,0:T(8,128)(2,1)S(1)}, bf16[128,3072]{1,0:T(8,128)(2,1)}, u32[]{:S(2)}) copy-start(bf16[128,3072]{1,0:T(8,128)(2,1)} %tokens.3) | copy-start | bytes 2359300
  4.4 9.1 %copy-start.7 = (bf16[128,3072]{1,0:T(8,128)(2,1)S(1)}, bf16[128,3072]{1,0:T(8,128)(2,1)}, u32[]{:S(2)}) copy-start(bf16[128,3072]{1,0:T(8,128)(2,1)} %cotangent.5) | copy-start | bytes 2359300
  6.9 29.1 %all-to-all-start = ((bf16[16,40,768]{2,1,0:T(8,128)(2,1)}), bf16[16,40,768]{2,1,0:T(8,128)(2,1)S(1)}, u32[]{:S(2)}, u32[]{:S(2)}) async-start(bf16[16,40,768]{2,1,0:T(8,128)(2,1)} %bitcast.4), calls=%async_computation | async-start | bytes 1966080 | tf_op jit(solution)/shard_map/all_to_all | solution.py:548
  36.0 27.7 %all-to-all-start.2 = ((bf16[16,40,768]{2,1,0:T(8,128)(2,1)}), bf16[16,40,768]{2,1,0:T(8,128)(2,1)S(1)}, u32[]{:S(2)}, u32[]{:S(2)}) async-start(bf16[16,40,768]{2,1,0:T(8,128)(2,1)} %bitcast.10), calls=%async_computation.2 | async-start | bytes 1966080 | tf_op jit(solution)/shard_map/all_to_all | solution.py:548
  40.9 4.8 %collective-permute-start = (bf16[640,768]{1,0:T(8,128)(2,1)S(1)}, bf16[640,768]{1,0:T(8,128)(2,1)S(1)}, u32[]{:S(2)}, u32[]{:S(2)}) collective-permute-start(bf16[640,768]{1,0:T(8,128)(2,1)S(1)} %bitcast.24), channel_id=1, source_target_pairs={{0,16},{16,0},{1,17},{17,1},{2,18},{18,2},{3,19},{19,3},{4,20},{20... | collective-permute-start | bytes 2949128 | tf_op jit(solution)/shard_map/ppermute | solution.py:522
  52.2 1.9 copy-start
  54.1 28.5 %collective-permute-start.1 = (bf16[1,320,1536]{2,1,0:T(8,128)(2,1)S(1)}, bf16[1,320,1536]{2,1,0:T(8,128)(2,1)S(1)}, u32[]{:S(2)}, u32[]{:S(2)}) collective-permute-start(bf16[1,320,1536]{2,1,0:T(8,128)(2,1)S(1)} %get-tuple-element.22.mine), channel_id=1, source_target_pairs={{0,1},{1,0},{2,3},{3,2},{4,5},{5,4},{6,7},{7,6},{8,9},{9,8},{10,11... | collective-permute-start | bytes 2949128 | tf_op jit(solution)/shard_map/ppermute | solution.py:527
  63.8 27.2 %copy-start.1 = (bf16[2,2,2,320,768]{4,3,2,1,0:T(8,128)(2,1)S(1)}, bf16[2,2,2,320,768]{4,3,2,1,0:T(8,128)(2,1)}, u32[]{:S(2)}) copy-start(bf16[2,2,2,320,768]{4,3,2,1,0:T(8,128)(2,1)} %copy-done) | copy-start | bytes 11796484
  63.8 27.2 %collective-permute-start.3 = (bf16[640,768]{1,0:T(8,128)(2,1)S(1)}, bf16[640,768]{1,0:T(8,128)(2,1)S(1)}, u32[]{:S(2)}, u32[]{:S(2)}) collective-permute-start(bf16[640,768]{1,0:T(8,128)(2,1)S(1)} %bitcast.22), channel_id=1, source_target_pairs={{0,16},{16,0},{1,17},{17,1},{2,18},{18,2},{3,19},{19,3},{4,20},{20... | collective-permute-start | bytes 2949128 | tf_op jit(solution)/shard_map/ppermute | solution.py:522
  90.4 10.0 %collective-permute-start.2 = (bf16[2,1,320,768]{3,2,1,0:T(8,128)(2,1)S(1)}, bf16[2,1,320,768]{3,2,1,0:T(8,128)(2,1)S(1)}, u32[]{:S(2)}, u32[]{:S(2)}) collective-permute-start(bf16[2,1,320,768]{3,2,1,0:T(8,128)(2,1)S(1)} %get-tuple-element.24), channel_id=1, source_target_pairs={{0,16},{16,0},{1,17},{17,1},{2,18},{18,2},{3,19},{19,3},{4,20},{20... | collective-permute-start | bytes 2949128 | tf_op jit(solution)/shard_map/ppermute | solution.py:522
  98.3 1.9 copy-start.2
  100.2 31.5 %collective-permute-start.4 = (bf16[1,320,1536]{2,1,0:T(8,128)(2,1)}, bf16[1,320,1536]{2,1,0:T(8,128)(2,1)S(1)}, u32[]{:S(2)}, u32[]{:S(2)}) collective-permute-start(bf16[1,320,1536]{2,1,0:T(8,128)(2,1)} %get-tuple-element.26.mine), channel_id=1, source_target_pairs={{0,1},{1,0},{2,3},{3,2},{4,5},{5,4},{6,7},{7,6},{8,9},{9,8},{10,11... | collective-permute-start | bytes 2949128 | tf_op jit(solution)/shard_map/ppermute | solution.py:527
  103.3 39.3 %all-to-all-start.1 = ((bf16[16,40,768]{2,1,0:T(8,128)(2,1)}), bf16[16,40,768]{2,1,0:T(8,128)(2,1)}, u32[]{:S(2)}, u32[]{:S(2)}) async-start(bf16[16,40,768]{2,1,0:T(8,128)(2,1)} %bitcast.8), calls=%async_computation.1 | async-start | bytes 1966080 | tf_op jit(solution)/shard_map/all_to_all | solution.py:548
  136.3 46.5 %copy-start.18 = (f32[128,2]{0,1:T(2,128)S(1)}, f32[128,2]{0,1:T(2,128)}, u32[]{:S(2)}) copy-start(f32[128,2]{0,1:T(2,128)} %param.9) | copy-start | bytes 3076
  136.3 47.2 %copy-start.14 = (s32[8,640]{1,0:T(8,128)S(1)}, s32[8,640]{1,0:T(8,128)}, u32[]{:S(2)}) copy-start(s32[8,640]{1,0:T(8,128)} %constant.29.clone.marks) | copy-start | bytes 61444
  136.3 50.9 %copy-start.8 = (bf16[128,3072]{1,0:T(8,128)(2,1)S(1)}, bf16[128,3072]{1,0:T(8,128)(2,1)}, u32[]{:S(2)}) copy-start(bf16[128,3072]{1,0:T(8,128)(2,1)} %cotangent.5) | copy-start | bytes 2359300
  136.3 3.5 %collective-permute-start.5 = (bf16[2,1,320,768]{3,2,1,0:T(8,128)(2,1)S(1)}, bf16[2,1,320,768]{3,2,1,0:T(8,128)(2,1)S(1)}, u32[]{:S(2)}, u32[]{:S(2)}) collective-permute-start(bf16[2,1,320,768]{3,2,1,0:T(8,128)(2,1)S(1)} %get-tuple-element.29), channel_id=1, source_target_pairs={{0,16},{16,0},{1,17},{17,1},{2,18},{18,2},{3,19},{19,3},{4,20},{20... | collective-permute-start | bytes 2949128 | tf_op jit(solution)/shard_map/ppermute | solution.py:522
  142.7 44.5 %all-to-all-start.3 = ((bf16[16,40,768]{2,1,0:T(8,128)(2,1)}), bf16[16,40,768]{2,1,0:T(8,128)(2,1)}, u32[]{:S(2)}, u32[]{:S(2)}) async-start(bf16[16,40,768]{2,1,0:T(8,128)(2,1)} %bitcast.13), calls=%async_computation.3 | async-start | bytes 1966080 | tf_op jit(solution)/shard_map/all_to_all | solution.py:548
  149.1 31.9 %collective-permute-start.8 = (bf16[2,320,768]{2,1,0:T(8,128)(2,1)S(1)}, bf16[2,320,768]{2,1,0:T(8,128)(2,1)}, u32[]{:S(2)}, u32[]{:S(2)}) collective-permute-start(bf16[2,320,768]{2,1,0:T(8,128)(2,1)S(1)} %dynamic-slice_bitcast_fusion), channel_id=1, source_target_pairs={{0,1},{1,0},{2,3},{3,2},{4,5},{5,4},{6,7},{7,6},{8,9},{9,8},{10,11... | collective-permute-start | bytes 2949128 | tf_op jit(solution)/shard_map/ppermute | solution.py:527
  181.1 14.8 %collective-permute-start.9 = (bf16[2,320,768]{2,1,0:T(8,128)(2,1)}, bf16[2,320,768]{2,1,0:T(8,128)(2,1)}, u32[]{:S(2)}, u32[]{:S(2)}) collective-permute-start(bf16[2,320,768]{2,1,0:T(8,128)(2,1)} %collective-permute-done.8.rest_2_), channel_id=1, source_target_pairs={{0,16},{16,0},{1,17},{17,1},{2,18},{18,2},{3,19},{19,3},{4,20},{20... | collective-permute-start | bytes 2949128 | tf_op jit(solution)/shard_map/ppermute | solution.py:522
  187.2 8.7 %copy-start.3 = (bf16[2,2,2,320,768]{4,3,2,1,0:T(8,128)(2,1)S(1)}, bf16[2,2,2,320,768]{4,3,2,1,0:T(8,128)(2,1)}, u32[]{:S(2)}) copy-start(bf16[2,2,2,320,768]{4,3,2,1,0:T(8,128)(2,1)} %copy-done.2) | copy-start | bytes 11796484
  195.3 10.6 %collective-permute-start.6 = (bf16[2,2,128,768]{3,2,1,0:T(8,128)(2,1)S(1)}, bf16[2,2,128,768]{3,2,1,0:T(8,128)(2,1)S(1)}, u32[]{:S(2)}, u32[]{:S(2)}) collective-permute-start(bf16[2,2,128,768]{3,2,1,0:T(8,128)(2,1)S(1)} %get-tuple-element.30.own), channel_id=1, source_target_pairs={{0,16},{16,0},{1,17},{17,1},{2,18},{18,2},{3,19},{19,3},{4,20},{20... | collective-permute-start | bytes 2359304 | tf_op jit(solution)/shard_map/ppermute | solution.py:522
  195.4 9.9 %collective-permute-start.7 = (f32[128,128]{1,0:T(8,128)S(1)}, f32[128,128]{1,0:T(8,128)S(1)}, u32[]{:S(2)}, u32[]{:S(2)}) collective-permute-start(f32[128,128]{1,0:T(8,128)S(1)} %get-tuple-element.33), channel_id=1, source_target_pairs={{0,16},{16,0},{1,17},{17,1},{2,18},{18,2},{3,19},{19,3},{4,20},{20... | collective-permute-start | bytes 196616 | tf_op jit(solution)/shard_map/ppermute | solution.py:522
  (13 other events, 13.5 us)
where the time goes:
time: 210 us; the launch traced here: 208 us
  waiting for transfers between devices  103 us (49%)
  Pallas kernels  51.6 us (25%)
  starting transfers between devices  32.9 us (16%)
  local copies, waits for them, and re-layouts  20.1 us (10%)
    ppermute x3, waiting for transfers between devices, swap_holders(): lax.ppermute(value, 'expert', [(source, source ^ mask) for source in rang...  70.9 us
    all_to_all x4, waiting for transfers between devices, exchange(): lax.all_to_all(blocks, 'expert', split_axis=0, concat_axis=0, tiled=True)  27.5 us
    all_to_all x4, starting transfers between devices, exchange(): lax.all_to_all(blocks, 'expert', split_axis=0, concat_axis=0, tiled=True)  22.1 us
    unnamed x49, local copies, waits for them, and re-layouts  18.8 us
    pallas_call x2, Pallas kernels, partial_products(): pl.pallas_call(functools.partial(partial_kernel, dims), out_shape=(jax.Sh...  13.7 us
    pallas_call x1, Pallas kernels, weight_grads(): pl.pallas_call(functools.partial(weight_grad_kernel, steps), out_shape=ja...  9.35 us
    pallas_call x2, Pallas kernels, output_products(): pl.pallas_call(functools.partial(output_kernel, dims), out_shape=(jax.Sha...  8.97 us
    ppermute x7, starting transfers between devices, swap_cores(): return lax.ppermute(value, 'dp', [(0, 1), (1, 0)])  8.06 us
  transfers between devices with their start and end apart: 14, of which 7 were waited for; matrix products, arithmetic and copies ran while one was open for 1% of the time, Pallas kernels for 22%

commit v1 on v0

v1 whole, which is shorter than its diff:
```python
import functools

import jax
import jax.numpy as jnp
import numpy as np
from jax import lax
from jax.experimental import pallas as pl
from jax.experimental.pallas import tpu as pltpu
from jax.sharding import PartitionSpec as P

F32 = jnp.float32
BF16 = jnp.bfloat16
CHUNKS = 2
MIB = 1024 * 1024
BIG = 48


def dot(left, right, left_dim, right_dim):
    return lax.dot_general(
        left, right, (((left_dim,), (right_dim,)), ((), ())), preferred_element_type=F32
    )


def params(mib=24):
    return pltpu.CompilerParams(vmem_limit_bytes=mib * MIB)


WEIGHTS = {"output_0": 30, "output_1": 30}


def cost(macs, moved, name=""):
    weight = WEIGHTS.get(name, 0.01)
    return pl.CostEstimate(
        flops=int(2 * weight * macs), bytes_accessed=int(weight * moved), transcendentals=0
    )


def iota(shape, dim):
    return lax.broadcasted_iota(jnp.int32, shape, dim)


def split_index(index, size):
    whole = jnp.floor((index.astype(F32) + 0.5) * (1.0 / size)).astype(jnp.int32)
    return whole, index - whole * size


def dispatch_kernel(dims, chunk, ids, routes, gates, tokens, cotangent, sent, picks, scales):
    subs, groups, per_chunk, cap, block = dims
    token_count = routes.shape[1]

    @pl.when(pl.program_id(0) == 0)
    def _():
        route = [routes[k : k + 1, :] for k in range(2)]
        gate = [gates[k : k + 1, :] for k in range(2)]
        sub = iota((subs, token_count), 0)
        hits = [(route[k] == sub).astype(F32) for k in range(2)]
        earlier = (iota((token_count,) * 2, 0) < iota((token_count,) * 2, 1)).astype(BF16)
        before = dot((hits[0] + hits[1]).astype(BF16), earlier, 1, 0)
        slot = [jnp.sum(hits[k] * before, axis=0, keepdims=True) for k in range(2)]
        slot[1] = slot[1] + (route[0] == route[1]).astype(F32)
        row = iota((block, token_count), 0)
        row = jnp.where(row >= block // 2, row - block // 2, row)
        local = jnp.zeros_like(row)
        for i in range(1, per_chunk):
            local = local + (row >= i * cap).astype(jnp.int32)
        place = (row - local * cap).astype(F32)
        for e in range(subs // groups):
            wanted = local + (e * groups + chunk * per_chunk)
            match = [(route[k] == wanted) & (slot[k] == place) for k in range(2)]
            scale = jnp.where(match[0], gate[0], 0.0) + jnp.where(match[1], gate[1], 0.0)
            scales[e * block : (e + 1) * block, :] = jnp.broadcast_to(
                jnp.sum(scale, axis=1, keepdims=True), scale.shape
            )
            picks[e * block : (e + 1) * block, :] = (
                match[0].astype(F32) + match[1].astype(F32)
            ).astype(BF16)

    rows = picks[...]
    chosen = dot(rows, tokens[...], 1, 0)
    graded = dot(rows, cotangent[...], 1, 0) * scales[:, :1]
    for e in range(subs // groups):
        part = slice(e * block, (e + 1) * block)
        first = iota((block, 1), 0) < block // 2
        sent[e] = jnp.where(first, chosen[part], graded[part]).astype(BF16)


def quarter(value, groups, width):
    rows = value.shape[0]
    if width % 128 == 0:
        return value, pl.BlockSpec((rows, width), lambda p, ids: (0, 2 * p + ids[0]))
    own = lax.dynamic_index_in_dim(
        value.reshape(rows, groups, 2, width), lax.axis_index("dp"), 2, keepdims=False
    )
    return own.transpose(1, 0, 2), pl.BlockSpec((None, rows, width), lambda p, ids: (p, 0, 0))


def dispatch(dims, chunk, width, ids, routes, gates, tokens, cotangent):
    subs, groups, per_chunk, cap, block = dims
    experts = subs // groups
    token_count = routes.shape[1]
    whole = lambda shape: pl.BlockSpec(shape, lambda p, ids: (0,) * len(shape))
    tokens, tokens_spec = tokens
    cotangent, cotangent_spec = cotangent
    return pl.pallas_call(
        functools.partial(dispatch_kernel, dims, chunk),
        out_shape=jax.ShapeDtypeStruct((experts, groups, block, width), BF16),
        grid_spec=pltpu.PrefetchScalarGridSpec(
            num_scalar_prefetch=1,
            grid=(groups,),
            in_specs=[whole(routes.shape), whole(gates.shape), tokens_spec, cotangent_spec],
            out_specs=pl.BlockSpec((experts, None, block, width), lambda p, ids: (0, p, 0, 0)),
            scratch_shapes=[
                pltpu.VMEM((experts * block, token_count), BF16),
                pltpu.VMEM((experts * block, token_count), F32),
            ],
        ),
        compiler_params=params(60),
        cost_estimate=cost(
            2 * experts * block * token_count * width * groups,
            2 * (2 * token_count + experts * block) * width * groups,
        ),
        name=f"dispatch_{chunk}",
    )(ids, routes, gates, tokens, cotangent)


def partial_kernel(dims, chunk, ids, own, other_low, other_high, weights, *rest):
    subs, groups, per_chunk, cap, block = dims
    features, partial, held, arrivals = rest
    q = ids[0]
    width = own.shape[1]
    units = weights.shape[3]
    loads = [
        pltpu.make_async_copy(
            weights.at[pl.ds(chunk * per_chunk, per_chunk), m], held.at[m], arrivals.at[m]
        )
        for m in range(3)
    ]
    for load in loads:
        load.start()
    together_count = gather_group(cap)
    inner = together_count * block
    part = together_count * cap
    kind, place = split_index(iota((inner, 1), 0), part)
    source, place = split_index(place, cap)
    target = source * block + kind * cap + place
    chooser = (iota((inner, inner), 1) == target).astype(F32).astype(BF16)
    sets = subs // together_count
    for side in range(2):
        for g in range(sets):
            if side == 0:
                rows = own[g * inner : (g + 1) * inner, :]
            elif g < sets // 2:
                rows = other_low[g * inner : (g + 1) * inner, :]
            else:
                rows = other_high[(g - sets // 2) * inner : (g + 1 - sets // 2) * inner, :]
            sorted_rows = dot(chooser, rows, 1, 0).astype(BF16)
            for half in range(2):
                for i in range(per_chunk):
                    start = (half * per_chunk + i) * part
                    features[i, side, half, g * part : (g + 1) * part, :] = sorted_rows[
                        start : start + part
                    ]
    for m in range(3):
        loads[m].wait()
        half = 1 if m == 2 else 0
        for i in range(per_chunk):
            total = None
            for side in range(2):
                first = q * width if side == 0 else (1 - q) * width
                block_rows = held[m, i, pl.ds(pl.multiple_of(first, 64), width), :]
                term = dot(features[i, side, half], block_rows, 1, 0)
                total = term if total is None else total + term
            partial[i, :, m * units : (m + 1) * units] = total.astype(BF16)


def gather_group(cap):
    count = 1
    while count * cap % 16:
        count *= 2
    return count


def partial_products(dims, chunk, ids, own, others, weights):
    subs, groups, per_chunk, cap, block = dims
    rows = subs * cap
    width = own.shape[1]
    depth, units = weights.shape[2:]
    whole = lambda shape: pl.BlockSpec(shape, lambda s, ids: (0,) * len(shape))
    in_specs = [whole(own.shape)] + [whole(o.shape) for o in others]
    in_specs.append(pl.BlockSpec(memory_space=pltpu.HBM))
    operands = [ids, own, *others, weights]
    return pl.pallas_call(
        functools.partial(partial_kernel, dims, chunk),
        out_shape=(
            jax.ShapeDtypeStruct((per_chunk, 2, 2, rows, width), BF16),
            jax.ShapeDtypeStruct((per_chunk, rows, 3 * units), BF16),
        ),
        grid_spec=pltpu.PrefetchScalarGridSpec(
            num_scalar_prefetch=1,
            grid=(1,),
            in_specs=in_specs,
            out_specs=(
                whole((per_chunk, 2, 2, rows, width)),
                whole((per_chunk, rows, 3 * units)),
            ),
            scratch_shapes=[
                pltpu.VMEM((3, per_chunk, depth, units), BF16),
                pltpu.SemaphoreType.DMA((3,)),
            ],
        ),
        compiler_params=params(BIG),
        cost_estimate=cost(
            per_chunk * rows * (3 * depth * units + 4 * subs * block * width),
            2 * per_chunk * (3 * depth * units + 8 * rows * width + 3 * rows * units),
        ),
        name=f"partial_{chunk}",
    )(*operands)


def output_kernel(dims, chunk, ids, mine, theirs, weights, *rest):
    per_chunk = dims[2]
    acts, own_out, own_grad, other_out, other_grad, held, arrivals = rest
    units = weights.shape[3]
    width = own_out.shape[2]
    q = ids[0]
    loads = [
        pltpu.make_async_copy(
            weights.at[
                pl.ds(chunk * per_chunk, per_chunk),
                :,
                pl.ds(pl.multiple_of((1 - q if side == 0 else q) * width, 64), width),
            ],
            held.at[side],
            arrivals.at[side],
        )
        for side in range(2)
    ]
    for load in loads:
        load.start()
    for i in range(per_chunk):
        total = lambda m: mine[i, :, m * units : (m + 1) * units].astype(F32) + theirs[
            i, :, m * units : (m + 1) * units
        ].astype(F32)
        gate, up, grad = total(0), total(1), total(2)
        sigmoid = jax.nn.sigmoid(gate)
        active = gate * sigmoid
        acts[i, :, :units] = (grad * up * sigmoid * (1.0 + gate * (1.0 - sigmoid))).astype(BF16)
        acts[i, :, units : 2 * units] = (grad * active).astype(BF16)
        acts[i, :, 2 * units :] = (active * up).astype(BF16)
    for side, target in enumerate(((other_out, other_grad), (own_out, own_grad))):
        loads[side].wait()
        for i in range(per_chunk):
            hidden = acts[i, :, 2 * units :]
            target[0][i] = dot(hidden, held[side, i, 2], 1, 1).astype(BF16)
            target[1][i] = (
                dot(acts[i, :, :units], held[side, i, 0], 1, 1)
                + dot(acts[i, :, units : 2 * units], held[side, i, 1], 1, 1)
            ).astype(BF16)


def output_products(dims, chunk, ids, mine, theirs, weights):
    subs, groups, per_chunk, cap, block = dims
    rows = subs * cap
    depth, units = weights.shape[2:]
    width = depth // 2
    whole = lambda shape: pl.BlockSpec(shape, lambda s, ids: (0,) * len(shape))
    in_specs = [whole(mine.shape), whole(theirs.shape), pl.BlockSpec(memory_space=pltpu.HBM)]
    operands = [ids, mine, theirs, weights]
    out = jax.ShapeDtypeStruct((per_chunk, rows, width), BF16)
    return pl.pallas_call(
        functools.partial(output_kernel, dims, chunk),
        out_shape=(jax.ShapeDtypeStruct((per_chunk, rows, 3 * units), BF16),) + (out,) * 4,
        grid_spec=pltpu.PrefetchScalarGridSpec(
            num_scalar_prefetch=1,
            grid=(1,),
            in_specs=in_specs,
            out_specs=(
                whole((per_chunk, rows, 3 * units)),
            )
            + (whole(out.shape),) * 4,
            scratch_shapes=[
                pltpu.VMEM((2, per_chunk, 3, width, units), BF16),
                pltpu.SemaphoreType.DMA((2,)),
            ],
        ),
        compiler_params=params(BIG),
        cost_estimate=cost(
            per_chunk * rows * 3 * depth * units,
            2 * per_chunk * (3 * depth * units + 2 * rows * depth + 9 * rows * units),
            f"output_{chunk}",
        ),
        name=f"output_{chunk}",
    )(*operands)


def pack_kernel(dims, own_out, own_grad, other_out, other_grad, packed):
    subs, groups, per_chunk, cap, block = dims
    count = gather_group(cap)
    inner, part = count * block, count * cap
    source, place = split_index(iota((inner, 1), 0), block)
    kind, place = split_index(place, cap)
    target = kind * part + source * cap + place
    chooser = (iota((inner, inner), 1) == target).astype(F32).astype(BF16)
    for g in range(subs // count):
        rows = slice(g * part, (g + 1) * part)
        summed = [
            (own[i, rows].astype(F32) + other[i, rows].astype(F32)).astype(BF16)
            for own, other in ((own_out, other_out), (own_grad, other_grad))
            for i in range(per_chunk)
        ]
        packed[g * inner : (g + 1) * inner, :] = dot(
            chooser, jnp.concatenate(summed, axis=0), 1, 0
        ).astype(BF16)


def pack(dims, chunk, parts):
    subs, groups, per_chunk, cap, block = dims
    rows = subs * cap
    width = parts[0].shape[2]
    columns = 256 if width % 256 == 0 else width
    spec = pl.BlockSpec((per_chunk, rows, columns), lambda c: (0, 0, c))
    return pl.pallas_call(
        functools.partial(pack_kernel, dims),
        out_shape=jax.ShapeDtypeStruct((subs * block, width), BF16),
        grid=(width // columns,),
        in_specs=[spec] * 4,
        out_specs=pl.BlockSpec((subs * block, columns), lambda c: (0, c)),
        compiler_params=params(),
        cost_estimate=cost(
            subs * block * 2 * per_chunk * rows * width, 6 * subs * block * width, f"pack_{chunk}"
        ),
        name=f"pack_{chunk}",
    )(*parts)


def chooser_kernel(dims, ids, routes, gates, marks, gates_out, *choosers):
    subs, groups, per_chunk, cap, block = dims
    token_count = routes.shape[0]
    p = pl.program_id(0)
    gates_out[...] = gates[...]
    route = [routes[:, k : k + 1] for k in range(2)]
    sub = iota((token_count, subs), 1)
    hits = [(route[k] == sub).astype(F32) for k in range(2)]
    earlier = (iota((token_count,) * 2, 1) < iota((token_count,) * 2, 0)).astype(BF16)
    before = dot(earlier, (hits[0] + hits[1]).astype(BF16), 1, 0)
    slot = [jnp.sum(hits[k] * before, axis=1, keepdims=True) for k in range(2)]
    slot[1] = slot[1] + (route[0] == route[1]).astype(F32)
    slot = [value.astype(jnp.int32) for value in slot]
    for chunk in range(CHUNKS):
        wanted = marks[0:1, :] + chunk * per_chunk
        place, half, holder = marks[1:2, :], marks[2:3, :], marks[3:4, :]
        match = [
            ((route[k] == wanted) & (slot[k] == place) & (holder == p)).astype(F32)
            for k in range(2)
        ]
        first = (half == 0).astype(F32)
        second = (half == 1).astype(F32)
        choosers[chunk][0:token_count, :] = (match[0] * first).astype(BF16)
        choosers[chunk][token_count : 2 * token_count, :] = (match[1] * first).astype(BF16)
        choosers[chunk][2 * token_count :, :] = ((match[0] + match[1]) * second).astype(BF16)


def return_choosers(dims, ids, routes, gates):
    subs, groups, per_chunk, cap, block = dims
    token_count = routes.shape[0]
    row = np.arange(subs * block)
    device, inner = row // block, row % block
    half, inner = inner // (per_chunk * cap), inner % (per_chunk * cap)
    local, place = inner // cap, inner % cap
    marks = np.zeros((8, subs * block), np.int32)
    marks[0] = device // groups * groups + local
    marks[1] = place
    marks[2] = half
    marks[3] = device % groups
    whole = lambda shape: pl.BlockSpec(shape, lambda p, ids: (0,) * len(shape))
    shape = jax.ShapeDtypeStruct((groups, 3 * token_count, subs * block), BF16)
    spec = pl.BlockSpec((None, 3 * token_count, subs * block), lambda p, ids: (p, 0, 0))
    return pl.pallas_call(
        functools.partial(chooser_kernel, dims),
        out_shape=(jax.ShapeDtypeStruct(gates.shape, F32),) + (shape,) * CHUNKS,
        grid_spec=pltpu.PrefetchScalarGridSpec(
            num_scalar_prefetch=1,
            grid=(groups,),
            in_specs=[whole(routes.shape), whole(gates.shape), whole(marks.shape)],
            out_specs=(whole(gates.shape),) + (spec,) * CHUNKS,
        ),
        compiler_params=params(),
        cost_estimate=cost(0, 2 * CHUNKS * groups * 3 * token_count * subs * block, "choosers"),
        name="choosers",
    )(ids, routes, gates, jnp.asarray(marks))


def gather_kernel(ids, chooser, returned, total):
    total[...] = dot(chooser[...], returned[...], 1, 0)


def gather_rows(ids, chooser, returned):
    groups, picks, rows = chooser.shape
    width = returned.shape[1]
    return pl.pallas_call(
        gather_kernel,
        out_shape=jax.ShapeDtypeStruct((groups, picks, width), F32),
        grid_spec=pltpu.PrefetchScalarGridSpec(
            num_scalar_prefetch=1,
            grid=(groups,),
            in_specs=[
                pl.BlockSpec((None, picks, rows), lambda p, ids: (p, 0, 0)),
                pl.BlockSpec(returned.shape, lambda p, ids: (0, 0)),
            ],
            out_specs=pl.BlockSpec((None, picks, width), lambda p, ids: (p, 0, 0)),
        ),
        compiler_params=params(),
        cost_estimate=cost(groups * picks * rows * width, 4 * groups * picks * width, "gather_rows"),
        name="gather_rows",
    )(ids, chooser, returned)


def combine_kernel(ids, gates, cotangent, chooser, returned, earlier, combined, gate_grad, *direct):
    token_count = gates.shape[0]
    p = pl.program_id(0)
    total = dot(chooser[...], returned[...], 1, 0) + earlier[...]
    picked = [total[k * token_count : (k + 1) * token_count] for k in range(3)]
    layer_out = (gates[:, 0:1] * picked[0] + gates[:, 1:2] * picked[1]).astype(BF16)
    input_grad = picked[2].astype(BF16)
    combined[0] = layer_out
    combined[1] = input_grad
    if direct:
        direct[0][...] = layer_out
        direct[1][...] = input_grad
    grads = cotangent[...].astype(F32)
    lane = iota((token_count, 128), 1)
    term = jnp.where(lane == 0, jnp.sum(grads * picked[0], axis=1, keepdims=True), 0.0)
    term += jnp.where(lane == 1, jnp.sum(grads * picked[1], axis=1, keepdims=True), 0.0)

    @pl.when(p == 0)
    def _():
        gate_grad[...] = term

    @pl.when(p > 0)
    def _():
        gate_grad[...] += term


def combine(dims, width, ids, gates, cotangent, chooser, returned, earlier):
    subs, groups, per_chunk, cap, block = dims
    token_count = gates.shape[0]
    cotangent, cotangent_spec = cotangent
    whole = lambda shape: pl.BlockSpec(shape, lambda p, ids: (0,) * len(shape))
    by_holder = lambda shape: pl.BlockSpec((None,) + shape[1:], lambda p, ids: (p, 0, 0))
    final = jax.ShapeDtypeStruct((token_count, 2 * groups * width), BF16)
    direct = 2 if width % 128 == 0 else 0
    return pl.pallas_call(
        combine_kernel,
        out_shape=(
            jax.ShapeDtypeStruct((2, groups, token_count, width), BF16),
            jax.ShapeDtypeStruct((token_count, 128), F32),
        )
        + (final,) * direct,
        grid_spec=pltpu.PrefetchScalarGridSpec(
            num_scalar_prefetch=1,
            grid=(groups,),
            in_specs=[
                whole(gates.shape),
                cotangent_spec,
                by_holder(chooser.shape),
                whole(returned.shape),
                by_holder(earlier.shape),
            ],
            out_specs=(
                pl.BlockSpec((2, None, token_count, width), lambda p, ids: (0, p, 0, 0)),
                whole((token_count, 128)),
            )
            + (pl.BlockSpec((token_count, width), lambda p, ids: (0, 2 * p + ids[0])),) * direct,
        ),
        compiler_params=params(),
        cost_estimate=cost(
            groups * 3 * token_count * subs * block * width,
            2 * subs * block * (width + 3 * groups * token_count),
        ),
        name="combine",
    )(ids, gates, cotangent, chooser, returned, earlier)


def merge_kernel(ids, other, started_out, started_grad, layer_out, input_grad):
    layer_out[...] = other[0]
    input_grad[...] = other[1]


def merge(ids, own, other, direct):
    _, groups, token_count, width = own.shape
    model_width = 2 * groups * width
    if not direct:
        q = lax.axis_index("dp")
        pair = jnp.stack([jnp.where(q == 0, own, other), jnp.where(q == 0, other, own)], axis=2)
        pair = pair.transpose(0, 3, 1, 2, 4).reshape(2, token_count, model_width)
        return pair[0], pair[1]
    in_spec = pl.BlockSpec((2, None, token_count, width), lambda p, ids: (0, p, 0, 0))
    out_spec = pl.BlockSpec((token_count, width), lambda p, ids: (0, 2 * p + 1 - ids[0]))
    shape = jax.ShapeDtypeStruct((token_count, model_width), BF16)
    return pl.pallas_call(
        merge_kernel,
        out_shape=(shape, shape),
        grid_spec=pltpu.PrefetchScalarGridSpec(
            num_scalar_prefetch=1,
            grid=(groups,),
            in_specs=[in_spec] + [pl.BlockSpec(memory_space=pl.ANY)] * 2,
            out_specs=(out_spec, out_spec),
        ),
        input_output_aliases={2: 0, 3: 1},
        compiler_params=params(),
        cost_estimate=cost(0, 8 * token_count * model_width),
        name="merge",
    )(ids, other, *direct)


def pick_acts(chunks, ids, acts, held, arrival):
    per_chunk = acts[0].shape[0]
    local = ids[1] % per_chunk
    for c in range(chunks):

        @pl.when(ids[1] // per_chunk == c)
        def _(c=c):
            pltpu.make_async_copy(acts[c].at[local], held, arrival).start()

    return pltpu.make_async_copy(acts[0].at[local], held, arrival)


def weight_grad_block(features, acts, grads):
    units = acts.shape[1] // 3
    both = dot(features[0], acts[:, : 2 * units], 0, 0).astype(BF16)
    grads[0] = both[:, :units]
    grads[1] = both[:, units:]
    grads[2] = dot(features[1], acts[:, 2 * units :], 0, 0).astype(BF16)


def near_kernel(ids, *refs):
    acts, features = refs[:CHUNKS], refs[CHUNKS : 2 * CHUNKS]
    grads, held, rows, arrivals = refs[2 * CHUNKS :]
    per_chunk = acts[0].shape[0]
    local = ids[1] % per_chunk
    side = pl.program_id(0)
    load = lambda c, s: pltpu.make_async_copy(
        features[c].at[local, s], rows.at[s], arrivals.at[1 + s]
    )

    @pl.when(side == 0)
    def _():
        ready = pick_acts(CHUNKS, ids, acts, held, arrivals.at[0])
        for c in range(CHUNKS):

            @pl.when(ids[1] // per_chunk == c)
            def _(c=c):
                load(c, 0).start()
                load(c, 1).start()

        ready.wait()
        load(0, 0).wait()
        weight_grad_block(rows.at[0], held, grads)

    @pl.when(side == 1)
    def _():
        load(0, 1).wait()
        weight_grad_block(rows.at[1], held, grads)


def near_weight_grads(ids, acts, features):
    rows, triple = acts[0].shape[1:]
    per_chunk = acts[0].shape[0]
    groups = per_chunk * CHUNKS
    width = features[0].shape[4]
    units = triple // 3
    return pl.pallas_call(
        near_kernel,
        out_shape=jax.ShapeDtypeStruct((3, 2 * groups * width, units), BF16),
        grid_spec=pltpu.PrefetchScalarGridSpec(
            num_scalar_prefetch=1,
            grid=(2,),
            in_specs=[pl.BlockSpec(memory_space=pl.ANY)] * (2 * CHUNKS),
            out_specs=pl.BlockSpec(
                (3, width, units),
                lambda s, ids: (0, 2 * ids[1] + jnp.where(s == 0, ids[0], 1 - ids[0]), 0),
            ),
            scratch_shapes=[
                pltpu.VMEM((rows, triple), BF16),
                pltpu.VMEM((2, 2, rows, width), BF16),
                pltpu.SemaphoreType.DMA((3,)),
            ],
        ),
        compiler_params=params(),
        cost_estimate=cost(6 * rows * width * units, 12 * width * units + 8 * rows * width, "near_weight_grads"),
        name="near_weight_grads",
    )(ids, *acts, *features)


def far_kernel(count, ids, *refs):
    acts, features = refs[:CHUNKS], refs[CHUNKS : CHUNKS + count]
    grads, held, arrival = refs[-3:]
    step = pl.program_id(0)

    @pl.when(step == 0)
    def _():
        pick_acts(CHUNKS, ids, acts, held, arrival).wait()

    for index in range(count):

        @pl.when(step == index)
        def _(index=index):
            weight_grad_block(features[index], held, grads)


def far_weight_grads(ids, acts, far, grads):
    rows, triple = acts[0].shape[1:]
    units = triple // 3
    operands = [value for pair in far for value in pair]
    count = len(operands)
    width = operands[0].shape[2]

    def target(s, ids):
        holder = ids[1] ^ (1 + s // 2)
        return 0, 2 * holder + jnp.where(s % 2 == 0, ids[0], 1 - ids[0]), 0

    return pl.pallas_call(
        functools.partial(far_kernel, count),
        out_shape=jax.ShapeDtypeStruct(grads.shape, BF16),
        grid_spec=pltpu.PrefetchScalarGridSpec(
            num_scalar_prefetch=1,
            grid=(count,),
            in_specs=[pl.BlockSpec(memory_space=pl.ANY)] * CHUNKS
            + [pl.BlockSpec((2, rows, width), lambda s, ids: (0, 0, 0))] * count
            + [pl.BlockSpec(memory_space=pl.ANY)],
            out_specs=pl.BlockSpec((3, width, units), target),
            scratch_shapes=[pltpu.VMEM((rows, triple), BF16), pltpu.SemaphoreType.DMA],
        ),
        input_output_aliases={1 + CHUNKS + count: 0},
        compiler_params=params(),
        cost_estimate=cost(
            3 * rows * count * width * units, 6 * count * width * units + 4 * count * rows * width
        ),
        name="far_weight_grads",
    )(ids, *acts, *operands, grads)


def choose(values, index):
    result = values[0]
    for i in range(1, len(values)):
        result = jnp.where(index == i, values[i], result)
    return result


def together(*values):
    return lax.optimization_barrier(values)


def swap_cores(value):
    return lax.ppermute(value, "dp", [(0, 1), (1, 0)])


def swap_holders(value, mask):
    size = lax.axis_size("expert")
    return lax.ppermute(value, "expert", [(source, source ^ mask) for source in range(size)])


def shards(tokens, cotangent, routes, gate_values, weights):
    groups, depth = weights.shape[:2]
    token_count, top_count = routes.shape
    subs = lax.axis_size("expert")
    cap = 5 * token_count * top_count // (4 * subs)
    per_chunk = groups // CHUNKS
    block = 2 * per_chunk * cap
    width = depth // 2
    dims = (subs, groups, per_chunk, cap, block)
    core = lax.axis_index("dp")
    holder = lax.axis_index("expert") % groups
    ids = jnp.stack([core, holder]).astype(jnp.int32)
    weights = weights[:, :, :, 0, :].transpose(0, 2, 1, 3)
    own_tokens = quarter(tokens, groups, width)
    own_cotangent = quarter(cotangent, groups, width)

    def exchange(rows):
        blocks = rows.reshape(subs, block, width)
        moved = lax.all_to_all(blocks, "expert", split_axis=0, concat_axis=0, tiled=True)
        return moved.reshape(subs * block, width)

    sent = [
        dispatch(dims, c, width, ids, routes.T, gate_values.T, own_tokens, own_cotangent)
        for c in range(CHUNKS)
    ]
    arrived = [exchange(value) for value in sent]
    features, acts, mine, theirs, returned = [], [], [], [], []
    for c in range(CHUNKS):
        others = [swap_cores(part) for part in jnp.split(arrived[c], 2)]
        rows, partial = partial_products(dims, c, ids, arrived[c], others, weights)
        features.append(rows)
        if c + 1 < CHUNKS:
            arrived[c + 1], _ = together(arrived[c + 1], partial)
        mask = 1
        while mask < groups // 2:
            partial = (partial.astype(F32) + swap_holders(partial, mask).astype(F32)).astype(BF16)
            mask *= 2
        mine.append(partial)
        theirs.append(swap_holders(partial, mask))
    by_sub = [features[s // per_chunk][s % per_chunk, 0] for s in range(groups)]
    leaving = [choose(by_sub, holder ^ mask) for mask in range(1, groups)]
    theirs[0], _, *leaving = together(theirs[0], mine[-1], *leaving)
    for c in range(CHUNKS):
        active, *parts = output_products(dims, c, ids, mine[c], theirs[c], weights)
        acts.append(active)
        parts[2:] = [swap_cores(part) for part in parts[2:]]
        packed = pack(dims, c, parts)
        if c + 1 < CHUNKS:
            theirs[c + 1], _ = together(theirs[c + 1], packed)
        if c > 0:
            packed, returned[c - 1] = together(packed, returned[c - 1])
        returned.append(exchange(packed))
    theirs[-1], *leaving = together(theirs[-1], *leaving)
    routes, packed = together(routes, packed)
    gates, *choosers = return_choosers(dims, ids, routes, gate_values)
    earlier = gather_rows(ids, choosers[0], returned[0])
    for c in range(1, CHUNKS - 1):
        earlier = earlier + gather_rows(ids, choosers[c], returned[c])
    weight_grad = near_weight_grads(ids, acts, features)
    far = []
    for mask in range(1, groups):
        near = swap_holders(leaving[mask - 1], mask)
        near, weight_grad, earlier = together(near, weight_grad, earlier)
        far.append((near, swap_cores(near)))
    weight_grad = far_weight_grads(ids, acts, far, weight_grad)
    returned[-1], earlier, weight_grad = together(returned[-1], earlier, weight_grad)
    combined, gate_part, *direct = combine(
        dims, width, ids, gates, own_cotangent, choosers[-1], returned[-1], earlier
    )
    layer_out, input_grad = merge(ids, combined, swap_cores(combined), direct)
    gate_grad = (gate_part + swap_cores(gate_part))[:, :top_count]
    weight_grad = weight_grad.transpose(1, 0, 2).reshape(1, groups * depth, 3, 1, -1)
    return layer_out, input_grad, gate_grad, weight_grad


def solution(mesh):
    in_specs = (
        P("expert", None),
        P("expert", None),
        P("expert", None),
        P("expert", None),
        P(None, "expert", None, "dp", None),
    )
    out_specs = (
        P("expert", None),
        P("expert", None),
        P("expert", None),
        P("expert", None, None, "dp", None),
    )
    return jax.shard_map(shards, mesh=mesh, in_specs=in_specs, out_specs=out_specs, check_vma=False)
```

time: 210 us -> 167 us (0.80)
  waiting for transfers between devices: 103 us -> 61.9 us
  local copies, waits for them, and re-layouts: 20.1 us -> 12.4 us
  Pallas kernels: 51.6 us -> 56.2 us
    ppermute x3, waiting for transfers between devices: 70.9 us -> 14.4 us  [swap_holders(): lax.ppermute(value, 'expert', [(source, source ^ mask) for source in rang...]
    ppermute x7 -> x11, waiting for transfers between devices: 4.4 us -> 12.8 us  [swap_cores(): return lax.ppermute(value, 'dp', [(0, 1), (1, 0)])]
    unnamed x49 -> x38, local copies, waits for them, and re-layouts: 18.8 us -> 11.2 us
    all_to_all x4, waiting for transfers between devices: 27.5 us -> 34.7 us  [exchange(): lax.all_to_all(blocks, 'expert', split_axis=0, concat_axis=0, tiled=True)]
    pallas_call x6 -> x8, Pallas kernels: 33.8 us -> 40.8 us  [the longest x2 12.3 us: output_products(): pl.pallas_call(functools.partial(output_kernel, dims, chunk), out_shape=(...]
    pallas_call x2, Pallas kernels: 5.78 us -> 2.4 us  [pack(): pl.pallas_call(functools.partial(pack_kernel, dims), out_shape=jax.ShapeD...]
    pallas_call x2, Pallas kernels: 5.12 us -> 7.28 us  [dispatch(): pl.pallas_call(functools.partial(dispatch_kernel, dims, chunk), out_shape...]
    ppermute x7 -> x11, starting transfers between devices: 8.06 us -> 8.11 us  [swap_cores(): return lax.ppermute(value, 'dp', [(0, 1), (1, 0)])]
  transfers between devices with their start and end apart: 14 -> 18, of which waited for: 7 -> 16; matrix products, arithmetic and copies ran while one was open for 1% -> 2% of each run, Pallas kernels for 22% -> 28%
where the time goes in v1:
time: 167 us; the launch traced here: 166 us
  waiting for transfers between devices  61.9 us (37%)
  Pallas kernels  56.2 us (34%)
  starting transfers between devices  32.7 us (20%)
  local copies, waits for them, and re-layouts  12.4 us (7%)
  other arithmetic  1.67 us (1%)
    all_to_all x4, waiting for transfers between devices, exchange(): lax.all_to_all(blocks, 'expert', split_axis=0, concat_axis=0, tiled=True)  34.7 us
    all_to_all x4, starting transfers between devices, exchange(): lax.all_to_all(blocks, 'expert', split_axis=0, concat_axis=0, tiled=True)  21.7 us
    ppermute x3, waiting for transfers between devices, swap_holders(): lax.ppermute(value, 'expert', [(source, source ^ mask) for source in rang...  14.4 us
    ppermute x11, waiting for transfers between devices, swap_cores(): return lax.ppermute(value, 'dp', [(0, 1), (1, 0)])  12.8 us
    pallas_call x2, Pallas kernels, output_products(): pl.pallas_call(functools.partial(output_kernel, dims, chunk), out_shape=(...  12.3 us
    pallas_call x2, Pallas kernels, partial_products(): pl.pallas_call(functools.partial(partial_kernel, dims, chunk), out_shape=...  11.5 us
    unnamed x38, local copies, waits for them, and re-layouts  11.2 us
    ppermute x11, starting transfers between devices, swap_cores(): return lax.ppermute(value, 'dp', [(0, 1), (1, 0)])  8.11 us
  transfers between devices with their start and end apart: 18, of which 16 were waited for; matrix products, arithmetic and copies ran while one was open for 2% of the time, Pallas kernels for 28%

profile of v1, /device:TPU:17, one launch (start us, length us, event | category | flops | bytes accessed | tf_op | source)
XLA Modules:
  0.0 165.8 jit_solution(11368284743247482091)
XLA Ops:
  1.2 3.6 %dispatch_0.1 = bf16[8,2,40,768]{3,2,1,0:T(8,128)(2,1)} custom-call(s32[2]{0:T(128)} %pad_add_fusion.ids, s32[2,128]{1,0:T(2,128)} %bitcast.40, f32[2,128]{1,0:T(2,128)} %bitcast.38, bf16[128,3072]{1,0:T(8,128)(2,1)} %tokens.3, bf16[128,3072]{1,0:T(8,128)(2,1)} %cotangent.5), custom_call_target="tpu_custom_call" | custom-call | flops 2516582 | bytes 17694 | tf_op jit(solution)/shard_map/dispatch_0/pallas_call | solution.py:104
  4.8 6.6 %all-to-all-start.1 = ((bf16[16,40,768]{2,1,0:T(8,128)(2,1)}), bf16[16,40,768]{2,1,0:T(8,128)(2,1)S(1)}, u32[]{:S(2)}, u32[]{:S(2)}) async-start(bf16[16,40,768]{2,1,0:T(8,128)(2,1)} %bitcast.35), calls=%async_computation.1 | async-start | bytes 1966080 | tf_op jit(solution)/shard_map/all_to_all | solution.py:681
  11.4 3.7 %dispatch_1.1 = bf16[8,2,40,768]{3,2,1,0:T(8,128)(2,1)} custom-call(s32[2]{0:T(128)} %pad_add_fusion.ids, s32[2,128]{1,0:T(2,128)} %bitcast.41, f32[2,128]{1,0:T(2,128)} %bitcast.39, bf16[128,3072]{1,0:T(8,128)(2,1)} %tokens.3, bf16[128,3072]{1,0:T(8,128)(2,1)} %cotangent.5), custom_call_target="tpu_custom_call" | custom-call | flops 2516582 | bytes 17694 | tf_op jit(solution)/shard_map/dispatch_1/pallas_call | solution.py:104
  15.1 18.9 %all-to-all-done.1 = bf16[16,40,768]{2,1,0:T(8,128)(2,1)S(1)} async-done(((bf16[16,40,768]{2,1,0:T(8,128)(2,1)}), bf16[16,40,768]{2,1,0:T(8,128)(2,1)S(1)}, u32[]{:S(2)}, u32[]{:S(2)}) %all-to-all-start.1) | async-done | bytes 983072 | tf_op jit(solution)/shard_map/all_to_all | solution.py:681
  34.0 4.9 %all-to-all-start = ((bf16[16,40,768]{2,1,0:T(8,128)(2,1)}), bf16[16,40,768]{2,1,0:T(8,128)(2,1)S(1)}, u32[]{:S(2)}, u32[]{:S(2)}) async-start(bf16[16,40,768]{2,1,0:T(8,128)(2,1)} %bitcast.34), calls=%async_computation | async-start | bytes 1966080 | tf_op jit(solution)/shard_map/all_to_all | solution.py:681
  39.0 2.7 %collective-permute-start = (bf16[320,768]{1,0:T(8,128)(2,1)S(1)}, bf16[320,768]{1,0:T(8,128)(2,1)S(1)}, u32[]{:S(2)}, u32[]{:S(2)}) collective-permute-start(bf16[320,768]{1,0:T(8,128)(2,1)S(1)} %bitcast.37), channel_id=1, source_target_pairs={{0,16},{16,0},{1,17},{17,1},{2,18},{18,2},{3,19},{19,3},{4,20},{20... | collective-permute-start | bytes 1474568 | tf_op jit(solution)/shard_map/ppermute | solution.py:655
  43.8 5.5 %partial_0.1 = (bf16[1,2,2,320,768]{4,3,2,1,0:T(8,128)(2,1)S(1)}, bf16[1,320,1536]{2,1,0:T(8,128)(2,1)}) custom-call(s32[2]{0:T(128)S(1)} %copy-done.14, bf16[640,768]{1,0:T(8,128)(2,1)S(1)} %bitcast.26, bf16[320,768]{1,0:T(8,128)(2,1)S(1)} %collective-permute-done.other_low, bf16[320,768]{1,0:T(8,128)(2,1)S(1)} %collective-permute-done.1.other_high, ...), custom_call_target="tpu_custom_call" | custom-call | flops 27682406 | bytes 96337 | tf_op jit(solution)/shard_map/partial_0/pallas_call | solution.py:192
  51.8 9.9 %all-to-all-done = bf16[16,40,768]{2,1,0:T(8,128)(2,1)S(1)} async-done(((bf16[16,40,768]{2,1,0:T(8,128)(2,1)}), bf16[16,40,768]{2,1,0:T(8,128)(2,1)S(1)}, u32[]{:S(2)}, u32[]{:S(2)}) %all-to-all-start) | async-done | bytes 983072 | tf_op jit(solution)/shard_map/all_to_all | solution.py:681
  64.2 2.4 %collective-permute-done.3.other_high = bf16[320,768]{1,0:T(8,128)(2,1)S(1)} collective-permute-done((bf16[320,768]{1,0:T(8,128)(2,1)}, bf16[320,768]{1,0:T(8,128)(2,1)S(1)}, u32[]{:S(2)}, u32[]{:S(2)}) %collective-permute-start.3) | collective-permute-done | bytes 491552 | tf_op jit(solution)/shard_map/ppermute | solution.py:655
  66.8 6.0 %partial_1.1 = (bf16[1,2,2,320,768]{4,3,2,1,0:T(8,128)(2,1)S(1)}, bf16[1,320,1536]{2,1,0:T(8,128)(2,1)}) custom-call(s32[2]{0:T(128)S(1)} %copy-done.14, bf16[640,768]{1,0:T(8,128)(2,1)S(1)} %bitcast.25, bf16[320,768]{1,0:T(8,128)(2,1)} %collective-permute-done.2.other_low, bf16[320,768]{1,0:T(8,128)(2,1)S(1)} %collective-permute-done.3.other_high, ...), custom_call_target="tpu_custom_call" | custom-call | flops 27682406 | bytes 96337 | tf_op jit(solution)/shard_map/partial_1/pallas_call | solution.py:192
  76.5 3.9 %collective-permute-done.5.theirs = bf16[1,320,1536]{2,1,0:T(8,128)(2,1)} collective-permute-done((bf16[1,320,1536]{2,1,0:T(8,128)(2,1)}, bf16[1,320,1536]{2,1,0:T(8,128)(2,1)}, u32[]{:S(2)}, u32[]{:S(2)}) %collective-permute-start.5) | collective-permute-done | bytes 983072 | tf_op jit(solution)/shard_map/ppermute | solution.py:660
  80.3 6.1 %output_0.1 = (bf16[1,320,1536]{2,1,0:T(8,128)(2,1)S(1)}, bf16[1,320,768]{2,1,0:T(8,128)(2,1)S(1)}, bf16[1,320,768]{2,1,0:T(8,128)(2,1)S(1)}, bf16[1,320,768]{2,1,0:T(8,128)(2,1)S(1)}, bf16[1,320,768]{2,1,0:T(8,128)(2,1)S(1)}) custom-call(s32[2]{0:T(128)S(1)} %copy-done.14, bf16[1,320,1536]{2,1,0:T(8,128)(2,1)} %get-tuple-element.41.mine, ...), custom_call_target="tpu_custom_call" | custom-call | flops 45298483200 | bytes 289013760 | tf_op jit(solution)/shard_map/output_0/pallas_call | solution.py:270
  91.8 5.0 %all-to-all-start.2 = ((bf16[16,40,768]{2,1,0:T(8,128)(2,1)}), bf16[16,40,768]{2,1,0:T(8,128)(2,1)}, u32[]{:S(2)}, u32[]{:S(2)}) async-start(bf16[16,40,768]{2,1,0:T(8,128)(2,1)} %bitcast.28), calls=%async_computation.2 | async-start | bytes 1966080 | tf_op jit(solution)/shard_map/all_to_all | solution.py:681
  96.8 4.6 %collective-permute-done.4.theirs = bf16[1,320,1536]{2,1,0:T(8,128)(2,1)} collective-permute-done((bf16[1,320,1536]{2,1,0:T(8,128)(2,1)}, bf16[1,320,1536]{2,1,0:T(8,128)(2,1)}, u32[]{:S(2)}, u32[]{:S(2)}) %collective-permute-start.4) | collective-permute-done | bytes 983072 | tf_op jit(solution)/shard_map/ppermute | solution.py:660
  101.4 6.1 %output_1.1 = (bf16[1,320,1536]{2,1,0:T(8,128)(2,1)S(1)}, bf16[1,320,768]{2,1,0:T(8,128)(2,1)S(1)}, bf16[1,320,768]{2,1,0:T(8,128)(2,1)S(1)}, bf16[1,320,768]{2,1,0:T(8,128)(2,1)S(1)}, bf16[1,320,768]{2,1,0:T(8,128)(2,1)S(1)}) custom-call(s32[2]{0:T(128)S(1)} %copy-done.14, bf16[1,320,1536]{2,1,0:T(8,128)(2,1)} %get-tuple-element.43.mine, ...), custom_call_target="tpu_custom_call" | custom-call | flops 45298483200 | bytes 289013760 | tf_op jit(solution)/shard_map/output_1/pallas_call | solution.py:270
  113.7 5.9 %all-to-all-done.2 = bf16[16,40,768]{2,1,0:T(8,128)(2,1)} async-done(((bf16[16,40,768]{2,1,0:T(8,128)(2,1)}), bf16[16,40,768]{2,1,0:T(8,128)(2,1)}, u32[]{:S(2)}, u32[]{:S(2)}) %all-to-all-start.2) | async-done | bytes 983072 | tf_op jit(solution)/shard_map/all_to_all | solution.py:681
  119.6 5.2 %all-to-all-start.3 = ((bf16[16,40,768]{2,1,0:T(8,128)(2,1)}), bf16[16,40,768]{2,1,0:T(8,128)(2,1)}, u32[]{:S(2)}, u32[]{:S(2)}) async-start(bf16[16,40,768]{2,1,0:T(8,128)(2,1)} %bitcast.27), calls=%async_computation.3 | async-start | bytes 1966080 | tf_op jit(solution)/shard_map/all_to_all | solution.py:681
  127.7 5.8 %near_weight_grads.1.refs_4_ = bf16[3,3072,512]{2,1,0:T(8,128)(2,1)} custom-call(s32[2]{0:T(128)S(1)} %copy-done.14, bf16[1,320,1536]{2,1,0:T(8,128)(2,1)S(1)} %get-tuple-element.62.refs_0_, bf16[1,320,1536]{2,1,0:T(8,128)(2,1)S(1)} %copy-done.8, bf16[1,2,2,320,768]{4,3,2,1,0:T(8,128)(2,1)S(1)} %copy-done.2, bf16[1,2,2,320,768]{4,3,2,1,0:T(8,128)(2,1)S(1)} %copy-done.4), custom_call_target="tpu_custom_call" | custom-call | flops 15099494 | bytes 66846 | tf_op jit(solution)/shard_map/near_weight_grads/pallas_call | solution.py:572
  136.4 3.0 %gather_rows.1.earlier = f32[2,384,768]{2,1,0:T(8,128)S(1)} custom-call(s32[2]{0:T(128)S(1)} %copy-done.14, bf16[2,384,640]{2,1,0:T(8,128)(2,1)S(1)} %get-tuple-element.64.chooser, bf16[640,768]{1,0:T(8,128)(2,1)} %bitcast.15.returned), custom_call_target="tpu_custom_call" | custom-call | flops 7549747 | bytes 23592 | tf_op jit(solution)/shard_map/gather_rows/pallas_call | solution.py:400
  139.5 5.9 %collective-permute-done.10.refs_2_ = bf16[2,320,768]{2,1,0:T(8,128)(2,1)} collective-permute-done((bf16[2,320,768]{2,1,0:T(8,128)(2,1)}, bf16[2,320,768]{2,1,0:T(8,128)(2,1)}, u32[]{:S(2)}, u32[]{:S(2)}) %collective-permute-start.10) | collective-permute-done | bytes 983072 | tf_op jit(solution)/shard_map/ppermute | solution.py:660
  147.0 2.4 %collective-permute-done.11.refs_3_ = bf16[2,320,768]{2,1,0:T(8,128)(2,1)S(1)} collective-permute-done((bf16[2,320,768]{2,1,0:T(8,128)(2,1)}, bf16[2,320,768]{2,1,0:T(8,128)(2,1)S(1)}, u32[]{:S(2)}, u32[]{:S(2)}) %collective-permute-start.11) | collective-permute-done | bytes 983072 | tf_op jit(solution)/shard_map/ppermute | solution.py:655
  149.4 6.4 %far_weight_grads.1 = bf16[3,3072,512]{2,1,0:T(8,128)(2,1)} custom-call(s32[2]{0:T(128)S(1)} %copy-done.14, bf16[1,320,1536]{2,1,0:T(8,128)(2,1)S(1)} %copy-done.6, bf16[1,320,1536]{2,1,0:T(8,128)(2,1)S(1)} %copy-done.9, bf16[2,320,768]{2,1,0:T(8,128)(2,1)} %collective-permute-done.10.refs_2_, ...), custom_call_target="tpu_custom_call", output_to_operand_aliasing={{}: (5, {})} | custom-call | flops 15099494 | bytes 66846 | tf_op jit(solution)/shard_map/far_weight_grads/pallas_call | solution.py:622
  157.0 4.2 %combine.1 = (bf16[2,2,128,768]{3,2,1,0:T(8,128)(2,1)}, f32[128,128]{1,0:T(8,128)S(1)}, bf16[128,3072]{1,0:T(8,128)(2,1)}, bf16[128,3072]{1,0:T(8,128)(2,1)}) custom-call(s32[2]{0:T(128)S(1)} %copy-done.14, f32[128,2]{1,0:T(8,128)S(1)} %get-tuple-element.58.gates, bf16[128,3072]{1,0:T(8,128)(2,1)S(1)} %copy-done, bf16[2,384,640]{2,1,0:T(8,128)(2,1)S(1)} %copy-done.13, ...), custom_call_target="tpu_custom_call" | custom-call | flops 7549747 | bytes 19660 | tf_op jit(solution)/shard_map/combine/pallas_call | solution.py:452
  161.7 1.9 %collective-permute-done.13 = f32[128,128]{1,0:T(8,128)S(1)} collective-permute-done((f32[128,128]{1,0:T(8,128)S(1)}, f32[128,128]{1,0:T(8,128)S(1)}, u32[]{:S(2)}, u32[]{:S(2)}) %collective-permute-start.13) | collective-permute-done | bytes 65568 | tf_op jit(solution)/shard_map/ppermute | solution.py:655
  (70 shorter events, 34.4 us)
Async XLA Ops:
  4.8 29.1 %all-to-all-start.1 = ((bf16[16,40,768]{2,1,0:T(8,128)(2,1)}), bf16[16,40,768]{2,1,0:T(8,128)(2,1)S(1)}, u32[]{:S(2)}, u32[]{:S(2)}) async-start(bf16[16,40,768]{2,1,0:T(8,128)(2,1)} %bitcast.35), calls=%async_computation.1 | async-start | bytes 1966080 | tf_op jit(solution)/shard_map/all_to_all | solution.py:681
  15.1 28.8 %copy-start.14 = (s32[2]{0:T(128)S(1)}, s32[2]{0:T(128)}, u32[]{:S(2)}) copy-start(s32[2]{0:T(128)} %pad_add_fusion.ids) | copy-start | bytes 28
  34.0 27.7 %all-to-all-start = ((bf16[16,40,768]{2,1,0:T(8,128)(2,1)}), bf16[16,40,768]{2,1,0:T(8,128)(2,1)S(1)}, u32[]{:S(2)}, u32[]{:S(2)}) async-start(bf16[16,40,768]{2,1,0:T(8,128)(2,1)} %bitcast.34), calls=%async_computation | async-start | bytes 1966080 | tf_op jit(solution)/shard_map/all_to_all | solution.py:681
  39.0 4.2 %collective-permute-start = (bf16[320,768]{1,0:T(8,128)(2,1)S(1)}, bf16[320,768]{1,0:T(8,128)(2,1)S(1)}, u32[]{:S(2)}, u32[]{:S(2)}) collective-permute-start(bf16[320,768]{1,0:T(8,128)(2,1)S(1)} %bitcast.37), channel_id=1, source_target_pairs={{0,16},{16,0},{1,17},{17,1},{2,18},{18,2},{3,19},{19,3},{4,20},{20... | collective-permute-start | bytes 1474568 | tf_op jit(solution)/shard_map/ppermute | solution.py:655
  41.6 2.2 %collective-permute-start.1 = (bf16[320,768]{1,0:T(8,128)(2,1)S(1)}, bf16[320,768]{1,0:T(8,128)(2,1)S(1)}, u32[]{:S(2)}, u32[]{:S(2)}) collective-permute-start(bf16[320,768]{1,0:T(8,128)(2,1)S(1)} %bitcast.36), channel_id=1, source_target_pairs={{0,16},{16,0},{1,17},{17,1},{2,18},{18,2},{3,19},{19,3},{4,20},{20... | collective-permute-start | bytes 1474568 | tf_op jit(solution)/shard_map/ppermute | solution.py:655
  50.6 29.8 %collective-permute-start.5 = (bf16[1,320,1536]{2,1,0:T(8,128)(2,1)}, bf16[1,320,1536]{2,1,0:T(8,128)(2,1)}, u32[]{:S(2)}, u32[]{:S(2)}) collective-permute-start(bf16[1,320,1536]{2,1,0:T(8,128)(2,1)} %get-tuple-element.41.mine), channel_id=1, source_target_pairs={{0,1},{1,0},{2,3},{3,2},{4,5},{5,4},{6,7},{7,6},{8,9},{9,8},{10,11... | collective-permute-start | bytes 2949128 | tf_op jit(solution)/shard_map/ppermute | solution.py:660
  62.7 3.9 %collective-permute-start.3 = (bf16[320,768]{1,0:T(8,128)(2,1)}, bf16[320,768]{1,0:T(8,128)(2,1)S(1)}, u32[]{:S(2)}, u32[]{:S(2)}) collective-permute-start(bf16[320,768]{1,0:T(8,128)(2,1)} %get-tuple-element.82), channel_id=1, source_target_pairs={{0,16},{16,0},{1,17},{17,1},{2,18},{18,2},{3,19},{19,3},{4,20},{20... | collective-permute-start | bytes 1474568 | tf_op jit(solution)/shard_map/ppermute | solution.py:655
  64.2 2.5 %collective-permute-start.2 = (bf16[320,768]{1,0:T(8,128)(2,1)}, bf16[320,768]{1,0:T(8,128)(2,1)}, u32[]{:S(2)}, u32[]{:S(2)}) collective-permute-start(bf16[320,768]{1,0:T(8,128)(2,1)} %get-tuple-element.83), channel_id=1, source_target_pairs={{0,16},{16,0},{1,17},{17,1},{2,18},{18,2},{3,19},{19,3},{4,20},{20... | collective-permute-start | bytes 1474568 | tf_op jit(solution)/shard_map/ppermute | solution.py:655
  72.8 28.6 %collective-permute-start.4 = (bf16[1,320,1536]{2,1,0:T(8,128)(2,1)}, bf16[1,320,1536]{2,1,0:T(8,128)(2,1)}, u32[]{:S(2)}, u32[]{:S(2)}) collective-permute-start(bf16[1,320,1536]{2,1,0:T(8,128)(2,1)} %get-tuple-element.43.mine), channel_id=1, source_target_pairs={{0,1},{1,0},{2,3},{3,2},{4,5},{5,4},{6,7},{7,6},{8,9},{9,8},{10,11... | collective-permute-start | bytes 2949128 | tf_op jit(solution)/shard_map/ppermute | solution.py:660
  86.5 38.4 %copy-start.5 = (bf16[1,320,1536]{2,1,0:T(8,128)(2,1)}, bf16[1,320,1536]{2,1,0:T(8,128)(2,1)S(1)}, u32[]{:S(2)}) copy-start(bf16[1,320,1536]{2,1,0:T(8,128)(2,1)S(1)} %get-tuple-element.62.refs_0_) | copy-start | bytes 2949124
  86.5 2.4 %collective-permute-start.6 = (bf16[1,320,768]{2,1,0:T(8,128)(2,1)S(1)}, bf16[1,320,768]{2,1,0:T(8,128)(2,1)S(1)}, u32[]{:S(2)}, u32[]{:S(2)}) collective-permute-start(bf16[1,320,768]{2,1,0:T(8,128)(2,1)S(1)} %get-tuple-element.49), channel_id=1, source_target_pairs={{0,16},{16,0},{1,17},{17,1},{2,18},{18,2},{3,19},{19,3},{4,20},{20... | collective-permute-start | bytes 1474568 | tf_op jit(solution)/shard_map/ppermute | solution.py:655
  87.4 2.2 %collective-permute-start.7 = (bf16[1,320,768]{2,1,0:T(8,128)(2,1)S(1)}, bf16[1,320,768]{2,1,0:T(8,128)(2,1)S(1)}, u32[]{:S(2)}, u32[]{:S(2)}) collective-permute-start(bf16[1,320,768]{2,1,0:T(8,128)(2,1)S(1)} %get-tuple-element.50), channel_id=1, source_target_pairs={{0,16},{16,0},{1,17},{17,1},{2,18},{18,2},{3,19},{19,3},{4,20},{20... | collective-permute-start | bytes 1474568 | tf_op jit(solution)/shard_map/ppermute | solution.py:655
  91.8 27.8 %all-to-all-start.2 = ((bf16[16,40,768]{2,1,0:T(8,128)(2,1)}), bf16[16,40,768]{2,1,0:T(8,128)(2,1)}, u32[]{:S(2)}, u32[]{:S(2)}) async-start(bf16[16,40,768]{2,1,0:T(8,128)(2,1)} %bitcast.28), calls=%async_computation.2 | async-start | bytes 1966080 | tf_op jit(solution)/shard_map/all_to_all | solution.py:681
  108.5 2.3 %collective-permute-start.8 = (bf16[1,320,768]{2,1,0:T(8,128)(2,1)S(1)}, bf16[1,320,768]{2,1,0:T(8,128)(2,1)S(1)}, u32[]{:S(2)}, u32[]{:S(2)}) collective-permute-start(bf16[1,320,768]{2,1,0:T(8,128)(2,1)S(1)} %get-tuple-element.54), channel_id=1, source_target_pairs={{0,16},{16,0},{1,17},{17,1},{2,18},{18,2},{3,19},{19,3},{4,20},{20... | collective-permute-start | bytes 1474568 | tf_op jit(solution)/shard_map/ppermute | solution.py:655
  109.3 2.2 %collective-permute-start.9 = (bf16[1,320,768]{2,1,0:T(8,128)(2,1)S(1)}, bf16[1,320,768]{2,1,0:T(8,128)(2,1)S(1)}, u32[]{:S(2)}, u32[]{:S(2)}) collective-permute-start(bf16[1,320,768]{2,1,0:T(8,128)(2,1)S(1)} %get-tuple-element.55), channel_id=1, source_target_pairs={{0,16},{16,0},{1,17},{17,1},{2,18},{18,2},{3,19},{19,3},{4,20},{20... | collective-permute-start | bytes 1474568 | tf_op jit(solution)/shard_map/ppermute | solution.py:655
  109.3 36.1 %collective-permute-start.10 = (bf16[2,320,768]{2,1,0:T(8,128)(2,1)}, bf16[2,320,768]{2,1,0:T(8,128)(2,1)}, u32[]{:S(2)}, u32[]{:S(2)}) collective-permute-start(bf16[2,320,768]{2,1,0:T(8,128)(2,1)} %select_bitcast_fusion), channel_id=1, source_target_pairs={{0,1},{1,0},{2,3},{3,2},{4,5},{5,4},{6,7},{7,6},{8,9},{9,8},{10,11... | collective-permute-start | bytes 2949128 | tf_op jit(solution)/shard_map/ppermute | solution.py:660
  111.5 13.3 %copy-start.16 = (f32[128,2]{0,1:T(2,128)S(1)}, f32[128,2]{0,1:T(2,128)}, u32[]{:S(2)}) copy-start(f32[128,2]{0,1:T(2,128)} %param.9) | copy-start | bytes 3076
  119.6 36.2 %all-to-all-start.3 = ((bf16[16,40,768]{2,1,0:T(8,128)(2,1)}), bf16[16,40,768]{2,1,0:T(8,128)(2,1)}, u32[]{:S(2)}, u32[]{:S(2)}) async-start(bf16[16,40,768]{2,1,0:T(8,128)(2,1)} %bitcast.27), calls=%async_computation.3 | async-start | bytes 1966080 | tf_op jit(solution)/shard_map/all_to_all | solution.py:681
  133.6 15.8 %copy-start.6 = (bf16[1,320,1536]{2,1,0:T(8,128)(2,1)S(1)}, bf16[1,320,1536]{2,1,0:T(8,128)(2,1)}, u32[]{:S(2)}) copy-start(bf16[1,320,1536]{2,1,0:T(8,128)(2,1)} %copy-done.5) | copy-start | bytes 2949124
  133.6 15.8 %copy-start.9 = (bf16[1,320,1536]{2,1,0:T(8,128)(2,1)S(1)}, bf16[1,320,1536]{2,1,0:T(8,128)(2,1)}, u32[]{:S(2)}) copy-start(bf16[1,320,1536]{2,1,0:T(8,128)(2,1)} %copy-done.7) | copy-start | bytes 2949124
  139.5 16.3 %copy-start = (bf16[128,3072]{1,0:T(8,128)(2,1)S(1)}, bf16[128,3072]{1,0:T(8,128)(2,1)}, u32[]{:S(2)}) copy-start(bf16[128,3072]{1,0:T(8,128)(2,1)} %cotangent.5) | copy-start | bytes 2359300
  145.4 4.0 %collective-permute-start.11 = (bf16[2,320,768]{2,1,0:T(8,128)(2,1)}, bf16[2,320,768]{2,1,0:T(8,128)(2,1)S(1)}, u32[]{:S(2)}, u32[]{:S(2)}) collective-permute-start(bf16[2,320,768]{2,1,0:T(8,128)(2,1)} %collective-permute-done.10.refs_2_), channel_id=1, source_target_pairs={{0,16},{16,0},{1,17},{17,1},{2,18},{18,2},{3,19},{19,3},{4,20},{20... | collective-permute-start | bytes 2949128 | tf_op jit(solution)/shard_map/ppermute | solution.py:655
  161.2 3.0 %collective-permute-start.12 = (bf16[2,2,128,768]{3,2,1,0:T(8,128)(2,1)}, bf16[2,2,128,768]{3,2,1,0:T(8,128)(2,1)S(1)}, u32[]{:S(2)}, u32[]{:S(2)}) collective-permute-start(bf16[2,2,128,768]{3,2,1,0:T(8,128)(2,1)} %get-tuple-element.71), channel_id=1, source_target_pairs={{0,16},{16,0},{1,17},{17,1},{2,18},{18,2},{3,19},{19,3},{4,20},{20... | collective-permute-start | bytes 2359304 | tf_op jit(solution)/shard_map/ppermute | solution.py:655
  161.6 2.0 %collective-permute-start.13 = (f32[128,128]{1,0:T(8,128)S(1)}, f32[128,128]{1,0:T(8,128)S(1)}, u32[]{:S(2)}, u32[]{:S(2)}) collective-permute-start(f32[128,128]{1,0:T(8,128)S(1)} %get-tuple-element.76), channel_id=1, source_target_pairs={{0,16},{16,0},{1,17},{17,1},{2,18},{18,2},{3,19},{19,3},{4,20},{20... | collective-permute-start | bytes 196616 | tf_op jit(solution)/shard_map/ppermute | solution.py:655
  (12 other events, 32.1 us)

commit v2 on v1

--- a/solution.py
+++ b/solution.py
@@ -12,7 +12,7 @@
 BF16 = jnp.bfloat16
 CHUNKS = 2
 MIB = 1024 * 1024
-BIG = 48
+BIG = 44
 
 
 def dot(left, right, left_dim, right_dim):
@@ -44,44 +44,107 @@
     return whole, index - whole * size
 
 
-def dispatch_kernel(dims, chunk, ids, routes, gates, tokens, cotangent, sent, picks, scales):
+def mark_picks(dims, chunk, routes, gates, picks, scales):
     subs, groups, per_chunk, cap, block = dims
     token_count = routes.shape[1]
-
-    @pl.when(pl.program_id(0) == 0)
-    def _():
-        route = [routes[k : k + 1, :] for k in range(2)]
-        gate = [gates[k : k + 1, :] for k in range(2)]
-        sub = iota((subs, token_count), 0)
-        hits = [(route[k] == sub).astype(F32) for k in range(2)]
-        earlier = (iota((token_count,) * 2, 0) < iota((token_count,) * 2, 1)).astype(BF16)
-        before = dot((hits[0] + hits[1]).astype(BF16), earlier, 1, 0)
-        slot = [jnp.sum(hits[k] * before, axis=0, keepdims=True) for k in range(2)]
-        slot[1] = slot[1] + (route[0] == route[1]).astype(F32)
-        row = iota((block, token_count), 0)
-        row = jnp.where(row >= block // 2, row - block // 2, row)
-        local = jnp.zeros_like(row)
-        for i in range(1, per_chunk):
-            local = local + (row >= i * cap).astype(jnp.int32)
-        place = (row - local * cap).astype(F32)
-        for e in range(subs // groups):
-            wanted = local + (e * groups + chunk * per_chunk)
-            match = [(route[k] == wanted) & (slot[k] == place) for k in range(2)]
-            scale = jnp.where(match[0], gate[0], 0.0) + jnp.where(match[1], gate[1], 0.0)
-            scales[e * block : (e + 1) * block, :] = jnp.broadcast_to(
-                jnp.sum(scale, axis=1, keepdims=True), scale.shape
-            )
-            picks[e * block : (e + 1) * block, :] = (
-                match[0].astype(F32) + match[1].astype(F32)
-            ).astype(BF16)
-
+    route = [routes[k : k + 1, :] for k in range(2)]
+    gate = [gates[k : k + 1, :] for k in range(2)]
+    sub = iota((subs, token_count), 0)
+    hits = [(route[k] == sub).astype(F32) for k in range(2)]
+    earlier = (iota((token_count,) * 2, 0) < iota((token_count,) * 2, 1)).astype(BF16)
+    before = dot((hits[0] + hits[1]).astype(BF16), earlier, 1, 0)
+    slot = [jnp.sum(hits[k] * before, axis=0, keepdims=True) for k in range(2)]
+    slot[1] = slot[1] + (route[0] == route[1]).astype(F32)
+    row = iota((block, token_count), 0)
+    row = jnp.where(row >= block // 2, row - block // 2, row)
+    local = jnp.zeros_like(row)
+    for i in range(1, per_chunk):
+        local = local + (row >= i * cap).astype(jnp.int32)
+    place = (row - local * cap).astype(F32)
+    for e in range(subs // groups):
+        wanted = local + (e * groups + chunk * per_chunk)
+        match = [(route[k] == wanted) & (slot[k] == place) for k in range(2)]
+        scale = jnp.where(match[0], gate[0], 0.0) + jnp.where(match[1], gate[1], 0.0)
+        scales[e * block : (e + 1) * block, :] = jnp.broadcast_to(
+            jnp.sum(scale, axis=1, keepdims=True), scale.shape
+        )
+        picks[e * block : (e + 1) * block, :] = (
+            match[0].astype(F32) + match[1].astype(F32)
+        ).astype(BF16)
+
+
+def place_rows(block, picks, scales, tokens, cotangent, store):
     rows = picks[...]
-    chosen = dot(rows, tokens[...], 1, 0)
-    graded = dot(rows, cotangent[...], 1, 0) * scales[:, :1]
-    for e in range(subs // groups):
+    chosen = dot(rows, tokens, 1, 0)
+    graded = dot(rows, cotangent, 1, 0) * scales[:, :1]
+    for e in range(rows.shape[0] // block):
         part = slice(e * block, (e + 1) * block)
         first = iota((block, 1), 0) < block // 2
-        sent[e] = jnp.where(first, chosen[part], graded[part]).astype(BF16)
+        store(e, jnp.where(first, chosen[part], graded[part]).astype(BF16))
+
+
+def dispatch_kernel(dims, chunk, aligned, routes, gates, tokens, cotangent, sent, *scratch):
+    subs, groups, per_chunk, cap, block = dims
+    picks, scales, columns, arrivals = scratch
+    token_count = routes.shape[1]
+    width = sent.shape[3]
+    loads = []
+    for p in range(groups):
+        for i, source in enumerate((tokens, cotangent)):
+            if aligned:
+                first = pl.multiple_of((2 * p + lax.axis_index("dp")) * width, 128)
+                source = source.at[:, pl.ds(first, width)]
+            else:
+                source = source.at[p]
+            loads.append(pltpu.make_async_copy(source, columns.at[p, i], arrivals.at[p, i]))
+            loads[-1].start()
+    mark_picks(dims, chunk, routes[...], gates[...], picks, scales)
+    for p in range(groups):
+        loads[2 * p].wait()
+        loads[2 * p + 1].wait()
+
+        def store(e, value, p=p):
+            sent[e, p] = value
+
+        place_rows(block, picks, scales, columns[p, 0], columns[p, 1], store)
+
+
+def group_kernel(dims, chunk, *refs):
+    groups, block = dims[1], dims[4]
+    infos, columns = refs[:groups], refs[groups : 2 * groups]
+    sent, picks, scales = refs[2 * groups :]
+    holder = lax.axis_index("expert") % groups
+    for mask in range(groups):
+        info = infos[mask][...]
+        mark_picks(dims, chunk, info[:2].astype(jnp.int32), info[2:], picks, scales)
+
+        def store(e, value, mask=mask):
+            sent[e, holder ^ mask] = value
+
+        place_rows(block, picks, scales, columns[mask][0], columns[mask][1], store)
+
+
+def group_dispatch(dims, chunk, infos, columns):
+    subs, groups, per_chunk, cap, block = dims
+    experts = subs // groups
+    token_count, width = columns[0].shape[1:]
+    vmem = pl.BlockSpec(memory_space=pltpu.VMEM)
+    return pl.pallas_call(
+        functools.partial(group_kernel, dims, chunk),
+        out_shape=jax.ShapeDtypeStruct((experts, groups, block, width), BF16),
+        in_specs=[vmem] * (2 * groups),
+        out_specs=vmem,
+        scratch_shapes=[
+            pltpu.VMEM((experts * block, token_count), BF16),
+            pltpu.VMEM((experts * block, token_count), F32),
+        ],
+        compiler_params=params(60),
+        cost_estimate=cost(
+            2 * experts * block * token_count * width * groups,
+            2 * (2 * token_count + experts * block) * width * groups,
+        ),
+        name=f"group_dispatch_{chunk}",
+    )(*infos, *columns)
 
 
 def quarter(value, groups, width):
@@ -94,33 +157,29 @@
     return own.transpose(1, 0, 2), pl.BlockSpec((None, rows, width), lambda p, ids: (p, 0, 0))
 
 
-def dispatch(dims, chunk, width, ids, routes, gates, tokens, cotangent):
+def dispatch(dims, chunk, width, routes, gates, tokens, cotangent):
     subs, groups, per_chunk, cap, block = dims
     experts = subs // groups
     token_count = routes.shape[1]
-    whole = lambda shape: pl.BlockSpec(shape, lambda p, ids: (0,) * len(shape))
-    tokens, tokens_spec = tokens
-    cotangent, cotangent_spec = cotangent
-    return pl.pallas_call(
-        functools.partial(dispatch_kernel, dims, chunk),
+    vmem = pl.BlockSpec(memory_space=pltpu.VMEM)
+    return pl.pallas_call(
+        functools.partial(dispatch_kernel, dims, chunk, tokens.ndim == 2),
         out_shape=jax.ShapeDtypeStruct((experts, groups, block, width), BF16),
-        grid_spec=pltpu.PrefetchScalarGridSpec(
-            num_scalar_prefetch=1,
-            grid=(groups,),
-            in_specs=[whole(routes.shape), whole(gates.shape), tokens_spec, cotangent_spec],
-            out_specs=pl.BlockSpec((experts, None, block, width), lambda p, ids: (0, p, 0, 0)),
-            scratch_shapes=[
-                pltpu.VMEM((experts * block, token_count), BF16),
-                pltpu.VMEM((experts * block, token_count), F32),
-            ],
-        ),
+        in_specs=[vmem, vmem] + [pl.BlockSpec(memory_space=pl.ANY)] * 2,
+        out_specs=vmem,
+        scratch_shapes=[
+            pltpu.VMEM((experts * block, token_count), BF16),
+            pltpu.VMEM((experts * block, token_count), F32),
+            pltpu.VMEM((groups, 2, token_count, width), BF16),
+            pltpu.SemaphoreType.DMA((groups, 2)),
+        ],
         compiler_params=params(60),
         cost_estimate=cost(
             2 * experts * block * token_count * width * groups,
             2 * (2 * token_count + experts * block) * width * groups,
         ),
         name=f"dispatch_{chunk}",
-    )(ids, routes, gates, tokens, cotangent)
+    )(routes, gates, tokens, cotangent)
 
 
 def partial_kernel(dims, chunk, ids, own, other_low, other_high, weights, *rest):
@@ -192,7 +251,7 @@
     return pl.pallas_call(
         functools.partial(partial_kernel, dims, chunk),
         out_shape=(
-            jax.ShapeDtypeStruct((per_chunk, 2, 2, rows, width), BF16),
+            pltpu.HBM((per_chunk, 2, 2, rows, width), BF16),
             jax.ShapeDtypeStruct((per_chunk, rows, 3 * units), BF16),
         ),
         grid_spec=pltpu.PrefetchScalarGridSpec(
@@ -269,7 +328,7 @@
     out = jax.ShapeDtypeStruct((per_chunk, rows, width), BF16)
     return pl.pallas_call(
         functools.partial(output_kernel, dims, chunk),
-        out_shape=(jax.ShapeDtypeStruct((per_chunk, rows, 3 * units), BF16),) + (out,) * 4,
+        out_shape=(pltpu.HBM((per_chunk, rows, 3 * units), BF16),) + (out,) * 4,
         grid_spec=pltpu.PrefetchScalarGridSpec(
             num_scalar_prefetch=1,
             grid=(1,),
@@ -321,7 +380,7 @@
     spec = pl.BlockSpec((per_chunk, rows, columns), lambda c: (0, 0, c))
     return pl.pallas_call(
         functools.partial(pack_kernel, dims),
-        out_shape=jax.ShapeDtypeStruct((subs * block, width), BF16),
+        out_shape=pltpu.HBM((subs * block, width), BF16),
         grid=(width // columns,),
         in_specs=[spec] * 4,
         out_specs=pl.BlockSpec((subs * block, columns), lambda c: (0, c)),
@@ -373,7 +432,7 @@
     marks[2] = half
     marks[3] = device % groups
     whole = lambda shape: pl.BlockSpec(shape, lambda p, ids: (0,) * len(shape))
-    shape = jax.ShapeDtypeStruct((groups, 3 * token_count, subs * block), BF16)
+    shape = pltpu.HBM((groups, 3 * token_count, subs * block), BF16)
     spec = pl.BlockSpec((None, 3 * token_count, subs * block), lambda p, ids: (p, 0, 0))
     return pl.pallas_call(
         functools.partial(chooser_kernel, dims),
@@ -676,16 +735,42 @@
     own_tokens = quarter(tokens, groups, width)
     own_cotangent = quarter(cotangent, groups, width)
 
+    aligned = width % 128 == 0
+    whole_or_own = (tokens, cotangent) if aligned else (own_tokens[0], own_cotangent[0])
+
     def exchange(rows):
         blocks = rows.reshape(subs, block, width)
         moved = lax.all_to_all(blocks, "expert", split_axis=0, concat_axis=0, tiled=True)
         return moved.reshape(subs * block, width)
 
-    sent = [
-        dispatch(dims, c, width, ids, routes.T, gate_values.T, own_tokens, own_cotangent)
-        for c in range(CHUNKS)
-    ]
-    arrived = [exchange(value) for value in sent]
+    sent = dispatch(dims, 0, width, routes.T, gate_values.T, *whole_or_own)
+    sent, tokens, cotangent = together(sent, tokens, cotangent)
+    arrived = [exchange(sent)]
+
+    def columns(mask):
+        first = (2 * (holder ^ mask) + core) * width
+        parts = [
+            lax.dynamic_slice_in_dim(value, first, width, 1) for value in (tokens, cotangent)
+        ]
+        return jnp.stack(parts)
+
+    info = jnp.concatenate([routes.T.astype(F32), gate_values.T], axis=0)
+    infos = [info] + [swap_holders(info, mask) for mask in range(1, groups)]
+    parts = [columns(0)] + [swap_holders(columns(mask), mask) for mask in range(1, groups)]
+    gates, *choosers = return_choosers(dims, ids, routes, gate_values)
+    peers = [list(range(p, subs, groups)) for p in range(groups)]
+    for c in range(1, CHUNKS):
+        sent = group_dispatch(dims, c, infos, parts)
+        sent, gates, *choosers = together(sent, gates, *choosers)
+        moved = lax.all_to_all(
+            sent.reshape(subs // groups, groups * block, width),
+            "expert",
+            split_axis=0,
+            concat_axis=0,
+            tiled=True,
+            axis_index_groups=peers,
+        )
+        arrived.append(moved.reshape(subs * block, width))
     features, acts, mine, theirs, returned = [], [], [], [], []
     for c in range(CHUNKS):
         others = [swap_cores(part) for part in jnp.split(arrived[c], 2)]
@@ -710,15 +795,13 @@
         if c + 1 < CHUNKS:
             theirs[c + 1], _ = together(theirs[c + 1], packed)
         if c > 0:
-            packed, returned[c - 1] = together(packed, returned[c - 1])
+            weight_grad = near_weight_grads(ids, acts, features)
+            packed, returned[c - 1], weight_grad = together(packed, returned[c - 1], weight_grad)
         returned.append(exchange(packed))
     theirs[-1], *leaving = together(theirs[-1], *leaving)
-    routes, packed = together(routes, packed)
-    gates, *choosers = return_choosers(dims, ids, routes, gate_values)
     earlier = gather_rows(ids, choosers[0], returned[0])
     for c in range(1, CHUNKS - 1):
         earlier = earlier + gather_rows(ids, choosers[c], returned[c])
-    weight_grad = near_weight_grads(ids, acts, features)
     far = []
     for mask in range(1, groups):
         near = swap_holders(leaving[mask - 1], mask)

time: 167 us -> 158 us (0.946); the launches traced: 166 us -> 155 us
  waiting for transfers between devices: 61.9 us -> 47.5 us
  starting transfers between devices: 32.7 us -> 37.6 us
  local copies, waits for them, and re-layouts: 12.4 us -> 9.06 us
    all_to_all x4 -> x3, waiting for transfers between devices: 34.7 us -> 6.14 us  [exchange(): lax.all_to_all(blocks, 'expert', split_axis=0, concat_axis=0, tiled=True)]
    all_to_all x0 -> x1, waiting for transfers between devices: none -> 8.28 us  [shards(): lax.all_to_all(sent.reshape(subs // groups, groups * block, width), 'expe...]
    ppermute x3 -> x5, waiting for transfers between devices: 14.4 us -> 22.1 us  [swap_holders(): lax.ppermute(value, 'expert', [(source, source ^ mask) for source in rang...]
    all_to_all x0 -> x1, starting transfers between devices: none -> 5.37 us  [shards(): lax.all_to_all(sent.reshape(subs // groups, groups * block, width), 'expe...]
    all_to_all x4 -> x3, starting transfers between devices: 21.7 us -> 16.9 us  [exchange(): lax.all_to_all(blocks, 'expert', split_axis=0, concat_axis=0, tiled=True)]
    ppermute x11, starting transfers between devices: 8.11 us -> 12.7 us  [swap_cores(): return lax.ppermute(value, 'dp', [(0, 1), (1, 0)])]
    unnamed x38 -> x41, local copies, waits for them, and re-layouts: 11.2 us -> 8.08 us
    ppermute x11, waiting for transfers between devices: 12.8 us -> 10.9 us  [swap_cores(): return lax.ppermute(value, 'dp', [(0, 1), (1, 0)])]
  transfers between devices with their start and end apart: 18 -> 20, of which waited for: 16 -> 14; matrix products, arithmetic and copies ran while one was open for 2% -> 3% of each run, Pallas kernels for 28% -> 31%
where the time goes in v2:
time: 158 us; the launch traced here: 155 us
  Pallas kernels  56.9 us (36%)
  waiting for transfers between devices  47.5 us (30%)
  starting transfers between devices  37.6 us (24%)
  local copies, waits for them, and re-layouts  9.06 us (6%)
  other arithmetic  3.17 us (2%)
    ppermute x5, waiting for transfers between devices, swap_holders(): lax.ppermute(value, 'expert', [(source, source ^ mask) for source in rang...  22.1 us
    all_to_all x3, starting transfers between devices, exchange(): lax.all_to_all(blocks, 'expert', split_axis=0, concat_axis=0, tiled=True)  16.9 us
    ppermute x11, starting transfers between devices, swap_cores(): return lax.ppermute(value, 'dp', [(0, 1), (1, 0)])  12.7 us
    pallas_call x2, Pallas kernels, output_products(): pl.pallas_call(functools.partial(output_kernel, dims, chunk), out_shape=(...  12 us
    pallas_call x2, Pallas kernels, partial_products(): pl.pallas_call(functools.partial(partial_kernel, dims, chunk), out_shape=...  11 us
    ppermute x11, waiting for transfers between devices, swap_cores(): return lax.ppermute(value, 'dp', [(0, 1), (1, 0)])  10.9 us
    all_to_all x1, waiting for transfers between devices, shards(): lax.all_to_all(sent.reshape(subs // groups, groups * block, width), 'expe...  8.28 us
    unnamed x41, local copies, waits for them, and re-layouts  8.08 us
  transfers between devices with their start and end apart: 20, of which 14 were waited for; matrix products, arithmetic and copies ran while one was open for 3% of the time, Pallas kernels for 31%

profile of v2, /device:TPU:17, one launch (start us, length us, event | category | flops | bytes accessed | tf_op | source)
XLA Modules:
  0.0 155.0 jit_solution(5979299228585876342)
XLA Ops:
  0.7 3.7 %dispatch_0.1 = bf16[8,2,40,768]{3,2,1,0:T(8,128)(2,1)} custom-call(s32[2,128]{1,0:T(2,128)} %bitcast.48, f32[2,128]{1,0:T(2,128)} %bitcast.49, bf16[128,3072]{1,0:T(8,128)(2,1)} %tokens.1, bf16[128,3072]{1,0:T(8,128)(2,1)} %cotangent.3), custom_call_target="tpu_custom_call" | custom-call | flops 2516582 | bytes 17694 | tf_op jit(solution)/shard_map/dispatch_0/pallas_call | solution.py:165
  4.4 6.7 %all-to-all-start.1 = ((bf16[16,40,768]{2,1,0:T(8,128)(2,1)}), bf16[16,40,768]{2,1,0:T(8,128)(2,1)S(1)}, u32[]{:S(2)}, u32[]{:S(2)}) async-start(bf16[16,40,768]{2,1,0:T(8,128)(2,1)} %bitcast.43), calls=%async_computation.1 | async-start | bytes 1966080 | tf_op jit(solution)/shard_map/all_to_all | solution.py:743
  13.9 2.7 %choosers.1 = (f32[128,2]{1,0:T(8,128)S(1)}, bf16[2,384,640]{2,1,0:T(8,128)(2,1)}, bf16[2,384,640]{2,1,0:T(8,128)(2,1)}) custom-call(s32[2]{0:T(128)S(1)} %pad_add_fusion.ids, s32[128,2]{1,0:T(8,128)S(1)} %copy.13.routes, f32[128,2]{1,0:T(8,128)S(1)} %copy.14.gates, s32[8,640]{1,0:T(8,128)S(1)} %copy-done.12), custom_call_target="tpu_custom_call" | custom-call | bytes 19660 | tf_op jit(solution)/shard_map/choosers/pallas_call | solution.py:437
  16.7 8.3 %collective-permute-done.refs_1_ = f32[4,128]{1,0:T(4,128)S(1)} collective-permute-done((f32[4,128]{1,0:T(4,128)S(1)}, f32[4,128]{1,0:T(4,128)S(1)}, u32[]{:S(2)}, u32[]{:S(2)}) %collective-permute-start) | collective-permute-done | bytes 2080 | tf_op jit(solution)/shard_map/ppermute | solution.py:719
  26.3 3.0 %group_dispatch_1.1 = bf16[8,2,40,768]{3,2,1,0:T(8,128)(2,1)} custom-call(f32[4,128]{1,0:T(4,128)} %copy-done.17, f32[4,128]{1,0:T(4,128)} %copy-done.18, bf16[2,128,768]{2,1,0:T(8,128)(2,1)} %pad_maximum_fusion.refs_2_, bf16[2,128,768]{2,1,0:T(8,128)(2,1)} %copy-done.14), custom_call_target="tpu_custom_call" | custom-call | flops 2516582 | bytes 17694 | tf_op jit(solution)/shard_map/group_dispatch_1/pallas_call | solution.py:132
  29.4 4.3 %all-to-all-done.1 = bf16[16,40,768]{2,1,0:T(8,128)(2,1)S(1)} async-done(((bf16[16,40,768]{2,1,0:T(8,128)(2,1)}), bf16[16,40,768]{2,1,0:T(8,128)(2,1)S(1)}, u32[]{:S(2)}, u32[]{:S(2)}) %all-to-all-start.1) | async-done | bytes 983072 | tf_op jit(solution)/shard_map/all_to_all | solution.py:743
  33.7 5.4 %all-to-all-start = ((bf16[8,80,768]{2,1,0:T(8,128)(2,1)}), bf16[8,80,768]{2,1,0:T(8,128)(2,1)S(1)}, u32[]{:S(2)}, u32[]{:S(2)}) async-start(bf16[8,80,768]{2,1,0:T(8,128)(2,1)} %bitcast.42), calls=%async_computation | async-start | bytes 1966080 | tf_op jit(solution)/shard_map/all_to_all | solution.py:765
  39.1 3.6 %collective-permute-start.2 = (bf16[320,768]{1,0:T(8,128)(2,1)S(1)}, bf16[320,768]{1,0:T(8,128)(2,1)S(1)}, u32[]{:S(2)}, u32[]{:S(2)}) collective-permute-start(bf16[320,768]{1,0:T(8,128)(2,1)S(1)} %bitcast.47), channel_id=1, source_target_pairs={{0,16},{16,0},{1,17},{17,1},{2,18},{18,2},{3,19},{19,3},{4,20},{20... | collective-permute-start | bytes 1474568 | tf_op jit(solution)/shard_map/ppermute | solution.py:714
  44.9 5.5 %partial_0.1 = (bf16[1,2,2,320,768]{4,3,2,1,0:T(8,128)(2,1)}, bf16[1,320,1536]{2,1,0:T(8,128)(2,1)}) custom-call(s32[2]{0:T(128)S(1)} %pad_add_fusion.ids, bf16[640,768]{1,0:T(8,128)(2,1)S(1)} %bitcast.33, bf16[320,768]{1,0:T(8,128)(2,1)S(1)} %collective-permute-done.2.other_low, bf16[320,768]{1,0:T(8,128)(2,1)S(1)} %collective-permute-done.3.other_high, ...), custom_call_target="tpu_custom_call" | custom-call | flops 27682406 | bytes 96337 | tf_op jit(solution)/shard_map/partial_0/pallas_call | solution.py:251
  50.7 8.3 %all-to-all-done = bf16[8,80,768]{2,1,0:T(8,128)(2,1)S(1)} async-done(((bf16[8,80,768]{2,1,0:T(8,128)(2,1)}), bf16[8,80,768]{2,1,0:T(8,128)(2,1)S(1)}, u32[]{:S(2)}, u32[]{:S(2)}) %all-to-all-start) | async-done | bytes 983072 | tf_op jit(solution)/shard_map/all_to_all | solution.py:765
  59.9 2.6 %collective-permute-start.5 = (bf16[320,768]{1,0:T(8,128)(2,1)}, bf16[320,768]{1,0:T(8,128)(2,1)S(1)}, u32[]{:S(2)}, u32[]{:S(2)}) collective-permute-start(bf16[320,768]{1,0:T(8,128)(2,1)} %get-tuple-element.96), channel_id=1, source_target_pairs={{0,16},{16,0},{1,17},{17,1},{2,18},{18,2},{3,19},{19,3},{4,20},{20... | collective-permute-start | bytes 1474568 | tf_op jit(solution)/shard_map/ppermute | solution.py:714
  62.5 2.4 %collective-permute-done.5.other_high = bf16[320,768]{1,0:T(8,128)(2,1)S(1)} collective-permute-done((bf16[320,768]{1,0:T(8,128)(2,1)}, bf16[320,768]{1,0:T(8,128)(2,1)S(1)}, u32[]{:S(2)}, u32[]{:S(2)}) %collective-permute-start.5) | collective-permute-done | bytes 491552 | tf_op jit(solution)/shard_map/ppermute | solution.py:714
  64.9 5.5 %partial_1.1 = (bf16[1,2,2,320,768]{4,3,2,1,0:T(8,128)(2,1)}, bf16[1,320,1536]{2,1,0:T(8,128)(2,1)}) custom-call(s32[2]{0:T(128)S(1)} %pad_add_fusion.ids, bf16[640,768]{1,0:T(8,128)(2,1)S(1)} %bitcast.35, bf16[320,768]{1,0:T(8,128)(2,1)S(1)} %collective-permute-done.4.other_low, bf16[320,768]{1,0:T(8,128)(2,1)S(1)} %collective-permute-done.5.other_high, ...), custom_call_target="tpu_custom_call" | custom-call | flops 27682406 | bytes 96337 | tf_op jit(solution)/shard_map/partial_1/pallas_call | solution.py:251
  73.7 6.1 %output_0.1 = (bf16[1,320,1536]{2,1,0:T(8,128)(2,1)}, bf16[1,320,768]{2,1,0:T(8,128)(2,1)S(1)}, bf16[1,320,768]{2,1,0:T(8,128)(2,1)S(1)}, bf16[1,320,768]{2,1,0:T(8,128)(2,1)S(1)}, bf16[1,320,768]{2,1,0:T(8,128)(2,1)S(1)}) custom-call(s32[2]{0:T(128)S(1)} %pad_add_fusion.ids, bf16[1,320,1536]{2,1,0:T(8,128)(2,1)} %get-tuple-element.57.mine, ...), custom_call_target="tpu_custom_call" | custom-call | flops 45298483200 | bytes 289013760 | tf_op jit(solution)/shard_map/output_0/pallas_call | solution.py:329
  84.2 2.4 %pack_0.1 = bf16[640,768]{1,0:T(8,128)(2,1)} custom-call(bf16[1,320,768]{2,1,0:T(8,128)(2,1)S(1)} %get-tuple-element.63.own_out, bf16[1,320,768]{2,1,0:T(8,128)(2,1)S(1)} %get-tuple-element.64.own_grad, bf16[1,320,768]{2,1,0:T(8,128)(2,1)S(1)} %collective-permute-done.8.other_out, bf16[1,320,768]{2,1,0:T(8,128)(2,1)S(1)} %collective-permute-done.9.other_grad), custom_call_target="tpu_custom_call" | custom-call | flops 6291456 | bytes 29491 | tf_op jit(solution)/shard_map/pack_0/pallas_call | solution.py:381
  86.5 5.0 %all-to-all-start.2 = ((bf16[16,40,768]{2,1,0:T(8,128)(2,1)}), bf16[16,40,768]{2,1,0:T(8,128)(2,1)S(1)}, u32[]{:S(2)}, u32[]{:S(2)}) async-start(bf16[16,40,768]{2,1,0:T(8,128)(2,1)} %bitcast.44), calls=%async_computation.2 | async-start | bytes 1966080 | tf_op jit(solution)/shard_map/all_to_all | solution.py:743
  91.5 3.2 %collective-permute-done.6.theirs = bf16[1,320,1536]{2,1,0:T(8,128)(2,1)S(1)} collective-permute-done((bf16[1,320,1536]{2,1,0:T(8,128)(2,1)}, bf16[1,320,1536]{2,1,0:T(8,128)(2,1)S(1)}, u32[]{:S(2)}, u32[]{:S(2)}) %collective-permute-start.6) | collective-permute-done | bytes 983072 | tf_op jit(solution)/shard_map/ppermute | solution.py:719
  94.7 5.8 %output_1.1 = (bf16[1,320,1536]{2,1,0:T(8,128)(2,1)}, bf16[1,320,768]{2,1,0:T(8,128)(2,1)S(1)}, bf16[1,320,768]{2,1,0:T(8,128)(2,1)S(1)}, bf16[1,320,768]{2,1,0:T(8,128)(2,1)S(1)}, bf16[1,320,768]{2,1,0:T(8,128)(2,1)S(1)}) custom-call(s32[2]{0:T(128)S(1)} %pad_add_fusion.ids, bf16[1,320,1536]{2,1,0:T(8,128)(2,1)} %get-tuple-element.59.mine, ...), custom_call_target="tpu_custom_call" | custom-call | flops 45298483200 | bytes 289013760 | tf_op jit(solution)/shard_map/output_1/pallas_call | solution.py:329
  104.2 5.8 %near_weight_grads.1.refs_4_ = bf16[3,3072,512]{2,1,0:T(8,128)(2,1)} custom-call(s32[2]{0:T(128)S(1)} %pad_add_fusion.ids, bf16[1,320,1536]{2,1,0:T(8,128)(2,1)S(1)} %copy-done.4, bf16[1,320,1536]{2,1,0:T(8,128)(2,1)S(1)} %copy-done.6, bf16[1,2,2,320,768]{4,3,2,1,0:T(8,128)(2,1)S(1)} %copy-done.2, bf16[1,2,2,320,768]{4,3,2,1,0:T(8,128)(2,1)S(1)} %copy-done.3), custom_call_target="tpu_custom_call" | custom-call | flops 15099494 | bytes 66846 | tf_op jit(solution)/shard_map/near_weight_grads/pallas_call | solution.py:631
  115.2 5.2 %all-to-all-start.3 = ((bf16[16,40,768]{2,1,0:T(8,128)(2,1)}), bf16[16,40,768]{2,1,0:T(8,128)(2,1)}, u32[]{:S(2)}, u32[]{:S(2)}) async-start(bf16[16,40,768]{2,1,0:T(8,128)(2,1)} %bitcast.45), calls=%async_computation.3 | async-start | bytes 1966080 | tf_op jit(solution)/shard_map/all_to_all | solution.py:743
  124.7 9.9 %collective-permute-done.12.refs_2_ = bf16[2,320,768]{2,1,0:T(8,128)(2,1)} collective-permute-done((bf16[2,320,768]{2,1,0:T(8,128)(2,1)}, bf16[2,320,768]{2,1,0:T(8,128)(2,1)}, u32[]{:S(2)}, u32[]{:S(2)}) %collective-permute-start.12) | collective-permute-done | bytes 983072 | tf_op jit(solution)/shard_map/ppermute | solution.py:719
  136.2 2.4 %collective-permute-done.13.refs_3_ = bf16[2,320,768]{2,1,0:T(8,128)(2,1)S(1)} collective-permute-done((bf16[2,320,768]{2,1,0:T(8,128)(2,1)}, bf16[2,320,768]{2,1,0:T(8,128)(2,1)S(1)}, u32[]{:S(2)}, u32[]{:S(2)}) %collective-permute-start.13) | collective-permute-done | bytes 983072 | tf_op jit(solution)/shard_map/ppermute | solution.py:714
  138.6 6.4 %far_weight_grads.1 = bf16[3,3072,512]{2,1,0:T(8,128)(2,1)} custom-call(s32[2]{0:T(128)S(1)} %pad_add_fusion.ids, bf16[1,320,1536]{2,1,0:T(8,128)(2,1)S(1)} %copy-done.5, bf16[1,320,1536]{2,1,0:T(8,128)(2,1)S(1)} %copy-done.7, bf16[2,320,768]{2,1,0:T(8,128)(2,1)} %collective-permute-done.12.refs_2_, ...), custom_call_target="tpu_custom_call", output_to_operand_aliasing={{}: (5, {})} | custom-call | flops 15099494 | bytes 66846 | tf_op jit(solution)/shard_map/far_weight_grads/pallas_call | solution.py:681
  146.2 4.2 %combine.1 = (bf16[2,2,128,768]{3,2,1,0:T(8,128)(2,1)}, f32[128,128]{1,0:T(8,128)S(1)}, bf16[128,3072]{1,0:T(8,128)(2,1)}, bf16[128,3072]{1,0:T(8,128)(2,1)}) custom-call(s32[2]{0:T(128)S(1)} %pad_add_fusion.ids, f32[128,2]{1,0:T(8,128)S(1)} %get-tuple-element.53.gates, bf16[128,3072]{1,0:T(8,128)(2,1)S(1)} %copy-done, bf16[2,384,640]{2,1,0:T(8,128)(2,1)S(1)} %copy-done.10, ...), custom_call_target="tpu_custom_call" | custom-call | flops 7549747 | bytes 19660 | tf_op jit(solution)/shard_map/combine/pallas_call | solution.py:511
  (81 shorter events, 35.7 us)
Async XLA Ops:
  4.4 29.3 %all-to-all-start.1 = ((bf16[16,40,768]{2,1,0:T(8,128)(2,1)}), bf16[16,40,768]{2,1,0:T(8,128)(2,1)S(1)}, u32[]{:S(2)}, u32[]{:S(2)}) async-start(bf16[16,40,768]{2,1,0:T(8,128)(2,1)} %bitcast.43), calls=%async_computation.1 | async-start | bytes 1966080 | tf_op jit(solution)/shard_map/all_to_all | solution.py:743
  11.2 13.8 %collective-permute-start.1 = (bf16[2,128,768]{2,1,0:T(8,128)(2,1)S(1)}, bf16[2,128,768]{2,1,0:T(8,128)(2,1)S(1)}, u32[]{:S(2)}, u32[]{:S(2)}) collective-permute-start(bf16[2,128,768]{2,1,0:T(8,128)(2,1)S(1)} %pad_maximum_fusion.1), channel_id=1, source_target_pairs={{0,1},{1,0},{2,3},{3,2},{4,5},{5,4},{6,7},{7,6},{8,9},{9,8},{10,11... | collective-permute-start | bytes 1179656 | tf_op jit(solution)/shard_map/ppermute | solution.py:719
  12.5 12.5 %copy-start.17 = (f32[4,128]{1,0:T(4,128)}, f32[4,128]{1,0:T(4,128)S(1)}, u32[]{:S(2)}) copy-start(f32[4,128]{1,0:T(4,128)S(1)} %pad_maximum_fusion.2.refs_0_) | copy-start | bytes 6148
  12.5 12.5 %collective-permute-start = (f32[4,128]{1,0:T(4,128)S(1)}, f32[4,128]{1,0:T(4,128)S(1)}, u32[]{:S(2)}, u32[]{:S(2)}) collective-permute-start(f32[4,128]{1,0:T(4,128)S(1)} %pad_maximum_fusion.2.refs_0_), channel_id=1, source_target_pairs={{0,1},{1,0},{2,3},{3,2},{4,5},{5,4},{6,7},{7,6},{8,9},{9,8},{10,11... | collective-permute-start | bytes 6152 | tf_op jit(solution)/shard_map/ppermute | solution.py:719
  33.7 25.4 %all-to-all-start = ((bf16[8,80,768]{2,1,0:T(8,128)(2,1)}), bf16[8,80,768]{2,1,0:T(8,128)(2,1)S(1)}, u32[]{:S(2)}, u32[]{:S(2)}) async-start(bf16[8,80,768]{2,1,0:T(8,128)(2,1)} %bitcast.42), calls=%async_computation | async-start | bytes 1966080 | tf_op jit(solution)/shard_map/all_to_all | solution.py:765
  39.1 5.1 %collective-permute-start.2 = (bf16[320,768]{1,0:T(8,128)(2,1)S(1)}, bf16[320,768]{1,0:T(8,128)(2,1)S(1)}, u32[]{:S(2)}, u32[]{:S(2)}) collective-permute-start(bf16[320,768]{1,0:T(8,128)(2,1)S(1)} %bitcast.47), channel_id=1, source_target_pairs={{0,16},{16,0},{1,17},{17,1},{2,18},{18,2},{3,19},{19,3},{4,20},{20... | collective-permute-start | bytes 1474568 | tf_op jit(solution)/shard_map/ppermute | solution.py:714
  42.7 2.2 %collective-permute-start.3 = (bf16[320,768]{1,0:T(8,128)(2,1)S(1)}, bf16[320,768]{1,0:T(8,128)(2,1)S(1)}, u32[]{:S(2)}, u32[]{:S(2)}) collective-permute-start(bf16[320,768]{1,0:T(8,128)(2,1)S(1)} %bitcast.46), channel_id=1, source_target_pairs={{0,16},{16,0},{1,17},{17,1},{2,18},{18,2},{3,19},{19,3},{4,20},{20... | collective-permute-start | bytes 1474568 | tf_op jit(solution)/shard_map/ppermute | solution.py:714
  50.4 23.3 %collective-permute-start.7 = (bf16[1,320,1536]{2,1,0:T(8,128)(2,1)}, bf16[1,320,1536]{2,1,0:T(8,128)(2,1)}, u32[]{:S(2)}, u32[]{:S(2)}) collective-permute-start(bf16[1,320,1536]{2,1,0:T(8,128)(2,1)} %get-tuple-element.57.mine), channel_id=1, source_target_pairs={{0,1},{1,0},{2,3},{3,2},{4,5},{5,4},{6,7},{7,6},{8,9},{9,8},{10,11... | collective-permute-start | bytes 2949128 | tf_op jit(solution)/shard_map/ppermute | solution.py:719
  59.9 5.0 %collective-permute-start.5 = (bf16[320,768]{1,0:T(8,128)(2,1)}, bf16[320,768]{1,0:T(8,128)(2,1)S(1)}, u32[]{:S(2)}, u32[]{:S(2)}) collective-permute-start(bf16[320,768]{1,0:T(8,128)(2,1)} %get-tuple-element.96), channel_id=1, source_target_pairs={{0,16},{16,0},{1,17},{17,1},{2,18},{18,2},{3,19},{19,3},{4,20},{20... | collective-permute-start | bytes 1474568 | tf_op jit(solution)/shard_map/ppermute | solution.py:714
  62.5 2.4 %collective-permute-start.4 = (bf16[320,768]{1,0:T(8,128)(2,1)S(1)}, bf16[320,768]{1,0:T(8,128)(2,1)S(1)}, u32[]{:S(2)}, u32[]{:S(2)}) collective-permute-start(bf16[320,768]{1,0:T(8,128)(2,1)S(1)} %get-tuple-element.97), channel_id=1, source_target_pairs={{0,16},{16,0},{1,17},{17,1},{2,18},{18,2},{3,19},{19,3},{4,20},{20... | collective-permute-start | bytes 1474568 | tf_op jit(solution)/shard_map/ppermute | solution.py:714
  70.4 24.3 %collective-permute-start.6 = (bf16[1,320,1536]{2,1,0:T(8,128)(2,1)}, bf16[1,320,1536]{2,1,0:T(8,128)(2,1)S(1)}, u32[]{:S(2)}, u32[]{:S(2)}) collective-permute-start(bf16[1,320,1536]{2,1,0:T(8,128)(2,1)} %get-tuple-element.59.mine), channel_id=1, source_target_pairs={{0,1},{1,0},{2,3},{3,2},{4,5},{5,4},{6,7},{7,6},{8,9},{9,8},{10,11... | collective-permute-start | bytes 2949128 | tf_op jit(solution)/shard_map/ppermute | solution.py:719
  79.9 3.6 %collective-permute-start.8 = (bf16[1,320,768]{2,1,0:T(8,128)(2,1)S(1)}, bf16[1,320,768]{2,1,0:T(8,128)(2,1)S(1)}, u32[]{:S(2)}, u32[]{:S(2)}) collective-permute-start(bf16[1,320,768]{2,1,0:T(8,128)(2,1)S(1)} %get-tuple-element.65), channel_id=1, source_target_pairs={{0,16},{16,0},{1,17},{17,1},{2,18},{18,2},{3,19},{19,3},{4,20},{20... | collective-permute-start | bytes 1474568 | tf_op jit(solution)/shard_map/ppermute | solution.py:714
  82.0 2.2 %collective-permute-start.9 = (bf16[1,320,768]{2,1,0:T(8,128)(2,1)S(1)}, bf16[1,320,768]{2,1,0:T(8,128)(2,1)S(1)}, u32[]{:S(2)}, u32[]{:S(2)}) collective-permute-start(bf16[1,320,768]{2,1,0:T(8,128)(2,1)S(1)} %get-tuple-element.66), channel_id=1, source_target_pairs={{0,16},{16,0},{1,17},{17,1},{2,18},{18,2},{3,19},{19,3},{4,20},{20... | collective-permute-start | bytes 1474568 | tf_op jit(solution)/shard_map/ppermute | solution.py:714
  86.5 27.7 %all-to-all-start.2 = ((bf16[16,40,768]{2,1,0:T(8,128)(2,1)}), bf16[16,40,768]{2,1,0:T(8,128)(2,1)S(1)}, u32[]{:S(2)}, u32[]{:S(2)}) async-start(bf16[16,40,768]{2,1,0:T(8,128)(2,1)} %bitcast.44), calls=%async_computation.2 | async-start | bytes 1966080 | tf_op jit(solution)/shard_map/all_to_all | solution.py:743
  91.5 11.5 %copy-start.2 = (bf16[1,2,2,320,768]{4,3,2,1,0:T(8,128)(2,1)S(1)}, bf16[1,2,2,320,768]{4,3,2,1,0:T(8,128)(2,1)}, u32[]{:S(2)}) copy-start(bf16[1,2,2,320,768]{4,3,2,1,0:T(8,128)(2,1)} %get-tuple-element.61.refs_2_) | copy-start | bytes 5898244
  100.5 9.5 %collective-permute-start.10 = (bf16[1,320,768]{2,1,0:T(8,128)(2,1)S(1)}, bf16[1,320,768]{2,1,0:T(8,128)(2,1)S(1)}, u32[]{:S(2)}, u32[]{:S(2)}) collective-permute-start(bf16[1,320,768]{2,1,0:T(8,128)(2,1)S(1)} %get-tuple-element.70), channel_id=1, source_target_pairs={{0,16},{16,0},{1,17},{17,1},{2,18},{18,2},{3,19},{19,3},{4,20},{20... | collective-permute-start | bytes 1474568 | tf_op jit(solution)/shard_map/ppermute | solution.py:714
  102.6 7.4 %collective-permute-start.11 = (bf16[1,320,768]{2,1,0:T(8,128)(2,1)S(1)}, bf16[1,320,768]{2,1,0:T(8,128)(2,1)S(1)}, u32[]{:S(2)}, u32[]{:S(2)}) collective-permute-start(bf16[1,320,768]{2,1,0:T(8,128)(2,1)S(1)} %get-tuple-element.71), channel_id=1, source_target_pairs={{0,16},{16,0},{1,17},{17,1},{2,18},{18,2},{3,19},{19,3},{4,20},{20... | collective-permute-start | bytes 1474568 | tf_op jit(solution)/shard_map/ppermute | solution.py:714
  102.7 31.9 %collective-permute-start.12 = (bf16[2,320,768]{2,1,0:T(8,128)(2,1)}, bf16[2,320,768]{2,1,0:T(8,128)(2,1)}, u32[]{:S(2)}, u32[]{:S(2)}) collective-permute-start(bf16[2,320,768]{2,1,0:T(8,128)(2,1)} %select_bitcast_fusion), channel_id=1, source_target_pairs={{0,1},{1,0},{2,3},{3,2},{4,5},{5,4},{6,7},{7,6},{8,9},{9,8},{10,11... | collective-permute-start | bytes 2949128 | tf_op jit(solution)/shard_map/ppermute | solution.py:719
  115.2 29.8 %all-to-all-start.3 = ((bf16[16,40,768]{2,1,0:T(8,128)(2,1)}), bf16[16,40,768]{2,1,0:T(8,128)(2,1)}, u32[]{:S(2)}, u32[]{:S(2)}) async-start(bf16[16,40,768]{2,1,0:T(8,128)(2,1)} %bitcast.45), calls=%async_computation.3 | async-start | bytes 1966080 | tf_op jit(solution)/shard_map/all_to_all | solution.py:743
  122.8 15.7 %copy-start.5 = (bf16[1,320,1536]{2,1,0:T(8,128)(2,1)S(1)}, bf16[1,320,1536]{2,1,0:T(8,128)(2,1)}, u32[]{:S(2)}) copy-start(bf16[1,320,1536]{2,1,0:T(8,128)(2,1)} %get-tuple-element.72.refs_0_) | copy-start | bytes 2949124
  122.8 15.7 %copy-start.7 = (bf16[1,320,1536]{2,1,0:T(8,128)(2,1)S(1)}, bf16[1,320,1536]{2,1,0:T(8,128)(2,1)}, u32[]{:S(2)}) copy-start(bf16[1,320,1536]{2,1,0:T(8,128)(2,1)} %get-tuple-element.73.refs_1_) | copy-start | bytes 2949124
  134.6 4.0 %collective-permute-start.13 = (bf16[2,320,768]{2,1,0:T(8,128)(2,1)}, bf16[2,320,768]{2,1,0:T(8,128)(2,1)S(1)}, u32[]{:S(2)}, u32[]{:S(2)}) collective-permute-start(bf16[2,320,768]{2,1,0:T(8,128)(2,1)} %collective-permute-done.12.refs_2_), channel_id=1, source_target_pairs={{0,16},{16,0},{1,17},{17,1},{2,18},{18,2},{3,19},{19,3},{4,20},{20... | collective-permute-start | bytes 2949128 | tf_op jit(solution)/shard_map/ppermute | solution.py:714
  150.4 3.0 %collective-permute-start.14 = (bf16[2,2,128,768]{3,2,1,0:T(8,128)(2,1)}, bf16[2,2,128,768]{3,2,1,0:T(8,128)(2,1)S(1)}, u32[]{:S(2)}, u32[]{:S(2)}) collective-permute-start(bf16[2,2,128,768]{3,2,1,0:T(8,128)(2,1)} %get-tuple-element.85), channel_id=1, source_target_pairs={{0,16},{16,0},{1,17},{17,1},{2,18},{18,2},{3,19},{19,3},{4,20},{20... | collective-permute-start | bytes 2359304 | tf_op jit(solution)/shard_map/ppermute | solution.py:714
  150.8 2.0 %collective-permute-start.15 = (f32[128,128]{1,0:T(8,128)S(1)}, f32[128,128]{1,0:T(8,128)S(1)}, u32[]{:S(2)}, u32[]{:S(2)}) collective-permute-start(f32[128,128]{1,0:T(8,128)S(1)} %get-tuple-element.90), channel_id=1, source_target_pairs={{0,16},{16,0},{1,17},{17,1},{2,18},{18,2},{3,19},{19,3},{4,20},{20... | collective-permute-start | bytes 196616 | tf_op jit(solution)/shard_map/ppermute | solution.py:714
  (15 other events, 85.1 us)

commit v3 on v2

--- a/solution.py
+++ b/solution.py
@@ -25,7 +25,7 @@
     return pltpu.CompilerParams(vmem_limit_bytes=mib * MIB)
 
 
-WEIGHTS = {"output_0": 30, "output_1": 30}
+WEIGHTS = {"output_0": 30, "output_1": 30, "far_weight_grads": 4}
 
 
 def cost(macs, moved, name=""):
@@ -271,6 +271,7 @@
         cost_estimate=cost(
             per_chunk * rows * (3 * depth * units + 4 * subs * block * width),
             2 * per_chunk * (3 * depth * units + 8 * rows * width + 3 * rows * units),
+            f"partial_{chunk}",
         ),
         name=f"partial_{chunk}",
     )(*operands)
@@ -540,9 +541,18 @@
     )(ids, gates, cotangent, chooser, returned, earlier)
 
 
-def merge_kernel(ids, other, started_out, started_grad, layer_out, input_grad):
-    layer_out[...] = other[0]
-    input_grad[...] = other[1]
+def merge_kernel(ids, other, started_out, started_grad, layer_out, input_grad, moved):
+    width = other.shape[3]
+    copies = []
+    for p in range(other.shape[1]):
+        columns = pl.ds(pl.multiple_of((2 * p + 1 - ids[0]) * width, 128), width)
+        for i, target in enumerate((layer_out, input_grad)):
+            copies.append(
+                pltpu.make_async_copy(other.at[i, p], target.at[:, columns], moved.at[p, i])
+            )
+            copies[-1].start()
+    for copy in copies:
+        copy.wait()
 
 
 def merge(ids, own, other, direct):
@@ -553,17 +563,17 @@
         pair = jnp.stack([jnp.where(q == 0, own, other), jnp.where(q == 0, other, own)], axis=2)
         pair = pair.transpose(0, 3, 1, 2, 4).reshape(2, token_count, model_width)
         return pair[0], pair[1]
-    in_spec = pl.BlockSpec((2, None, token_count, width), lambda p, ids: (0, p, 0, 0))
-    out_spec = pl.BlockSpec((token_count, width), lambda p, ids: (0, 2 * p + 1 - ids[0]))
     shape = jax.ShapeDtypeStruct((token_count, model_width), BF16)
+    free = pl.BlockSpec(memory_space=pl.ANY)
     return pl.pallas_call(
         merge_kernel,
         out_shape=(shape, shape),
         grid_spec=pltpu.PrefetchScalarGridSpec(
             num_scalar_prefetch=1,
-            grid=(groups,),
-            in_specs=[in_spec] + [pl.BlockSpec(memory_space=pl.ANY)] * 2,
-            out_specs=(out_spec, out_spec),
+            grid=(1,),
+            in_specs=[free] * 3,
+            out_specs=(free, free),
+            scratch_shapes=[pltpu.SemaphoreType.DMA((groups, 2))],
         ),
         input_output_aliases={2: 0, 3: 1},
         compiler_params=params(),
@@ -693,7 +703,8 @@
         input_output_aliases={1 + CHUNKS + count: 0},
         compiler_params=params(),
         cost_estimate=cost(
-            3 * rows * count * width * units, 6 * count * width * units + 4 * count * rows * width
+            3 * rows * count * width * units, 6 * count * width * units + 4 * count * rows * width,
+            "far_weight_grads",
         ),
         name="far_weight_grads",
     )(ids, *acts, *operands, grads)
@@ -762,6 +773,8 @@
     for c in range(1, CHUNKS):
         sent = group_dispatch(dims, c, infos, parts)
         sent, gates, *choosers = together(sent, gates, *choosers)
+        if c == 1:
+            arrived[0], _ = together(arrived[0], sent)
         moved = lax.all_to_all(
             sent.reshape(subs // groups, groups * block, width),
             "expert",
@@ -795,8 +808,8 @@
         if c + 1 < CHUNKS:
             theirs[c + 1], _ = together(theirs[c + 1], packed)
         if c > 0:
+            packed, returned[c - 1] = together(packed, returned[c - 1])
             weight_grad = near_weight_grads(ids, acts, features)
-            packed, returned[c - 1], weight_grad = together(packed, returned[c - 1], weight_grad)
         returned.append(exchange(packed))
     theirs[-1], *leaving = together(theirs[-1], *leaving)
     earlier = gather_rows(ids, choosers[0], returned[0])

time: 158 us -> 156 us (0.987)
  waiting for transfers between devices: 47.5 us -> 44.5 us
    ppermute x5, waiting for transfers between devices: 22.1 us -> 12.4 us  [swap_holders(): lax.ppermute(value, 'expert', [(source, source ^ mask) for source in rang...]
    all_to_all x3, waiting for transfers between devices: 6.14 us -> 10.8 us  [exchange(): lax.all_to_all(blocks, 'expert', split_axis=0, concat_axis=0, tiled=True)]
    ppermute x11, waiting for transfers between devices: 10.9 us -> 13 us  [swap_cores(): return lax.ppermute(value, 'dp', [(0, 1), (1, 0)])]
    unnamed x41 -> x37, local copies, waits for them, and re-layouts: 8.08 us -> 7.38 us
  transfers between devices with their start and end apart: 20 -> 20, of which waited for: 14 -> 15; matrix products, arithmetic and copies ran while one was open for 3% -> 3% of each run, Pallas kernels for 31% -> 32%
where the time goes in v3:
time: 156 us; the launch traced here: 154 us
  Pallas kernels  58 us (37%)
  waiting for transfers between devices  44.5 us (29%)
  starting transfers between devices  38.6 us (25%)
  local copies, waits for them, and re-layouts  8.36 us (5%)
  other arithmetic  3.18 us (2%)
    all_to_all x3, starting transfers between devices, exchange(): lax.all_to_all(blocks, 'expert', split_axis=0, concat_axis=0, tiled=True)  16.9 us
    ppermute x11, starting transfers between devices, swap_cores(): return lax.ppermute(value, 'dp', [(0, 1), (1, 0)])  13.9 us
    ppermute x11, waiting for transfers between devices, swap_cores(): return lax.ppermute(value, 'dp', [(0, 1), (1, 0)])  13 us
    ppermute x5, waiting for transfers between devices, swap_holders(): lax.ppermute(value, 'expert', [(source, source ^ mask) for source in rang...  12.4 us
    pallas_call x2, Pallas kernels, output_products(): pl.pallas_call(functools.partial(output_kernel, dims, chunk), out_shape=(...  12 us
    pallas_call x2, Pallas kernels, partial_products(): pl.pallas_call(functools.partial(partial_kernel, dims, chunk), out_shape=...  11 us
    all_to_all x3, waiting for transfers between devices, exchange(): lax.all_to_all(blocks, 'expert', split_axis=0, concat_axis=0, tiled=True)  10.8 us
    all_to_all x1, waiting for transfers between devices, shards(): lax.all_to_all(sent.reshape(subs // groups, groups * block, width), 'expe...  8.27 us
  transfers between devices with their start and end apart: 20, of which 15 were waited for; matrix products, arithmetic and copies ran while one was open for 3% of the time, Pallas kernels for 32%

profile of v3, /device:TPU:17, one launch (start us, length us, event | category | flops | bytes accessed | tf_op | source)
XLA Modules:
  0.0 153.7 jit_solution(5289796279730258525)
XLA Ops:
  0.7 3.7 %dispatch_0.1 = bf16[8,2,40,768]{3,2,1,0:T(8,128)(2,1)} custom-call(s32[2,128]{1,0:T(2,128)} %bitcast.44, f32[2,128]{1,0:T(2,128)} %bitcast.45, bf16[128,3072]{1,0:T(8,128)(2,1)} %tokens.1, bf16[128,3072]{1,0:T(8,128)(2,1)} %cotangent.3), custom_call_target="tpu_custom_call" | custom-call | flops 2516582 | bytes 17694 | tf_op jit(solution)/shard_map/dispatch_0/pallas_call | solution.py:165
  4.4 6.7 %all-to-all-start.1 = ((bf16[16,40,768]{2,1,0:T(8,128)(2,1)}), bf16[16,40,768]{2,1,0:T(8,128)(2,1)S(1)}, u32[]{:S(2)}, u32[]{:S(2)}) async-start(bf16[16,40,768]{2,1,0:T(8,128)(2,1)} %bitcast.41), calls=%async_computation.1 | async-start | bytes 1966080 | tf_op jit(solution)/shard_map/all_to_all | solution.py:754
  13.9 2.8 %choosers.1 = (f32[128,2]{1,0:T(8,128)S(1)}, bf16[2,384,640]{2,1,0:T(8,128)(2,1)}, bf16[2,384,640]{2,1,0:T(8,128)(2,1)}) custom-call(s32[2]{0:T(128)S(1)} %pad_add_fusion.ids, s32[128,2]{1,0:T(8,128)S(1)} %copy.13.routes, f32[128,2]{1,0:T(8,128)S(1)} %copy.14.gates, s32[8,640]{1,0:T(8,128)S(1)} %copy-done.10), custom_call_target="tpu_custom_call" | custom-call | bytes 19660 | tf_op jit(solution)/shard_map/choosers/pallas_call | solution.py:438
  16.7 8.3 %collective-permute-done.refs_1_ = f32[4,128]{1,0:T(4,128)S(1)} collective-permute-done((f32[4,128]{1,0:T(4,128)S(1)}, f32[4,128]{1,0:T(4,128)S(1)}, u32[]{:S(2)}, u32[]{:S(2)}) %collective-permute-start) | collective-permute-done | bytes 2080 | tf_op jit(solution)/shard_map/ppermute | solution.py:730
  26.4 3.0 %group_dispatch_1.1 = bf16[8,2,40,768]{3,2,1,0:T(8,128)(2,1)} custom-call(f32[4,128]{1,0:T(4,128)} %copy-done.15, f32[4,128]{1,0:T(4,128)} %copy-done.16, bf16[2,128,768]{2,1,0:T(8,128)(2,1)} %pad_maximum_fusion.refs_2_, bf16[2,128,768]{2,1,0:T(8,128)(2,1)} %copy-done.12), custom_call_target="tpu_custom_call" | custom-call | flops 2516582 | bytes 17694 | tf_op jit(solution)/shard_map/group_dispatch_1/pallas_call | solution.py:132
  29.4 4.3 %all-to-all-done.1 = bf16[16,40,768]{2,1,0:T(8,128)(2,1)S(1)} async-done(((bf16[16,40,768]{2,1,0:T(8,128)(2,1)}), bf16[16,40,768]{2,1,0:T(8,128)(2,1)S(1)}, u32[]{:S(2)}, u32[]{:S(2)}) %all-to-all-start.1) | async-done | bytes 983072 | tf_op jit(solution)/shard_map/all_to_all | solution.py:754
  33.7 5.4 %all-to-all-start = ((bf16[8,80,768]{2,1,0:T(8,128)(2,1)}), bf16[8,80,768]{2,1,0:T(8,128)(2,1)S(1)}, u32[]{:S(2)}, u32[]{:S(2)}) async-start(bf16[8,80,768]{2,1,0:T(8,128)(2,1)} %bitcast.40), calls=%async_computation | async-start | bytes 1966080 | tf_op jit(solution)/shard_map/all_to_all | solution.py:778
  39.1 3.6 %collective-permute-start.3 = (bf16[320,768]{1,0:T(8,128)(2,1)S(1)}, bf16[320,768]{1,0:T(8,128)(2,1)S(1)}, u32[]{:S(2)}, u32[]{:S(2)}) collective-permute-start(bf16[320,768]{1,0:T(8,128)(2,1)S(1)} %get-tuple-element.98), channel_id=1, source_target_pairs={{0,16},{16,0},{1,17},{17,1},{2,18},{18,2},{3,19},{19,3},{4,20},{20... | collective-permute-start | bytes 1474568 | tf_op jit(solution)/shard_map/ppermute | solution.py:725
  44.9 5.5 %partial_0.1 = (bf16[1,2,2,320,768]{4,3,2,1,0:T(8,128)(2,1)}, bf16[1,320,1536]{2,1,0:T(8,128)(2,1)}) custom-call(s32[2]{0:T(128)S(1)} %pad_add_fusion.ids, bf16[640,768]{1,0:T(8,128)(2,1)S(1)} %bitcast.32, bf16[320,768]{1,0:T(8,128)(2,1)S(1)} %collective-permute-done.2.other_low, bf16[320,768]{1,0:T(8,128)(2,1)S(1)} %collective-permute-done.3.other_high, ...), custom_call_target="tpu_custom_call" | custom-call | flops 27682406 | bytes 96337 | tf_op jit(solution)/shard_map/partial_0/pallas_call | solution.py:251
  50.8 8.3 %all-to-all-done = bf16[8,80,768]{2,1,0:T(8,128)(2,1)S(1)} async-done(((bf16[8,80,768]{2,1,0:T(8,128)(2,1)}), bf16[8,80,768]{2,1,0:T(8,128)(2,1)S(1)}, u32[]{:S(2)}, u32[]{:S(2)}) %all-to-all-start) | async-done | bytes 983072 | tf_op jit(solution)/shard_map/all_to_all | solution.py:778
  59.9 2.6 %collective-permute-start.5 = (bf16[320,768]{1,0:T(8,128)(2,1)}, bf16[320,768]{1,0:T(8,128)(2,1)S(1)}, u32[]{:S(2)}, u32[]{:S(2)}) collective-permute-start(bf16[320,768]{1,0:T(8,128)(2,1)} %get-tuple-element.96), channel_id=1, source_target_pairs={{0,16},{16,0},{1,17},{17,1},{2,18},{18,2},{3,19},{19,3},{4,20},{20... | collective-permute-start | bytes 1474568 | tf_op jit(solution)/shard_map/ppermute | solution.py:725
  64.9 5.5 %partial_1.1 = (bf16[1,2,2,320,768]{4,3,2,1,0:T(8,128)(2,1)}, bf16[1,320,1536]{2,1,0:T(8,128)(2,1)}) custom-call(s32[2]{0:T(128)S(1)} %pad_add_fusion.ids, bf16[640,768]{1,0:T(8,128)(2,1)S(1)} %bitcast.34, bf16[320,768]{1,0:T(8,128)(2,1)S(1)} %collective-permute-done.4.other_low, bf16[320,768]{1,0:T(8,128)(2,1)S(1)} %collective-permute-done.5.other_high, ...), custom_call_target="tpu_custom_call" | custom-call | flops 27682406 | bytes 96337 | tf_op jit(solution)/shard_map/partial_1/pallas_call | solution.py:251
  73.8 6.1 %output_0.1 = (bf16[1,320,1536]{2,1,0:T(8,128)(2,1)}, bf16[1,320,768]{2,1,0:T(8,128)(2,1)S(1)}, bf16[1,320,768]{2,1,0:T(8,128)(2,1)S(1)}, bf16[1,320,768]{2,1,0:T(8,128)(2,1)S(1)}, bf16[1,320,768]{2,1,0:T(8,128)(2,1)S(1)}) custom-call(s32[2]{0:T(128)S(1)} %pad_add_fusion.ids, bf16[1,320,1536]{2,1,0:T(8,128)(2,1)} %get-tuple-element.58.mine, ...), custom_call_target="tpu_custom_call" | custom-call | flops 45298483200 | bytes 289013760 | tf_op jit(solution)/shard_map/output_0/pallas_call | solution.py:330
  86.5 5.0 %all-to-all-start.2 = ((bf16[16,40,768]{2,1,0:T(8,128)(2,1)}), bf16[16,40,768]{2,1,0:T(8,128)(2,1)}, u32[]{:S(2)}, u32[]{:S(2)}) async-start(bf16[16,40,768]{2,1,0:T(8,128)(2,1)} %bitcast.42), calls=%async_computation.2 | async-start | bytes 1966080 | tf_op jit(solution)/shard_map/all_to_all | solution.py:754
  91.5 3.4 %collective-permute-done.6.theirs = bf16[1,320,1536]{2,1,0:T(8,128)(2,1)S(1)} collective-permute-done((bf16[1,320,1536]{2,1,0:T(8,128)(2,1)}, bf16[1,320,1536]{2,1,0:T(8,128)(2,1)S(1)}, u32[]{:S(2)}, u32[]{:S(2)}) %collective-permute-start.6) | collective-permute-done | bytes 983072 | tf_op jit(solution)/shard_map/ppermute | solution.py:730
  95.0 5.8 %output_1.1 = (bf16[1,320,1536]{2,1,0:T(8,128)(2,1)}, bf16[1,320,768]{2,1,0:T(8,128)(2,1)S(1)}, bf16[1,320,768]{2,1,0:T(8,128)(2,1)S(1)}, bf16[1,320,768]{2,1,0:T(8,128)(2,1)S(1)}, bf16[1,320,768]{2,1,0:T(8,128)(2,1)S(1)}) custom-call(s32[2]{0:T(128)S(1)} %pad_add_fusion.ids, bf16[1,320,1536]{2,1,0:T(8,128)(2,1)} %get-tuple-element.60.mine, ...), custom_call_target="tpu_custom_call" | custom-call | flops 45298483200 | bytes 289013760 | tf_op jit(solution)/shard_map/output_1/pallas_call | solution.py:330
  107.8 6.5 %all-to-all-done.2 = bf16[16,40,768]{2,1,0:T(8,128)(2,1)} async-done(((bf16[16,40,768]{2,1,0:T(8,128)(2,1)}), bf16[16,40,768]{2,1,0:T(8,128)(2,1)}, u32[]{:S(2)}, u32[]{:S(2)}) %all-to-all-start.2) | async-done | bytes 983072 | tf_op jit(solution)/shard_map/all_to_all | solution.py:754
  114.2 5.2 %all-to-all-start.3 = ((bf16[16,40,768]{2,1,0:T(8,128)(2,1)}), bf16[16,40,768]{2,1,0:T(8,128)(2,1)}, u32[]{:S(2)}, u32[]{:S(2)}) async-start(bf16[16,40,768]{2,1,0:T(8,128)(2,1)} %bitcast.43), calls=%async_computation.3 | async-start | bytes 1966080 | tf_op jit(solution)/shard_map/all_to_all | solution.py:754
  123.4 5.8 %near_weight_grads.1.refs_4_ = bf16[3,3072,512]{2,1,0:T(8,128)(2,1)} custom-call(s32[2]{0:T(128)S(1)} %pad_add_fusion.ids, bf16[1,320,1536]{2,1,0:T(8,128)(2,1)S(1)} %copy-done.4, bf16[1,320,1536]{2,1,0:T(8,128)(2,1)S(1)} %copy-done.6, bf16[1,2,2,320,768]{4,3,2,1,0:T(8,128)(2,1)S(1)} %copy-done.2, bf16[1,2,2,320,768]{4,3,2,1,0:T(8,128)(2,1)S(1)} %copy-done.3), custom_call_target="tpu_custom_call" | custom-call | flops 15099494 | bytes 66846 | tf_op jit(solution)/shard_map/near_weight_grads/pallas_call | solution.py:641
  129.2 3.1 %gather_rows.1.earlier = f32[2,384,768]{2,1,0:T(8,128)S(1)} custom-call(s32[2]{0:T(128)S(1)} %pad_add_fusion.ids, bf16[2,384,640]{2,1,0:T(8,128)(2,1)S(1)} %copy-done.9, bf16[640,768]{1,0:T(8,128)(2,1)} %bitcast.17.returned), custom_call_target="tpu_custom_call" | custom-call | flops 7549747 | bytes 23592 | tf_op jit(solution)/shard_map/gather_rows/pallas_call | solution.py:460
  132.3 2.4 %collective-permute-start.13 = (bf16[2,320,768]{2,1,0:T(8,128)(2,1)}, bf16[2,320,768]{2,1,0:T(8,128)(2,1)S(1)}, u32[]{:S(2)}, u32[]{:S(2)}) collective-permute-start(bf16[2,320,768]{2,1,0:T(8,128)(2,1)} %collective-permute-done.12.refs_2_), channel_id=1, source_target_pairs={{0,16},{16,0},{1,17},{17,1},{2,18},{18,2},{3,19},{19,3},{4,20},{20... | collective-permute-start | bytes 2949128 | tf_op jit(solution)/shard_map/ppermute | solution.py:725
  134.8 2.4 %collective-permute-done.13.refs_3_ = bf16[2,320,768]{2,1,0:T(8,128)(2,1)S(1)} collective-permute-done((bf16[2,320,768]{2,1,0:T(8,128)(2,1)}, bf16[2,320,768]{2,1,0:T(8,128)(2,1)S(1)}, u32[]{:S(2)}, u32[]{:S(2)}) %collective-permute-start.13) | collective-permute-done | bytes 983072 | tf_op jit(solution)/shard_map/ppermute | solution.py:725
  137.2 6.4 %far_weight_grads.1 = bf16[3,3072,512]{2,1,0:T(8,128)(2,1)} custom-call(s32[2]{0:T(128)S(1)} %pad_add_fusion.ids, bf16[1,320,1536]{2,1,0:T(8,128)(2,1)S(1)} %copy-done.5, bf16[1,320,1536]{2,1,0:T(8,128)(2,1)S(1)} %copy-done.7, bf16[2,320,768]{2,1,0:T(8,128)(2,1)} %collective-permute-done.12.refs_2_, ...), custom_call_target="tpu_custom_call", output_to_operand_aliasing={{}: (5, {})} | custom-call | flops 6039797760 | bytes 26738688 | tf_op jit(solution)/shard_map/far_weight_grads/pallas_call | solution.py:691
  144.8 4.2 %combine.1 = (bf16[2,2,128,768]{3,2,1,0:T(8,128)(2,1)}, f32[128,128]{1,0:T(8,128)S(1)}, bf16[128,3072]{1,0:T(8,128)(2,1)}, bf16[128,3072]{1,0:T(8,128)(2,1)}) custom-call(s32[2]{0:T(128)S(1)} %pad_add_fusion.ids, f32[128,2]{1,0:T(8,128)S(1)} %get-tuple-element.53.gates, bf16[128,3072]{1,0:T(8,128)(2,1)S(1)} %copy-done, bf16[2,384,640]{2,1,0:T(8,128)(2,1)S(1)} %copy-done.8, ...), custom_call_target="tpu_custom_call" | custom-call | flops 7549747 | bytes 19660 | tf_op jit(solution)/shard_map/combine/pallas_call | solution.py:512
  (77 shorter events, 36.6 us)
Async XLA Ops:
  0.6 10.5 %copy-start = (bf16[128,3072]{1,0:T(8,128)(2,1)S(1)}, bf16[128,3072]{1,0:T(8,128)(2,1)}, u32[]{:S(2)}) copy-start(bf16[128,3072]{1,0:T(8,128)(2,1)} %cotangent.3) | copy-start | bytes 2359300
  0.6 10.4 %copy-start.11 = (bf16[128,3072]{1,0:T(8,128)(2,1)S(1)}, bf16[128,3072]{1,0:T(8,128)(2,1)}, u32[]{:S(2)}) copy-start(bf16[128,3072]{1,0:T(8,128)(2,1)} %tokens.1) | copy-start | bytes 2359300
  4.4 29.3 %all-to-all-start.1 = ((bf16[16,40,768]{2,1,0:T(8,128)(2,1)}), bf16[16,40,768]{2,1,0:T(8,128)(2,1)S(1)}, u32[]{:S(2)}, u32[]{:S(2)}) async-start(bf16[16,40,768]{2,1,0:T(8,128)(2,1)} %bitcast.41), calls=%async_computation.1 | async-start | bytes 1966080 | tf_op jit(solution)/shard_map/all_to_all | solution.py:754
  11.2 13.8 %collective-permute-start.1 = (bf16[2,128,768]{2,1,0:T(8,128)(2,1)S(1)}, bf16[2,128,768]{2,1,0:T(8,128)(2,1)S(1)}, u32[]{:S(2)}, u32[]{:S(2)}) collective-permute-start(bf16[2,128,768]{2,1,0:T(8,128)(2,1)S(1)} %pad_maximum_fusion.1), channel_id=1, source_target_pairs={{0,1},{1,0},{2,3},{3,2},{4,5},{5,4},{6,7},{7,6},{8,9},{9,8},{10,11... | collective-permute-start | bytes 1179656 | tf_op jit(solution)/shard_map/ppermute | solution.py:730
  12.5 12.5 %copy-start.15 = (f32[4,128]{1,0:T(4,128)}, f32[4,128]{1,0:T(4,128)S(1)}, u32[]{:S(2)}) copy-start(f32[4,128]{1,0:T(4,128)S(1)} %pad_maximum_fusion.2.refs_0_) | copy-start | bytes 6148
  12.5 12.5 %collective-permute-start = (f32[4,128]{1,0:T(4,128)S(1)}, f32[4,128]{1,0:T(4,128)S(1)}, u32[]{:S(2)}, u32[]{:S(2)}) collective-permute-start(f32[4,128]{1,0:T(4,128)S(1)} %pad_maximum_fusion.2.refs_0_), channel_id=1, source_target_pairs={{0,1},{1,0},{2,3},{3,2},{4,5},{5,4},{6,7},{7,6},{8,9},{9,8},{10,11... | collective-permute-start | bytes 6152 | tf_op jit(solution)/shard_map/ppermute | solution.py:730
  33.7 25.4 %all-to-all-start = ((bf16[8,80,768]{2,1,0:T(8,128)(2,1)}), bf16[8,80,768]{2,1,0:T(8,128)(2,1)S(1)}, u32[]{:S(2)}, u32[]{:S(2)}) async-start(bf16[8,80,768]{2,1,0:T(8,128)(2,1)} %bitcast.40), calls=%async_computation | async-start | bytes 1966080 | tf_op jit(solution)/shard_map/all_to_all | solution.py:778
  39.1 5.1 %collective-permute-start.3 = (bf16[320,768]{1,0:T(8,128)(2,1)S(1)}, bf16[320,768]{1,0:T(8,128)(2,1)S(1)}, u32[]{:S(2)}, u32[]{:S(2)}) collective-permute-start(bf16[320,768]{1,0:T(8,128)(2,1)S(1)} %get-tuple-element.98), channel_id=1, source_target_pairs={{0,16},{16,0},{1,17},{17,1},{2,18},{18,2},{3,19},{19,3},{4,20},{20... | collective-permute-start | bytes 1474568 | tf_op jit(solution)/shard_map/ppermute | solution.py:725
  42.7 2.2 %collective-permute-start.2 = (bf16[320,768]{1,0:T(8,128)(2,1)S(1)}, bf16[320,768]{1,0:T(8,128)(2,1)S(1)}, u32[]{:S(2)}, u32[]{:S(2)}) collective-permute-start(bf16[320,768]{1,0:T(8,128)(2,1)S(1)} %get-tuple-element.99), channel_id=1, source_target_pairs={{0,16},{16,0},{1,17},{17,1},{2,18},{18,2},{3,19},{19,3},{4,20},{20... | collective-permute-start | bytes 1474568 | tf_op jit(solution)/shard_map/ppermute | solution.py:725
  50.4 23.3 %collective-permute-start.7 = (bf16[1,320,1536]{2,1,0:T(8,128)(2,1)}, bf16[1,320,1536]{2,1,0:T(8,128)(2,1)}, u32[]{:S(2)}, u32[]{:S(2)}) collective-permute-start(bf16[1,320,1536]{2,1,0:T(8,128)(2,1)} %get-tuple-element.58.mine), channel_id=1, source_target_pairs={{0,1},{1,0},{2,3},{3,2},{4,5},{5,4},{6,7},{7,6},{8,9},{9,8},{10,11... | collective-permute-start | bytes 2949128 | tf_op jit(solution)/shard_map/ppermute | solution.py:730
  59.9 5.0 %collective-permute-start.5 = (bf16[320,768]{1,0:T(8,128)(2,1)}, bf16[320,768]{1,0:T(8,128)(2,1)S(1)}, u32[]{:S(2)}, u32[]{:S(2)}) collective-permute-start(bf16[320,768]{1,0:T(8,128)(2,1)} %get-tuple-element.96), channel_id=1, source_target_pairs={{0,16},{16,0},{1,17},{17,1},{2,18},{18,2},{3,19},{19,3},{4,20},{20... | collective-permute-start | bytes 1474568 | tf_op jit(solution)/shard_map/ppermute | solution.py:725
  62.5 2.4 %collective-permute-start.4 = (bf16[320,768]{1,0:T(8,128)(2,1)S(1)}, bf16[320,768]{1,0:T(8,128)(2,1)S(1)}, u32[]{:S(2)}, u32[]{:S(2)}) collective-permute-start(bf16[320,768]{1,0:T(8,128)(2,1)S(1)} %get-tuple-element.97), channel_id=1, source_target_pairs={{0,16},{16,0},{1,17},{17,1},{2,18},{18,2},{3,19},{19,3},{4,20},{20... | collective-permute-start | bytes 1474568 | tf_op jit(solution)/shard_map/ppermute | solution.py:725
  70.4 24.4 %collective-permute-start.6 = (bf16[1,320,1536]{2,1,0:T(8,128)(2,1)}, bf16[1,320,1536]{2,1,0:T(8,128)(2,1)S(1)}, u32[]{:S(2)}, u32[]{:S(2)}) collective-permute-start(bf16[1,320,1536]{2,1,0:T(8,128)(2,1)} %get-tuple-element.60.mine), channel_id=1, source_target_pairs={{0,1},{1,0},{2,3},{3,2},{4,5},{5,4},{6,7},{7,6},{8,9},{9,8},{10,11... | collective-permute-start | bytes 2949128 | tf_op jit(solution)/shard_map/ppermute | solution.py:730
  79.9 3.6 %collective-permute-start.8 = (bf16[1,320,768]{2,1,0:T(8,128)(2,1)S(1)}, bf16[1,320,768]{2,1,0:T(8,128)(2,1)S(1)}, u32[]{:S(2)}, u32[]{:S(2)}) collective-permute-start(bf16[1,320,768]{2,1,0:T(8,128)(2,1)S(1)} %get-tuple-element.66), channel_id=1, source_target_pairs={{0,16},{16,0},{1,17},{17,1},{2,18},{18,2},{3,19},{19,3},{4,20},{20... | collective-permute-start | bytes 1474568 | tf_op jit(solution)/shard_map/ppermute | solution.py:725
  82.0 2.2 %collective-permute-start.9 = (bf16[1,320,768]{2,1,0:T(8,128)(2,1)S(1)}, bf16[1,320,768]{2,1,0:T(8,128)(2,1)S(1)}, u32[]{:S(2)}, u32[]{:S(2)}) collective-permute-start(bf16[1,320,768]{2,1,0:T(8,128)(2,1)S(1)} %get-tuple-element.67), channel_id=1, source_target_pairs={{0,16},{16,0},{1,17},{17,1},{2,18},{18,2},{3,19},{19,3},{4,20},{20... | collective-permute-start | bytes 1474568 | tf_op jit(solution)/shard_map/ppermute | solution.py:725
  86.5 27.8 %all-to-all-start.2 = ((bf16[16,40,768]{2,1,0:T(8,128)(2,1)}), bf16[16,40,768]{2,1,0:T(8,128)(2,1)}, u32[]{:S(2)}, u32[]{:S(2)}) async-start(bf16[16,40,768]{2,1,0:T(8,128)(2,1)} %bitcast.42), calls=%async_computation.2 | async-start | bytes 1966080 | tf_op jit(solution)/shard_map/all_to_all | solution.py:754
  94.8 37.5 %collective-permute-start.12 = (bf16[2,320,768]{2,1,0:T(8,128)(2,1)}, bf16[2,320,768]{2,1,0:T(8,128)(2,1)}, u32[]{:S(2)}, u32[]{:S(2)}) collective-permute-start(bf16[2,320,768]{2,1,0:T(8,128)(2,1)} %select_bitcast_fusion), channel_id=1, source_target_pairs={{0,1},{1,0},{2,3},{3,2},{4,5},{5,4},{6,7},{7,6},{8,9},{9,8},{10,11... | collective-permute-start | bytes 2949128 | tf_op jit(solution)/shard_map/ppermute | solution.py:730
  100.8 3.9 %collective-permute-start.10 = (bf16[1,320,768]{2,1,0:T(8,128)(2,1)S(1)}, bf16[1,320,768]{2,1,0:T(8,128)(2,1)S(1)}, u32[]{:S(2)}, u32[]{:S(2)}) collective-permute-start(bf16[1,320,768]{2,1,0:T(8,128)(2,1)S(1)} %get-tuple-element.71), channel_id=1, source_target_pairs={{0,16},{16,0},{1,17},{17,1},{2,18},{18,2},{3,19},{19,3},{4,20},{20... | collective-permute-start | bytes 1474568 | tf_op jit(solution)/shard_map/ppermute | solution.py:725
  103.2 2.2 %collective-permute-start.11 = (bf16[1,320,768]{2,1,0:T(8,128)(2,1)S(1)}, bf16[1,320,768]{2,1,0:T(8,128)(2,1)S(1)}, u32[]{:S(2)}, u32[]{:S(2)}) collective-permute-start(bf16[1,320,768]{2,1,0:T(8,128)(2,1)S(1)} %get-tuple-element.72), channel_id=1, source_target_pairs={{0,16},{16,0},{1,17},{17,1},{2,18},{18,2},{3,19},{19,3},{4,20},{20... | collective-permute-start | bytes 1474568 | tf_op jit(solution)/shard_map/ppermute | solution.py:725
  105.4 14.0 %copy-start.2 = (bf16[1,2,2,320,768]{4,3,2,1,0:T(8,128)(2,1)S(1)}, bf16[1,2,2,320,768]{4,3,2,1,0:T(8,128)(2,1)}, u32[]{:S(2)}) copy-start(bf16[1,2,2,320,768]{4,3,2,1,0:T(8,128)(2,1)} %get-tuple-element.62.refs_2_) | copy-start | bytes 5898244
  114.2 29.4 %all-to-all-start.3 = ((bf16[16,40,768]{2,1,0:T(8,128)(2,1)}), bf16[16,40,768]{2,1,0:T(8,128)(2,1)}, u32[]{:S(2)}, u32[]{:S(2)}) async-start(bf16[16,40,768]{2,1,0:T(8,128)(2,1)} %bitcast.43), calls=%async_computation.3 | async-start | bytes 1966080 | tf_op jit(solution)/shard_map/all_to_all | solution.py:754
  132.3 4.8 %collective-permute-start.13 = (bf16[2,320,768]{2,1,0:T(8,128)(2,1)}, bf16[2,320,768]{2,1,0:T(8,128)(2,1)S(1)}, u32[]{:S(2)}, u32[]{:S(2)}) collective-permute-start(bf16[2,320,768]{2,1,0:T(8,128)(2,1)} %collective-permute-done.12.refs_2_), channel_id=1, source_target_pairs={{0,16},{16,0},{1,17},{17,1},{2,18},{18,2},{3,19},{19,3},{4,20},{20... | collective-permute-start | bytes 2949128 | tf_op jit(solution)/shard_map/ppermute | solution.py:725
  149.0 3.0 %collective-permute-start.14 = (bf16[2,2,128,768]{3,2,1,0:T(8,128)(2,1)}, bf16[2,2,128,768]{3,2,1,0:T(8,128)(2,1)S(1)}, u32[]{:S(2)}, u32[]{:S(2)}) collective-permute-start(bf16[2,2,128,768]{3,2,1,0:T(8,128)(2,1)} %get-tuple-element.85), channel_id=1, source_target_pairs={{0,16},{16,0},{1,17},{17,1},{2,18},{18,2},{3,19},{19,3},{4,20},{20... | collective-permute-start | bytes 2359304 | tf_op jit(solution)/shard_map/ppermute | solution.py:725
  149.4 2.0 %collective-permute-start.15 = (f32[128,128]{1,0:T(8,128)S(1)}, f32[128,128]{1,0:T(8,128)S(1)}, u32[]{:S(2)}, u32[]{:S(2)}) collective-permute-start(f32[128,128]{1,0:T(8,128)S(1)} %get-tuple-element.90), channel_id=1, source_target_pairs={{0,16},{16,0},{1,17},{17,1},{2,18},{18,2},{3,19},{19,3},{4,20},{20... | collective-permute-start | bytes 196616 | tf_op jit(solution)/shard_map/ppermute | solution.py:725
  (13 other events, 62.3 us)

commit v4 on v3

--- a/solution.py
+++ b/solution.py
@@ -182,9 +182,12 @@
     )(routes, gates, tokens, cotangent)
 
 
-def partial_kernel(dims, chunk, ids, own, other_low, other_high, weights, *rest):
-    subs, groups, per_chunk, cap, block = dims
-    features, partial, held, arrivals = rest
+def partial_kernel(dims, chunk, pick, ids, own, other_low, other_high, weights, *rest):
+    subs, groups, per_chunk, cap, block = dims
+    if pick:
+        features, partial, leaving, held, arrivals, departure = rest[chunk:]
+    else:
+        features, partial, held, arrivals = rest
     q = ids[0]
     width = own.shape[1]
     units = weights.shape[3]
@@ -219,6 +222,12 @@
                     features[i, side, half, g * part : (g + 1) * part, :] = sorted_rows[
                         start : start + part
                     ]
+    if pick:
+
+        @pl.when(ids[1] != chunk)
+        def _():
+            pltpu.make_async_copy(features.at[0, 0], leaving, departure).start()
+
     for m in range(3):
         loads[m].wait()
         half = 1 if m == 2 else 0
@@ -230,6 +239,11 @@
                 term = dot(features[i, side, half], block_rows, 1, 0)
                 total = term if total is None else total + term
             partial[i, :, m * units : (m + 1) * units] = total.astype(BF16)
+    if pick:
+
+        @pl.when(ids[1] != chunk)
+        def _():
+            pltpu.make_async_copy(features.at[0, 0], leaving, departure).wait()
 
 
 def gather_group(cap):
@@ -239,7 +253,7 @@
     return count
 
 
-def partial_products(dims, chunk, ids, own, others, weights):
+def partial_products(dims, chunk, ids, own, others, weights, leaving):
     subs, groups, per_chunk, cap, block = dims
     rows = subs * cap
     width = own.shape[1]
@@ -248,12 +262,24 @@
     in_specs = [whole(own.shape)] + [whole(o.shape) for o in others]
     in_specs.append(pl.BlockSpec(memory_space=pltpu.HBM))
     operands = [ids, own, *others, weights]
-    return pl.pallas_call(
-        functools.partial(partial_kernel, dims, chunk),
+    pick = groups == 2
+    leaving_shape, leaving_spec, departure, aliases = (), (), [], {}
+    if pick:
+        leaving_shape = (pltpu.HBM((2, rows, width), BF16),)
+        leaving_spec = (pl.BlockSpec(memory_space=pl.ANY),)
+        departure = [pltpu.SemaphoreType.DMA]
+        if chunk:
+            in_specs.append(pl.BlockSpec(memory_space=pl.ANY))
+            aliases = {len(operands): 2}
+            operands.append(leaving)
+    return pl.pallas_call(
+        functools.partial(partial_kernel, dims, chunk, pick),
         out_shape=(
             pltpu.HBM((per_chunk, 2, 2, rows, width), BF16),
             jax.ShapeDtypeStruct((per_chunk, rows, 3 * units), BF16),
-        ),
+        )
+        + leaving_shape,
+        input_output_aliases=aliases,
         grid_spec=pltpu.PrefetchScalarGridSpec(
             num_scalar_prefetch=1,
             grid=(1,),
@@ -261,11 +287,13 @@
             out_specs=(
                 whole((per_chunk, 2, 2, rows, width)),
                 whole((per_chunk, rows, 3 * units)),
-            ),
+            )
+            + leaving_spec,
             scratch_shapes=[
                 pltpu.VMEM((3, per_chunk, depth, units), BF16),
                 pltpu.SemaphoreType.DMA((3,)),
-            ],
+            ]
+            + departure,
         ),
         compiler_params=params(BIG),
         cost_estimate=cost(
@@ -784,10 +812,12 @@
             axis_index_groups=peers,
         )
         arrived.append(moved.reshape(subs * block, width))
-    features, acts, mine, theirs, returned = [], [], [], [], []
+    features, acts, mine, theirs, returned, leaving = [], [], [], [], [], []
     for c in range(CHUNKS):
         others = [swap_cores(part) for part in jnp.split(arrived[c], 2)]
-        rows, partial = partial_products(dims, c, ids, arrived[c], others, weights)
+        rows, partial, *leaving = partial_products(
+            dims, c, ids, arrived[c], others, weights, leaving[0] if leaving else None
+        )
         features.append(rows)
         if c + 1 < CHUNKS:
             arrived[c + 1], _ = together(arrived[c + 1], partial)
@@ -797,8 +827,9 @@
             mask *= 2
         mine.append(partial)
         theirs.append(swap_holders(partial, mask))
-    by_sub = [features[s // per_chunk][s % per_chunk, 0] for s in range(groups)]
-    leaving = [choose(by_sub, holder ^ mask) for mask in range(1, groups)]
+    if not leaving:
+        by_sub = [features[s // per_chunk][s % per_chunk, 0] for s in range(groups)]
+        leaving = [choose(by_sub, holder ^ mask) for mask in range(1, groups)]
     theirs[0], _, *leaving = together(theirs[0], mine[-1], *leaving)
     for c in range(CHUNKS):
         active, *parts = output_products(dims, c, ids, mine[c], theirs[c], weights)

time: 156 us -> 155 us (level)
  local copies, waits for them, and re-layouts: 8.36 us -> 12.3 us
  waiting for transfers between devices: 44.5 us -> 40.7 us
  starting transfers between devices: 38.6 us -> 40.2 us
    unnamed x37 -> x27, local copies, waits for them, and re-layouts: 7.38 us -> 10.9 us
    select_n x1 -> x0, other arithmetic: 2.26 us -> none  [choose(): result = jnp.where(index == i, values[i], result)]
  transfers between devices with their start and end apart: 20 -> 20, of which waited for: 15 -> 16; matrix products, arithmetic and copies ran while one was open for 3% -> 4% of each run, Pallas kernels for 32% -> 31%
where the time goes in v4:
time: 155 us; the launch traced here: 153 us
  Pallas kernels  56.8 us (37%)
  waiting for transfers between devices  40.7 us (26%)
  starting transfers between devices  40.2 us (26%)
  local copies, waits for them, and re-layouts  12.3 us (8%)
  other arithmetic  2.27 us (1%)
    all_to_all x3, starting transfers between devices, exchange(): lax.all_to_all(blocks, 'expert', split_axis=0, concat_axis=0, tiled=True)  17.6 us
    ppermute x11, starting transfers between devices, swap_cores(): return lax.ppermute(value, 'dp', [(0, 1), (1, 0)])  14.3 us
    ppermute x11, waiting for transfers between devices, swap_cores(): return lax.ppermute(value, 'dp', [(0, 1), (1, 0)])  12.7 us
    pallas_call x2, Pallas kernels, partial_products(): pl.pallas_call(functools.partial(partial_kernel, dims, chunk, pick), out_...  12.3 us
    ppermute x5, waiting for transfers between devices, swap_holders(): lax.ppermute(value, 'expert', [(source, source ^ mask) for source in rang...  11.2 us
    pallas_call x2, Pallas kernels, output_products(): pl.pallas_call(functools.partial(output_kernel, dims, chunk), out_shape=(...  10.9 us
    unnamed x27, local copies, waits for them, and re-layouts  10.9 us
    all_to_all x3, waiting for transfers between devices, exchange(): lax.all_to_all(blocks, 'expert', split_axis=0, concat_axis=0, tiled=True)  9.35 us
  transfers between devices with their start and end apart: 20, of which 16 were waited for; matrix products, arithmetic and copies ran while one was open for 4% of the time, Pallas kernels for 31%

profile of v4, /device:TPU:17, one launch (start us, length us, event | category | flops | bytes accessed | tf_op | source)
XLA Modules:
  0.0 153.3 jit_solution(17947615196865881160)
XLA Ops:
  0.6 3.5 %dispatch_0.1 = bf16[8,2,40,768]{3,2,1,0:T(8,128)(2,1)} custom-call(s32[2,128]{1,0:T(2,128)} %bitcast.43, f32[2,128]{1,0:T(2,128)} %bitcast.44, bf16[128,3072]{1,0:T(8,128)(2,1)} %tokens.1, bf16[128,3072]{1,0:T(8,128)(2,1)} %cotangent.3), custom_call_target="tpu_custom_call" | custom-call | flops 2516582 | bytes 17694 | tf_op jit(solution)/shard_map/dispatch_0/pallas_call | solution.py:165
  4.2 6.6 %all-to-all-start.1 = ((bf16[16,40,768]{2,1,0:T(8,128)(2,1)}), bf16[16,40,768]{2,1,0:T(8,128)(2,1)S(1)}, u32[]{:S(2)}, u32[]{:S(2)}) async-start(bf16[16,40,768]{2,1,0:T(8,128)(2,1)} %bitcast.40), calls=%async_computation.1 | async-start | bytes 1966080 | tf_op jit(solution)/shard_map/all_to_all | solution.py:782
  18.1 2.8 %choosers.1 = (f32[128,2]{1,0:T(8,128)S(1)}, bf16[2,384,640]{2,1,0:T(8,128)(2,1)}, bf16[2,384,640]{2,1,0:T(8,128)(2,1)}) custom-call(s32[2]{0:T(128)S(1)} %pad_add_fusion.ids, s32[128,2]{1,0:T(8,128)S(1)} %copy.14.routes, f32[128,2]{1,0:T(8,128)S(1)} %copy.15.gates, s32[8,640]{1,0:T(8,128)S(1)} %copy-done.8), custom_call_target="tpu_custom_call" | custom-call | bytes 19660 | tf_op jit(solution)/shard_map/choosers/pallas_call | solution.py:466
  20.9 4.5 %collective-permute-done.refs_1_ = f32[4,128]{1,0:T(4,128)S(1)} collective-permute-done((f32[4,128]{1,0:T(4,128)S(1)}, f32[4,128]{1,0:T(4,128)S(1)}, u32[]{:S(2)}, u32[]{:S(2)}) %collective-permute-start) | collective-permute-done | bytes 2080 | tf_op jit(solution)/shard_map/ppermute | solution.py:758
  26.7 3.1 %group_dispatch_1.1 = bf16[8,2,40,768]{3,2,1,0:T(8,128)(2,1)} custom-call(f32[4,128]{1,0:T(4,128)} %copy-done.10, f32[4,128]{1,0:T(4,128)} %copy-done.11, bf16[2,128,768]{2,1,0:T(8,128)(2,1)} %pad_maximum_fusion.refs_2_, bf16[2,128,768]{2,1,0:T(8,128)(2,1)} %copy-done.9), custom_call_target="tpu_custom_call" | custom-call | flops 2516582 | bytes 17694 | tf_op jit(solution)/shard_map/group_dispatch_1/pallas_call | solution.py:132
  29.7 3.6 %all-to-all-done.1 = bf16[16,40,768]{2,1,0:T(8,128)(2,1)S(1)} async-done(((bf16[16,40,768]{2,1,0:T(8,128)(2,1)}), bf16[16,40,768]{2,1,0:T(8,128)(2,1)S(1)}, u32[]{:S(2)}, u32[]{:S(2)}) %all-to-all-start.1) | async-done | bytes 983072 | tf_op jit(solution)/shard_map/all_to_all | solution.py:782
  33.3 5.4 %all-to-all-start = ((bf16[8,80,768]{2,1,0:T(8,128)(2,1)}), bf16[8,80,768]{2,1,0:T(8,128)(2,1)S(1)}, u32[]{:S(2)}, u32[]{:S(2)}) async-start(bf16[8,80,768]{2,1,0:T(8,128)(2,1)} %bitcast.39), calls=%async_computation | async-start | bytes 1966080 | tf_op jit(solution)/shard_map/all_to_all | solution.py:806
  38.8 3.7 %collective-permute-start.3 = (bf16[320,768]{1,0:T(8,128)(2,1)S(1)}, bf16[320,768]{1,0:T(8,128)(2,1)S(1)}, u32[]{:S(2)}, u32[]{:S(2)}) collective-permute-start(bf16[320,768]{1,0:T(8,128)(2,1)S(1)} %get-tuple-element.102), channel_id=1, source_target_pairs={{0,16},{16,0},{1,17},{17,1},{2,18},{18,2},{3,19},{19,3},{4,20},{20... | collective-permute-start | bytes 1474568 | tf_op jit(solution)/shard_map/ppermute | solution.py:753
  44.7 5.8 %partial_0.1 = (bf16[1,2,2,320,768]{4,3,2,1,0:T(8,128)(2,1)}, bf16[1,320,1536]{2,1,0:T(8,128)(2,1)S(1)}, bf16[2,320,768]{2,1,0:T(8,128)(2,1)}) custom-call(s32[2]{0:T(128)S(1)} %pad_add_fusion.ids, bf16[640,768]{1,0:T(8,128)(2,1)S(1)} %bitcast.30, bf16[320,768]{1,0:T(8,128)(2,1)S(1)} %collective-permute-done.2.other_low, ...), custom_call_target="tpu_custom_call" | custom-call | flops 27682406 | bytes 96337 | tf_op jit(solution)/shard_map/partial_0/pallas_call | solution.py:275
  51.2 7.4 %all-to-all-done = bf16[8,80,768]{2,1,0:T(8,128)(2,1)S(1)} async-done(((bf16[8,80,768]{2,1,0:T(8,128)(2,1)}), bf16[8,80,768]{2,1,0:T(8,128)(2,1)S(1)}, u32[]{:S(2)}, u32[]{:S(2)}) %all-to-all-start) | async-done | bytes 983072 | tf_op jit(solution)/shard_map/all_to_all | solution.py:806
  58.7 2.9 %collective-permute-start.5 = (bf16[320,768]{1,0:T(8,128)(2,1)S(1)}, bf16[320,768]{1,0:T(8,128)(2,1)S(1)}, u32[]{:S(2)}, u32[]{:S(2)}) collective-permute-start(bf16[320,768]{1,0:T(8,128)(2,1)S(1)} %get-tuple-element.100), channel_id=1, source_target_pairs={{0,16},{16,0},{1,17},{17,1},{2,18},{18,2},{3,19},{19,3},{4,20},{20... | collective-permute-start | bytes 1474568 | tf_op jit(solution)/shard_map/ppermute | solution.py:753
  63.7 6.5 %partial_1.1 = (bf16[1,2,2,320,768]{4,3,2,1,0:T(8,128)(2,1)}, bf16[1,320,1536]{2,1,0:T(8,128)(2,1)}, bf16[2,320,768]{2,1,0:T(8,128)(2,1)}) custom-call(s32[2]{0:T(128)S(1)} %pad_add_fusion.ids, bf16[640,768]{1,0:T(8,128)(2,1)S(1)} %bitcast.32, bf16[320,768]{1,0:T(8,128)(2,1)S(1)} %collective-permute-done.4.other_low, ...), custom_call_target="tpu_custom_call", output_to_operand_aliasing={{2}: (5, {})} | custom-call | flops 27682406 | bytes 96337 | tf_op jit(solution)/shard_map/partial_1/pallas_call | solution.py:275
  70.3 3.2 %collective-permute-done.7.theirs = bf16[1,320,1536]{2,1,0:T(8,128)(2,1)S(1)} collective-permute-done((bf16[1,320,1536]{2,1,0:T(8,128)(2,1)S(1)}, bf16[1,320,1536]{2,1,0:T(8,128)(2,1)S(1)}, u32[]{:S(2)}, u32[]{:S(2)}) %collective-permute-start.7) | collective-permute-done | bytes 983072 | tf_op jit(solution)/shard_map/ppermute | solution.py:758
  73.5 5.1 %output_0.1 = (bf16[1,320,1536]{2,1,0:T(8,128)(2,1)}, bf16[1,320,768]{2,1,0:T(8,128)(2,1)S(1)}, bf16[1,320,768]{2,1,0:T(8,128)(2,1)S(1)}, bf16[1,320,768]{2,1,0:T(8,128)(2,1)S(1)}, bf16[1,320,768]{2,1,0:T(8,128)(2,1)S(1)}) custom-call(s32[2]{0:T(128)S(1)} %pad_add_fusion.ids, bf16[1,320,1536]{2,1,0:T(8,128)(2,1)S(1)} %get-tuple-element.60.mine, ...), custom_call_target="tpu_custom_call" | custom-call | flops 45298483200 | bytes 289013760 | tf_op jit(solution)/shard_map/output_0/pallas_call | solution.py:358
  85.2 5.8 %all-to-all-start.2 = ((bf16[16,40,768]{2,1,0:T(8,128)(2,1)}), bf16[16,40,768]{2,1,0:T(8,128)(2,1)S(1)}, u32[]{:S(2)}, u32[]{:S(2)}) async-start(bf16[16,40,768]{2,1,0:T(8,128)(2,1)} %bitcast.41), calls=%async_computation.2 | async-start | bytes 1966080 | tf_op jit(solution)/shard_map/all_to_all | solution.py:782
  91.0 3.6 %collective-permute-done.6.theirs = bf16[1,320,1536]{2,1,0:T(8,128)(2,1)S(1)} collective-permute-done((bf16[1,320,1536]{2,1,0:T(8,128)(2,1)}, bf16[1,320,1536]{2,1,0:T(8,128)(2,1)S(1)}, u32[]{:S(2)}, u32[]{:S(2)}) %collective-permute-start.6) | collective-permute-done | bytes 983072 | tf_op jit(solution)/shard_map/ppermute | solution.py:758
  95.2 5.8 %output_1.1 = (bf16[1,320,1536]{2,1,0:T(8,128)(2,1)}, bf16[1,320,768]{2,1,0:T(8,128)(2,1)S(1)}, bf16[1,320,768]{2,1,0:T(8,128)(2,1)S(1)}, bf16[1,320,768]{2,1,0:T(8,128)(2,1)S(1)}, bf16[1,320,768]{2,1,0:T(8,128)(2,1)S(1)}) custom-call(s32[2]{0:T(128)S(1)} %pad_add_fusion.ids, bf16[1,320,1536]{2,1,0:T(8,128)(2,1)} %get-tuple-element.63.mine, ...), custom_call_target="tpu_custom_call" | custom-call | flops 45298483200 | bytes 289013760 | tf_op jit(solution)/shard_map/output_1/pallas_call | solution.py:358
  107.9 5.7 %all-to-all-done.2 = bf16[16,40,768]{2,1,0:T(8,128)(2,1)S(1)} async-done(((bf16[16,40,768]{2,1,0:T(8,128)(2,1)}), bf16[16,40,768]{2,1,0:T(8,128)(2,1)S(1)}, u32[]{:S(2)}, u32[]{:S(2)}) %all-to-all-start.2) | async-done | bytes 983072 | tf_op jit(solution)/shard_map/all_to_all | solution.py:782
  113.6 5.2 %all-to-all-start.3 = ((bf16[16,40,768]{2,1,0:T(8,128)(2,1)}), bf16[16,40,768]{2,1,0:T(8,128)(2,1)}, u32[]{:S(2)}, u32[]{:S(2)}) async-start(bf16[16,40,768]{2,1,0:T(8,128)(2,1)} %bitcast.42), calls=%async_computation.3 | async-start | bytes 1966080 | tf_op jit(solution)/shard_map/all_to_all | solution.py:782
  123.2 5.8 %near_weight_grads.1.refs_4_ = bf16[3,3072,512]{2,1,0:T(8,128)(2,1)} custom-call(s32[2]{0:T(128)S(1)} %pad_add_fusion.ids, bf16[1,320,1536]{2,1,0:T(8,128)(2,1)S(1)} %copy-done.1, bf16[1,320,1536]{2,1,0:T(8,128)(2,1)S(1)} %copy-done.3, bf16[1,2,2,320,768]{4,3,2,1,0:T(8,128)(2,1)S(1)} %copy-done.4, bf16[1,2,2,320,768]{4,3,2,1,0:T(8,128)(2,1)S(1)} %copy-done.5), custom_call_target="tpu_custom_call" | custom-call | flops 15099494 | bytes 66846 | tf_op jit(solution)/shard_map/near_weight_grads/pallas_call | solution.py:669
  132.0 2.5 %collective-permute-start.13 = (bf16[2,320,768]{2,1,0:T(8,128)(2,1)}, bf16[2,320,768]{2,1,0:T(8,128)(2,1)S(1)}, u32[]{:S(2)}, u32[]{:S(2)}) collective-permute-start(bf16[2,320,768]{2,1,0:T(8,128)(2,1)} %collective-permute-done.12.refs_2_), channel_id=1, source_target_pairs={{0,16},{16,0},{1,17},{17,1},{2,18},{18,2},{3,19},{19,3},{4,20},{20... | collective-permute-start | bytes 2949128 | tf_op jit(solution)/shard_map/ppermute | solution.py:753
  134.5 2.4 %collective-permute-done.13.refs_3_ = bf16[2,320,768]{2,1,0:T(8,128)(2,1)S(1)} collective-permute-done((bf16[2,320,768]{2,1,0:T(8,128)(2,1)}, bf16[2,320,768]{2,1,0:T(8,128)(2,1)S(1)}, u32[]{:S(2)}, u32[]{:S(2)}) %collective-permute-start.13) | collective-permute-done | bytes 983072 | tf_op jit(solution)/shard_map/ppermute | solution.py:753
  136.9 6.4 %far_weight_grads.1 = bf16[3,3072,512]{2,1,0:T(8,128)(2,1)} custom-call(s32[2]{0:T(128)S(1)} %pad_add_fusion.ids, bf16[1,320,1536]{2,1,0:T(8,128)(2,1)S(1)} %copy-done.2, bf16[1,320,1536]{2,1,0:T(8,128)(2,1)S(1)} %copy-done.3, bf16[2,320,768]{2,1,0:T(8,128)(2,1)} %collective-permute-done.12.refs_2_, ...), custom_call_target="tpu_custom_call", output_to_operand_aliasing={{}: (5, {})} | custom-call | flops 6039797760 | bytes 26738688 | tf_op jit(solution)/shard_map/far_weight_grads/pallas_call | solution.py:719
  144.5 4.2 %combine.1 = (bf16[2,2,128,768]{3,2,1,0:T(8,128)(2,1)}, f32[128,128]{1,0:T(8,128)S(1)}, bf16[128,3072]{1,0:T(8,128)(2,1)}, bf16[128,3072]{1,0:T(8,128)(2,1)}) custom-call(s32[2]{0:T(128)S(1)} %pad_add_fusion.ids, f32[128,2]{1,0:T(8,128)S(1)} %get-tuple-element.55.gates, bf16[128,3072]{1,0:T(8,128)(2,1)S(1)} %copy-done, bf16[2,384,640]{2,1,0:T(8,128)(2,1)S(1)} %copy-done.6, ...), custom_call_target="tpu_custom_call" | custom-call | flops 7549747 | bytes 19660 | tf_op jit(solution)/shard_map/combine/pallas_call | solution.py:540
  (66 shorter events, 41.0 us)
Async XLA Ops:
  4.2 29.1 %all-to-all-start.1 = ((bf16[16,40,768]{2,1,0:T(8,128)(2,1)}), bf16[16,40,768]{2,1,0:T(8,128)(2,1)S(1)}, u32[]{:S(2)}, u32[]{:S(2)}) async-start(bf16[16,40,768]{2,1,0:T(8,128)(2,1)} %bitcast.40), calls=%async_computation.1 | async-start | bytes 1966080 | tf_op jit(solution)/shard_map/all_to_all | solution.py:782
  12.1 13.3 %collective-permute-start.1 = (bf16[2,128,768]{2,1,0:T(8,128)(2,1)S(1)}, bf16[2,128,768]{2,1,0:T(8,128)(2,1)S(1)}, u32[]{:S(2)}, u32[]{:S(2)}) collective-permute-start(bf16[2,128,768]{2,1,0:T(8,128)(2,1)S(1)} %pad_maximum_fusion.1), channel_id=1, source_target_pairs={{0,1},{1,0},{2,3},{3,2},{4,5},{5,4},{6,7},{7,6},{8,9},{9,8},{10,11... | collective-permute-start | bytes 1179656 | tf_op jit(solution)/shard_map/ppermute | solution.py:758
  14.7 10.7 %copy-start.10 = (f32[4,128]{1,0:T(4,128)}, f32[4,128]{1,0:T(4,128)S(1)}, u32[]{:S(2)}) copy-start(f32[4,128]{1,0:T(4,128)S(1)} %pad_maximum_fusion.2.refs_0_) | copy-start | bytes 6148
  14.7 10.7 %collective-permute-start = (f32[4,128]{1,0:T(4,128)S(1)}, f32[4,128]{1,0:T(4,128)S(1)}, u32[]{:S(2)}, u32[]{:S(2)}) collective-permute-start(f32[4,128]{1,0:T(4,128)S(1)} %pad_maximum_fusion.2.refs_0_), channel_id=1, source_target_pairs={{0,1},{1,0},{2,3},{3,2},{4,5},{5,4},{6,7},{7,6},{8,9},{9,8},{10,11... | collective-permute-start | bytes 6152 | tf_op jit(solution)/shard_map/ppermute | solution.py:758
  33.3 25.3 %all-to-all-start = ((bf16[8,80,768]{2,1,0:T(8,128)(2,1)}), bf16[8,80,768]{2,1,0:T(8,128)(2,1)S(1)}, u32[]{:S(2)}, u32[]{:S(2)}) async-start(bf16[8,80,768]{2,1,0:T(8,128)(2,1)} %bitcast.39), calls=%async_computation | async-start | bytes 1966080 | tf_op jit(solution)/shard_map/all_to_all | solution.py:806
  38.8 5.2 %collective-permute-start.3 = (bf16[320,768]{1,0:T(8,128)(2,1)S(1)}, bf16[320,768]{1,0:T(8,128)(2,1)S(1)}, u32[]{:S(2)}, u32[]{:S(2)}) collective-permute-start(bf16[320,768]{1,0:T(8,128)(2,1)S(1)} %get-tuple-element.102), channel_id=1, source_target_pairs={{0,16},{16,0},{1,17},{17,1},{2,18},{18,2},{3,19},{19,3},{4,20},{20... | collective-permute-start | bytes 1474568 | tf_op jit(solution)/shard_map/ppermute | solution.py:753
  42.5 2.2 %collective-permute-start.2 = (bf16[320,768]{1,0:T(8,128)(2,1)S(1)}, bf16[320,768]{1,0:T(8,128)(2,1)S(1)}, u32[]{:S(2)}, u32[]{:S(2)}) collective-permute-start(bf16[320,768]{1,0:T(8,128)(2,1)S(1)} %get-tuple-element.103), channel_id=1, source_target_pairs={{0,16},{16,0},{1,17},{17,1},{2,18},{18,2},{3,19},{19,3},{4,20},{20... | collective-permute-start | bytes 1474568 | tf_op jit(solution)/shard_map/ppermute | solution.py:753
  50.5 23.0 %collective-permute-start.7 = (bf16[1,320,1536]{2,1,0:T(8,128)(2,1)S(1)}, bf16[1,320,1536]{2,1,0:T(8,128)(2,1)S(1)}, u32[]{:S(2)}, u32[]{:S(2)}) collective-permute-start(bf16[1,320,1536]{2,1,0:T(8,128)(2,1)S(1)} %get-tuple-element.60.mine), channel_id=1, source_target_pairs={{0,1},{1,0},{2,3},{3,2},{4,5},{5,4},{6,7},{7,6},{8,9},{9,8},{10,11... | collective-permute-start | bytes 2949128 | tf_op jit(solution)/shard_map/ppermute | solution.py:758
  58.7 4.4 %collective-permute-start.5 = (bf16[320,768]{1,0:T(8,128)(2,1)S(1)}, bf16[320,768]{1,0:T(8,128)(2,1)S(1)}, u32[]{:S(2)}, u32[]{:S(2)}) collective-permute-start(bf16[320,768]{1,0:T(8,128)(2,1)S(1)} %get-tuple-element.100), channel_id=1, source_target_pairs={{0,16},{16,0},{1,17},{17,1},{2,18},{18,2},{3,19},{19,3},{4,20},{20... | collective-permute-start | bytes 1474568 | tf_op jit(solution)/shard_map/ppermute | solution.py:753
  61.5 2.2 %collective-permute-start.4 = (bf16[320,768]{1,0:T(8,128)(2,1)S(1)}, bf16[320,768]{1,0:T(8,128)(2,1)S(1)}, u32[]{:S(2)}, u32[]{:S(2)}) collective-permute-start(bf16[320,768]{1,0:T(8,128)(2,1)S(1)} %get-tuple-element.101), channel_id=1, source_target_pairs={{0,16},{16,0},{1,17},{17,1},{2,18},{18,2},{3,19},{19,3},{4,20},{20... | collective-permute-start | bytes 1474568 | tf_op jit(solution)/shard_map/ppermute | solution.py:753
  70.2 24.3 %collective-permute-start.6 = (bf16[1,320,1536]{2,1,0:T(8,128)(2,1)}, bf16[1,320,1536]{2,1,0:T(8,128)(2,1)S(1)}, u32[]{:S(2)}, u32[]{:S(2)}) collective-permute-start(bf16[1,320,1536]{2,1,0:T(8,128)(2,1)} %get-tuple-element.63.mine), channel_id=1, source_target_pairs={{0,1},{1,0},{2,3},{3,2},{4,5},{5,4},{6,7},{7,6},{8,9},{9,8},{10,11... | collective-permute-start | bytes 2949128 | tf_op jit(solution)/shard_map/ppermute | solution.py:758
  78.6 3.6 %collective-permute-start.8 = (bf16[1,320,768]{2,1,0:T(8,128)(2,1)S(1)}, bf16[1,320,768]{2,1,0:T(8,128)(2,1)S(1)}, u32[]{:S(2)}, u32[]{:S(2)}) collective-permute-start(bf16[1,320,768]{2,1,0:T(8,128)(2,1)S(1)} %get-tuple-element.68), channel_id=1, source_target_pairs={{0,16},{16,0},{1,17},{17,1},{2,18},{18,2},{3,19},{19,3},{4,20},{20... | collective-permute-start | bytes 1474568 | tf_op jit(solution)/shard_map/ppermute | solution.py:753
  80.7 2.2 %collective-permute-start.9 = (bf16[1,320,768]{2,1,0:T(8,128)(2,1)S(1)}, bf16[1,320,768]{2,1,0:T(8,128)(2,1)S(1)}, u32[]{:S(2)}, u32[]{:S(2)}) collective-permute-start(bf16[1,320,768]{2,1,0:T(8,128)(2,1)S(1)} %get-tuple-element.69), channel_id=1, source_target_pairs={{0,16},{16,0},{1,17},{17,1},{2,18},{18,2},{3,19},{19,3},{4,20},{20... | collective-permute-start | bytes 1474568 | tf_op jit(solution)/shard_map/ppermute | solution.py:753
  85.2 28.5 %all-to-all-start.2 = ((bf16[16,40,768]{2,1,0:T(8,128)(2,1)}), bf16[16,40,768]{2,1,0:T(8,128)(2,1)S(1)}, u32[]{:S(2)}, u32[]{:S(2)}) async-start(bf16[16,40,768]{2,1,0:T(8,128)(2,1)} %bitcast.41), calls=%async_computation.2 | async-start | bytes 1966080 | tf_op jit(solution)/shard_map/all_to_all | solution.py:782
  91.0 27.9 %copy-start.1 = (bf16[1,320,1536]{2,1,0:T(8,128)(2,1)S(1)}, bf16[1,320,1536]{2,1,0:T(8,128)(2,1)}, u32[]{:S(2)}) copy-start(bf16[1,320,1536]{2,1,0:T(8,128)(2,1)} %get-tuple-element.78.refs_0_) | copy-start | bytes 2949124
  94.6 37.4 %collective-permute-start.12 = (bf16[2,320,768]{2,1,0:T(8,128)(2,1)}, bf16[2,320,768]{2,1,0:T(8,128)(2,1)}, u32[]{:S(2)}, u32[]{:S(2)}) collective-permute-start(bf16[2,320,768]{2,1,0:T(8,128)(2,1)} %get-tuple-element.77), channel_id=1, source_target_pairs={{0,1},{1,0},{2,3},{3,2},{4,5},{5,4},{6,7},{7,6},{8,9},{9,8},{10,11... | collective-permute-start | bytes 2949128 | tf_op jit(solution)/shard_map/ppermute | solution.py:758
  101.1 3.8 %collective-permute-start.10 = (bf16[1,320,768]{2,1,0:T(8,128)(2,1)S(1)}, bf16[1,320,768]{2,1,0:T(8,128)(2,1)S(1)}, u32[]{:S(2)}, u32[]{:S(2)}) collective-permute-start(bf16[1,320,768]{2,1,0:T(8,128)(2,1)S(1)} %get-tuple-element.73), channel_id=1, source_target_pairs={{0,16},{16,0},{1,17},{17,1},{2,18},{18,2},{3,19},{19,3},{4,20},{20... | collective-permute-start | bytes 1474568 | tf_op jit(solution)/shard_map/ppermute | solution.py:753
  103.4 2.2 %collective-permute-start.11 = (bf16[1,320,768]{2,1,0:T(8,128)(2,1)S(1)}, bf16[1,320,768]{2,1,0:T(8,128)(2,1)S(1)}, u32[]{:S(2)}, u32[]{:S(2)}) collective-permute-start(bf16[1,320,768]{2,1,0:T(8,128)(2,1)S(1)} %get-tuple-element.74), channel_id=1, source_target_pairs={{0,16},{16,0},{1,17},{17,1},{2,18},{18,2},{3,19},{19,3},{4,20},{20... | collective-permute-start | bytes 1474568 | tf_op jit(solution)/shard_map/ppermute | solution.py:753
  113.6 29.6 %all-to-all-start.3 = ((bf16[16,40,768]{2,1,0:T(8,128)(2,1)}), bf16[16,40,768]{2,1,0:T(8,128)(2,1)}, u32[]{:S(2)}, u32[]{:S(2)}) async-start(bf16[16,40,768]{2,1,0:T(8,128)(2,1)} %bitcast.42), calls=%async_computation.3 | async-start | bytes 1966080 | tf_op jit(solution)/shard_map/all_to_all | solution.py:782
  123.1 13.7 %copy-start.2 = (bf16[1,320,1536]{2,1,0:T(8,128)(2,1)S(1)}, bf16[1,320,1536]{2,1,0:T(8,128)(2,1)}, u32[]{:S(2)}) copy-start(bf16[1,320,1536]{2,1,0:T(8,128)(2,1)} %get-tuple-element.78.refs_0_) | copy-start | bytes 2949124
  132.0 11.3 %copy-start = (bf16[128,3072]{1,0:T(8,128)(2,1)S(1)}, bf16[128,3072]{1,0:T(8,128)(2,1)}, u32[]{:S(2)}) copy-start(bf16[128,3072]{1,0:T(8,128)(2,1)} %cotangent.3) | copy-start | bytes 2359300
  132.0 4.9 %collective-permute-start.13 = (bf16[2,320,768]{2,1,0:T(8,128)(2,1)}, bf16[2,320,768]{2,1,0:T(8,128)(2,1)S(1)}, u32[]{:S(2)}, u32[]{:S(2)}) collective-permute-start(bf16[2,320,768]{2,1,0:T(8,128)(2,1)} %collective-permute-done.12.refs_2_), channel_id=1, source_target_pairs={{0,16},{16,0},{1,17},{17,1},{2,18},{18,2},{3,19},{19,3},{4,20},{20... | collective-permute-start | bytes 2949128 | tf_op jit(solution)/shard_map/ppermute | solution.py:753
  148.7 3.0 %collective-permute-start.14 = (bf16[2,2,128,768]{3,2,1,0:T(8,128)(2,1)}, bf16[2,2,128,768]{3,2,1,0:T(8,128)(2,1)S(1)}, u32[]{:S(2)}, u32[]{:S(2)}) collective-permute-start(bf16[2,2,128,768]{3,2,1,0:T(8,128)(2,1)} %get-tuple-element.89), channel_id=1, source_target_pairs={{0,16},{16,0},{1,17},{17,1},{2,18},{18,2},{3,19},{19,3},{4,20},{20... | collective-permute-start | bytes 2359304 | tf_op jit(solution)/shard_map/ppermute | solution.py:753
  149.1 2.0 %collective-permute-start.15 = (f32[128,128]{1,0:T(8,128)S(1)}, f32[128,128]{1,0:T(8,128)S(1)}, u32[]{:S(2)}, u32[]{:S(2)}) collective-permute-start(f32[128,128]{1,0:T(8,128)S(1)} %get-tuple-element.94), channel_id=1, source_target_pairs={{0,16},{16,0},{1,17},{17,1},{2,18},{18,2},{3,19},{19,3},{4,20},{20... | collective-permute-start | bytes 196616 | tf_op jit(solution)/shard_map/ppermute | solution.py:753
  (8 other events, 8.7 us)

commit v5 on v4

--- a/solution.py
+++ b/solution.py
@@ -405,7 +405,7 @@
     subs, groups, per_chunk, cap, block = dims
     rows = subs * cap
     width = parts[0].shape[2]
-    columns = 256 if width % 256 == 0 else width
+    columns = 384 if width % 384 == 0 else width
     spec = pl.BlockSpec((per_chunk, rows, columns), lambda c: (0, 0, c))
     return pl.pallas_call(
         functools.partial(pack_kernel, dims),

time: 155 us -> 155 us (level)
  no operation moved by 1% of the time
where the time goes in v5:
time: 155 us; the launch traced here: 153 us
  Pallas kernels  56 us (36%)
  waiting for transfers between devices  41.2 us (27%)
  starting transfers between devices  40.2 us (26%)
  local copies, waits for them, and re-layouts  12.3 us (8%)
  other arithmetic  2.27 us (1%)
    all_to_all x3, starting transfers between devices, exchange(): lax.all_to_all(blocks, 'expert', split_axis=0, concat_axis=0, tiled=True)  17.6 us
    ppermute x11, starting transfers between devices, swap_cores(): return lax.ppermute(value, 'dp', [(0, 1), (1, 0)])  14.3 us
    ppermute x11, waiting for transfers between devices, swap_cores(): return lax.ppermute(value, 'dp', [(0, 1), (1, 0)])  12.7 us
    pallas_call x2, Pallas kernels, partial_products(): pl.pallas_call(functools.partial(partial_kernel, dims, chunk, pick), out_...  12.3 us
    ppermute x5, waiting for transfers between devices, swap_holders(): lax.ppermute(value, 'expert', [(source, source ^ mask) for source in rang...  11.6 us
    pallas_call x2, Pallas kernels, output_products(): pl.pallas_call(functools.partial(output_kernel, dims, chunk), out_shape=(...  10.9 us
    unnamed x27, local copies, waits for them, and re-layouts  10.9 us
    all_to_all x3, waiting for transfers between devices, exchange(): lax.all_to_all(blocks, 'expert', split_axis=0, concat_axis=0, tiled=True)  9.36 us
  transfers between devices with their start and end apart: 20, of which 16 were waited for; matrix products, arithmetic and copies ran while one was open for 4% of the time, Pallas kernels for 31%

profile of v5, /device:TPU:17, one launch (start us, length us, event | category | flops | bytes accessed | tf_op | source)
XLA Modules:
  0.0 152.9 jit_solution(16448343082695956723)
XLA Ops:
  0.6 3.5 %dispatch_0.1 = bf16[8,2,40,768]{3,2,1,0:T(8,128)(2,1)} custom-call(s32[2,128]{1,0:T(2,128)} %bitcast.43, f32[2,128]{1,0:T(2,128)} %bitcast.44, bf16[128,3072]{1,0:T(8,128)(2,1)} %tokens.1, bf16[128,3072]{1,0:T(8,128)(2,1)} %cotangent.3), custom_call_target="tpu_custom_call" | custom-call | flops 2516582 | bytes 17694 | tf_op jit(solution)/shard_map/dispatch_0/pallas_call | solution.py:165
  4.2 6.6 %all-to-all-start.1 = ((bf16[16,40,768]{2,1,0:T(8,128)(2,1)}), bf16[16,40,768]{2,1,0:T(8,128)(2,1)S(1)}, u32[]{:S(2)}, u32[]{:S(2)}) async-start(bf16[16,40,768]{2,1,0:T(8,128)(2,1)} %bitcast.40), calls=%async_computation.1 | async-start | bytes 1966080 | tf_op jit(solution)/shard_map/all_to_all | solution.py:782
  18.1 2.8 %choosers.1 = (f32[128,2]{1,0:T(8,128)S(1)}, bf16[2,384,640]{2,1,0:T(8,128)(2,1)}, bf16[2,384,640]{2,1,0:T(8,128)(2,1)}) custom-call(s32[2]{0:T(128)S(1)} %pad_add_fusion.ids, s32[128,2]{1,0:T(8,128)S(1)} %copy.14.routes, f32[128,2]{1,0:T(8,128)S(1)} %copy.15.gates, s32[8,640]{1,0:T(8,128)S(1)} %copy-done.8), custom_call_target="tpu_custom_call" | custom-call | bytes 19660 | tf_op jit(solution)/shard_map/choosers/pallas_call | solution.py:466
  20.9 4.5 %collective-permute-done.refs_1_ = f32[4,128]{1,0:T(4,128)S(1)} collective-permute-done((f32[4,128]{1,0:T(4,128)S(1)}, f32[4,128]{1,0:T(4,128)S(1)}, u32[]{:S(2)}, u32[]{:S(2)}) %collective-permute-start) | collective-permute-done | bytes 2080 | tf_op jit(solution)/shard_map/ppermute | solution.py:758
  26.7 3.1 %group_dispatch_1.1 = bf16[8,2,40,768]{3,2,1,0:T(8,128)(2,1)} custom-call(f32[4,128]{1,0:T(4,128)} %copy-done.10, f32[4,128]{1,0:T(4,128)} %copy-done.11, bf16[2,128,768]{2,1,0:T(8,128)(2,1)} %pad_maximum_fusion.refs_2_, bf16[2,128,768]{2,1,0:T(8,128)(2,1)} %copy-done.9), custom_call_target="tpu_custom_call" | custom-call | flops 2516582 | bytes 17694 | tf_op jit(solution)/shard_map/group_dispatch_1/pallas_call | solution.py:132
  29.7 3.6 %all-to-all-done.1 = bf16[16,40,768]{2,1,0:T(8,128)(2,1)S(1)} async-done(((bf16[16,40,768]{2,1,0:T(8,128)(2,1)}), bf16[16,40,768]{2,1,0:T(8,128)(2,1)S(1)}, u32[]{:S(2)}, u32[]{:S(2)}) %all-to-all-start.1) | async-done | bytes 983072 | tf_op jit(solution)/shard_map/all_to_all | solution.py:782
  33.3 5.4 %all-to-all-start = ((bf16[8,80,768]{2,1,0:T(8,128)(2,1)}), bf16[8,80,768]{2,1,0:T(8,128)(2,1)S(1)}, u32[]{:S(2)}, u32[]{:S(2)}) async-start(bf16[8,80,768]{2,1,0:T(8,128)(2,1)} %bitcast.39), calls=%async_computation | async-start | bytes 1966080 | tf_op jit(solution)/shard_map/all_to_all | solution.py:806
  38.8 3.7 %collective-permute-start.3 = (bf16[320,768]{1,0:T(8,128)(2,1)S(1)}, bf16[320,768]{1,0:T(8,128)(2,1)S(1)}, u32[]{:S(2)}, u32[]{:S(2)}) collective-permute-start(bf16[320,768]{1,0:T(8,128)(2,1)S(1)} %get-tuple-element.102), channel_id=1, source_target_pairs={{0,16},{16,0},{1,17},{17,1},{2,18},{18,2},{3,19},{19,3},{4,20},{20... | collective-permute-start | bytes 1474568 | tf_op jit(solution)/shard_map/ppermute | solution.py:753
  44.7 5.8 %partial_0.1 = (bf16[1,2,2,320,768]{4,3,2,1,0:T(8,128)(2,1)}, bf16[1,320,1536]{2,1,0:T(8,128)(2,1)S(1)}, bf16[2,320,768]{2,1,0:T(8,128)(2,1)}) custom-call(s32[2]{0:T(128)S(1)} %pad_add_fusion.ids, bf16[640,768]{1,0:T(8,128)(2,1)S(1)} %bitcast.30, bf16[320,768]{1,0:T(8,128)(2,1)S(1)} %collective-permute-done.2.other_low, ...), custom_call_target="tpu_custom_call" | custom-call | flops 27682406 | bytes 96337 | tf_op jit(solution)/shard_map/partial_0/pallas_call | solution.py:275
  51.2 7.4 %all-to-all-done = bf16[8,80,768]{2,1,0:T(8,128)(2,1)S(1)} async-done(((bf16[8,80,768]{2,1,0:T(8,128)(2,1)}), bf16[8,80,768]{2,1,0:T(8,128)(2,1)S(1)}, u32[]{:S(2)}, u32[]{:S(2)}) %all-to-all-start) | async-done | bytes 983072 | tf_op jit(solution)/shard_map/all_to_all | solution.py:806
  58.7 2.9 %collective-permute-start.5 = (bf16[320,768]{1,0:T(8,128)(2,1)S(1)}, bf16[320,768]{1,0:T(8,128)(2,1)S(1)}, u32[]{:S(2)}, u32[]{:S(2)}) collective-permute-start(bf16[320,768]{1,0:T(8,128)(2,1)S(1)} %get-tuple-element.100), channel_id=1, source_target_pairs={{0,16},{16,0},{1,17},{17,1},{2,18},{18,2},{3,19},{19,3},{4,20},{20... | collective-permute-start | bytes 1474568 | tf_op jit(solution)/shard_map/ppermute | solution.py:753
  63.7 6.5 %partial_1.1 = (bf16[1,2,2,320,768]{4,3,2,1,0:T(8,128)(2,1)}, bf16[1,320,1536]{2,1,0:T(8,128)(2,1)}, bf16[2,320,768]{2,1,0:T(8,128)(2,1)}) custom-call(s32[2]{0:T(128)S(1)} %pad_add_fusion.ids, bf16[640,768]{1,0:T(8,128)(2,1)S(1)} %bitcast.32, bf16[320,768]{1,0:T(8,128)(2,1)S(1)} %collective-permute-done.4.other_low, ...), custom_call_target="tpu_custom_call", output_to_operand_aliasing={{2}: (5, {})} | custom-call | flops 27682406 | bytes 96337 | tf_op jit(solution)/shard_map/partial_1/pallas_call | solution.py:275
  70.3 3.2 %collective-permute-done.7.theirs = bf16[1,320,1536]{2,1,0:T(8,128)(2,1)S(1)} collective-permute-done((bf16[1,320,1536]{2,1,0:T(8,128)(2,1)S(1)}, bf16[1,320,1536]{2,1,0:T(8,128)(2,1)S(1)}, u32[]{:S(2)}, u32[]{:S(2)}) %collective-permute-start.7) | collective-permute-done | bytes 983072 | tf_op jit(solution)/shard_map/ppermute | solution.py:758
  73.5 5.1 %output_0.1 = (bf16[1,320,1536]{2,1,0:T(8,128)(2,1)}, bf16[1,320,768]{2,1,0:T(8,128)(2,1)S(1)}, bf16[1,320,768]{2,1,0:T(8,128)(2,1)S(1)}, bf16[1,320,768]{2,1,0:T(8,128)(2,1)S(1)}, bf16[1,320,768]{2,1,0:T(8,128)(2,1)S(1)}) custom-call(s32[2]{0:T(128)S(1)} %pad_add_fusion.ids, bf16[1,320,1536]{2,1,0:T(8,128)(2,1)S(1)} %get-tuple-element.60.mine, ...), custom_call_target="tpu_custom_call" | custom-call | flops 45298483200 | bytes 289013760 | tf_op jit(solution)/shard_map/output_0/pallas_call | solution.py:358
  84.8 5.8 %all-to-all-start.2 = ((bf16[16,40,768]{2,1,0:T(8,128)(2,1)}), bf16[16,40,768]{2,1,0:T(8,128)(2,1)S(1)}, u32[]{:S(2)}, u32[]{:S(2)}) async-start(bf16[16,40,768]{2,1,0:T(8,128)(2,1)} %bitcast.41), calls=%async_computation.2 | async-start | bytes 1966080 | tf_op jit(solution)/shard_map/all_to_all | solution.py:782
  90.6 4.0 %collective-permute-done.6.theirs = bf16[1,320,1536]{2,1,0:T(8,128)(2,1)S(1)} collective-permute-done((bf16[1,320,1536]{2,1,0:T(8,128)(2,1)}, bf16[1,320,1536]{2,1,0:T(8,128)(2,1)S(1)}, u32[]{:S(2)}, u32[]{:S(2)}) %collective-permute-start.6) | collective-permute-done | bytes 983072 | tf_op jit(solution)/shard_map/ppermute | solution.py:758
  95.2 5.8 %output_1.1 = (bf16[1,320,1536]{2,1,0:T(8,128)(2,1)}, bf16[1,320,768]{2,1,0:T(8,128)(2,1)S(1)}, bf16[1,320,768]{2,1,0:T(8,128)(2,1)S(1)}, bf16[1,320,768]{2,1,0:T(8,128)(2,1)S(1)}, bf16[1,320,768]{2,1,0:T(8,128)(2,1)S(1)}) custom-call(s32[2]{0:T(128)S(1)} %pad_add_fusion.ids, bf16[1,320,1536]{2,1,0:T(8,128)(2,1)} %get-tuple-element.63.mine, ...), custom_call_target="tpu_custom_call" | custom-call | flops 45298483200 | bytes 289013760 | tf_op jit(solution)/shard_map/output_1/pallas_call | solution.py:358
  107.5 5.8 %all-to-all-done.2 = bf16[16,40,768]{2,1,0:T(8,128)(2,1)S(1)} async-done(((bf16[16,40,768]{2,1,0:T(8,128)(2,1)}), bf16[16,40,768]{2,1,0:T(8,128)(2,1)S(1)}, u32[]{:S(2)}, u32[]{:S(2)}) %all-to-all-start.2) | async-done | bytes 983072 | tf_op jit(solution)/shard_map/all_to_all | solution.py:782
  113.2 5.2 %all-to-all-start.3 = ((bf16[16,40,768]{2,1,0:T(8,128)(2,1)}), bf16[16,40,768]{2,1,0:T(8,128)(2,1)}, u32[]{:S(2)}, u32[]{:S(2)}) async-start(bf16[16,40,768]{2,1,0:T(8,128)(2,1)} %bitcast.42), calls=%async_computation.3 | async-start | bytes 1966080 | tf_op jit(solution)/shard_map/all_to_all | solution.py:782
  122.7 5.8 %near_weight_grads.1.refs_4_ = bf16[3,3072,512]{2,1,0:T(8,128)(2,1)} custom-call(s32[2]{0:T(128)S(1)} %pad_add_fusion.ids, bf16[1,320,1536]{2,1,0:T(8,128)(2,1)S(1)} %copy-done.1, bf16[1,320,1536]{2,1,0:T(8,128)(2,1)S(1)} %copy-done.3, bf16[1,2,2,320,768]{4,3,2,1,0:T(8,128)(2,1)S(1)} %copy-done.4, bf16[1,2,2,320,768]{4,3,2,1,0:T(8,128)(2,1)S(1)} %copy-done.5), custom_call_target="tpu_custom_call" | custom-call | flops 15099494 | bytes 66846 | tf_op jit(solution)/shard_map/near_weight_grads/pallas_call | solution.py:669
  131.6 2.4 %collective-permute-start.13 = (bf16[2,320,768]{2,1,0:T(8,128)(2,1)}, bf16[2,320,768]{2,1,0:T(8,128)(2,1)S(1)}, u32[]{:S(2)}, u32[]{:S(2)}) collective-permute-start(bf16[2,320,768]{2,1,0:T(8,128)(2,1)} %collective-permute-done.12.refs_2_), channel_id=1, source_target_pairs={{0,16},{16,0},{1,17},{17,1},{2,18},{18,2},{3,19},{19,3},{4,20},{20... | collective-permute-start | bytes 2949128 | tf_op jit(solution)/shard_map/ppermute | solution.py:753
  134.0 2.4 %collective-permute-done.13.refs_3_ = bf16[2,320,768]{2,1,0:T(8,128)(2,1)S(1)} collective-permute-done((bf16[2,320,768]{2,1,0:T(8,128)(2,1)}, bf16[2,320,768]{2,1,0:T(8,128)(2,1)S(1)}, u32[]{:S(2)}, u32[]{:S(2)}) %collective-permute-start.13) | collective-permute-done | bytes 983072 | tf_op jit(solution)/shard_map/ppermute | solution.py:753
  136.4 6.4 %far_weight_grads.1 = bf16[3,3072,512]{2,1,0:T(8,128)(2,1)} custom-call(s32[2]{0:T(128)S(1)} %pad_add_fusion.ids, bf16[1,320,1536]{2,1,0:T(8,128)(2,1)S(1)} %copy-done.2, bf16[1,320,1536]{2,1,0:T(8,128)(2,1)S(1)} %copy-done.3, bf16[2,320,768]{2,1,0:T(8,128)(2,1)} %collective-permute-done.12.refs_2_, ...), custom_call_target="tpu_custom_call", output_to_operand_aliasing={{}: (5, {})} | custom-call | flops 6039797760 | bytes 26738688 | tf_op jit(solution)/shard_map/far_weight_grads/pallas_call | solution.py:719
  144.1 4.2 %combine.1 = (bf16[2,2,128,768]{3,2,1,0:T(8,128)(2,1)}, f32[128,128]{1,0:T(8,128)S(1)}, bf16[128,3072]{1,0:T(8,128)(2,1)}, bf16[128,3072]{1,0:T(8,128)(2,1)}) custom-call(s32[2]{0:T(128)S(1)} %pad_add_fusion.ids, f32[128,2]{1,0:T(8,128)S(1)} %get-tuple-element.55.gates, bf16[128,3072]{1,0:T(8,128)(2,1)S(1)} %copy-done, bf16[2,384,640]{2,1,0:T(8,128)(2,1)S(1)} %copy-done.6, ...), custom_call_target="tpu_custom_call" | custom-call | flops 7549747 | bytes 19660 | tf_op jit(solution)/shard_map/combine/pallas_call | solution.py:540
  (66 shorter events, 40.2 us)
Async XLA Ops:
  4.2 29.1 %all-to-all-start.1 = ((bf16[16,40,768]{2,1,0:T(8,128)(2,1)}), bf16[16,40,768]{2,1,0:T(8,128)(2,1)S(1)}, u32[]{:S(2)}, u32[]{:S(2)}) async-start(bf16[16,40,768]{2,1,0:T(8,128)(2,1)} %bitcast.40), calls=%async_computation.1 | async-start | bytes 1966080 | tf_op jit(solution)/shard_map/all_to_all | solution.py:782
  12.1 13.3 %collective-permute-start.1 = (bf16[2,128,768]{2,1,0:T(8,128)(2,1)S(1)}, bf16[2,128,768]{2,1,0:T(8,128)(2,1)S(1)}, u32[]{:S(2)}, u32[]{:S(2)}) collective-permute-start(bf16[2,128,768]{2,1,0:T(8,128)(2,1)S(1)} %pad_maximum_fusion.1), channel_id=1, source_target_pairs={{0,1},{1,0},{2,3},{3,2},{4,5},{5,4},{6,7},{7,6},{8,9},{9,8},{10,11... | collective-permute-start | bytes 1179656 | tf_op jit(solution)/shard_map/ppermute | solution.py:758
  14.7 10.7 %copy-start.10 = (f32[4,128]{1,0:T(4,128)}, f32[4,128]{1,0:T(4,128)S(1)}, u32[]{:S(2)}) copy-start(f32[4,128]{1,0:T(4,128)S(1)} %pad_maximum_fusion.2.refs_0_) | copy-start | bytes 6148
  14.7 10.7 %collective-permute-start = (f32[4,128]{1,0:T(4,128)S(1)}, f32[4,128]{1,0:T(4,128)S(1)}, u32[]{:S(2)}, u32[]{:S(2)}) collective-permute-start(f32[4,128]{1,0:T(4,128)S(1)} %pad_maximum_fusion.2.refs_0_), channel_id=1, source_target_pairs={{0,1},{1,0},{2,3},{3,2},{4,5},{5,4},{6,7},{7,6},{8,9},{9,8},{10,11... | collective-permute-start | bytes 6152 | tf_op jit(solution)/shard_map/ppermute | solution.py:758
  33.3 25.3 %all-to-all-start = ((bf16[8,80,768]{2,1,0:T(8,128)(2,1)}), bf16[8,80,768]{2,1,0:T(8,128)(2,1)S(1)}, u32[]{:S(2)}, u32[]{:S(2)}) async-start(bf16[8,80,768]{2,1,0:T(8,128)(2,1)} %bitcast.39), calls=%async_computation | async-start | bytes 1966080 | tf_op jit(solution)/shard_map/all_to_all | solution.py:806
  38.8 5.2 %collective-permute-start.3 = (bf16[320,768]{1,0:T(8,128)(2,1)S(1)}, bf16[320,768]{1,0:T(8,128)(2,1)S(1)}, u32[]{:S(2)}, u32[]{:S(2)}) collective-permute-start(bf16[320,768]{1,0:T(8,128)(2,1)S(1)} %get-tuple-element.102), channel_id=1, source_target_pairs={{0,16},{16,0},{1,17},{17,1},{2,18},{18,2},{3,19},{19,3},{4,20},{20... | collective-permute-start | bytes 1474568 | tf_op jit(solution)/shard_map/ppermute | solution.py:753
  42.5 2.2 %collective-permute-start.2 = (bf16[320,768]{1,0:T(8,128)(2,1)S(1)}, bf16[320,768]{1,0:T(8,128)(2,1)S(1)}, u32[]{:S(2)}, u32[]{:S(2)}) collective-permute-start(bf16[320,768]{1,0:T(8,128)(2,1)S(1)} %get-tuple-element.103), channel_id=1, source_target_pairs={{0,16},{16,0},{1,17},{17,1},{2,18},{18,2},{3,19},{19,3},{4,20},{20... | collective-permute-start | bytes 1474568 | tf_op jit(solution)/shard_map/ppermute | solution.py:753
  50.5 23.0 %collective-permute-start.7 = (bf16[1,320,1536]{2,1,0:T(8,128)(2,1)S(1)}, bf16[1,320,1536]{2,1,0:T(8,128)(2,1)S(1)}, u32[]{:S(2)}, u32[]{:S(2)}) collective-permute-start(bf16[1,320,1536]{2,1,0:T(8,128)(2,1)S(1)} %get-tuple-element.60.mine), channel_id=1, source_target_pairs={{0,1},{1,0},{2,3},{3,2},{4,5},{5,4},{6,7},{7,6},{8,9},{9,8},{10,11... | collective-permute-start | bytes 2949128 | tf_op jit(solution)/shard_map/ppermute | solution.py:758
  58.7 4.4 %collective-permute-start.5 = (bf16[320,768]{1,0:T(8,128)(2,1)S(1)}, bf16[320,768]{1,0:T(8,128)(2,1)S(1)}, u32[]{:S(2)}, u32[]{:S(2)}) collective-permute-start(bf16[320,768]{1,0:T(8,128)(2,1)S(1)} %get-tuple-element.100), channel_id=1, source_target_pairs={{0,16},{16,0},{1,17},{17,1},{2,18},{18,2},{3,19},{19,3},{4,20},{20... | collective-permute-start | bytes 1474568 | tf_op jit(solution)/shard_map/ppermute | solution.py:753
  61.5 2.2 %collective-permute-start.4 = (bf16[320,768]{1,0:T(8,128)(2,1)S(1)}, bf16[320,768]{1,0:T(8,128)(2,1)S(1)}, u32[]{:S(2)}, u32[]{:S(2)}) collective-permute-start(bf16[320,768]{1,0:T(8,128)(2,1)S(1)} %get-tuple-element.101), channel_id=1, source_target_pairs={{0,16},{16,0},{1,17},{17,1},{2,18},{18,2},{3,19},{19,3},{4,20},{20... | collective-permute-start | bytes 1474568 | tf_op jit(solution)/shard_map/ppermute | solution.py:753
  70.2 24.3 %collective-permute-start.6 = (bf16[1,320,1536]{2,1,0:T(8,128)(2,1)}, bf16[1,320,1536]{2,1,0:T(8,128)(2,1)S(1)}, u32[]{:S(2)}, u32[]{:S(2)}) collective-permute-start(bf16[1,320,1536]{2,1,0:T(8,128)(2,1)} %get-tuple-element.63.mine), channel_id=1, source_target_pairs={{0,1},{1,0},{2,3},{3,2},{4,5},{5,4},{6,7},{7,6},{8,9},{9,8},{10,11... | collective-permute-start | bytes 2949128 | tf_op jit(solution)/shard_map/ppermute | solution.py:758
  78.6 3.6 %collective-permute-start.8 = (bf16[1,320,768]{2,1,0:T(8,128)(2,1)S(1)}, bf16[1,320,768]{2,1,0:T(8,128)(2,1)S(1)}, u32[]{:S(2)}, u32[]{:S(2)}) collective-permute-start(bf16[1,320,768]{2,1,0:T(8,128)(2,1)S(1)} %get-tuple-element.68), channel_id=1, source_target_pairs={{0,16},{16,0},{1,17},{17,1},{2,18},{18,2},{3,19},{19,3},{4,20},{20... | collective-permute-start | bytes 1474568 | tf_op jit(solution)/shard_map/ppermute | solution.py:753
  80.7 2.2 %collective-permute-start.9 = (bf16[1,320,768]{2,1,0:T(8,128)(2,1)S(1)}, bf16[1,320,768]{2,1,0:T(8,128)(2,1)S(1)}, u32[]{:S(2)}, u32[]{:S(2)}) collective-permute-start(bf16[1,320,768]{2,1,0:T(8,128)(2,1)S(1)} %get-tuple-element.69), channel_id=1, source_target_pairs={{0,16},{16,0},{1,17},{17,1},{2,18},{18,2},{3,19},{19,3},{4,20},{20... | collective-permute-start | bytes 1474568 | tf_op jit(solution)/shard_map/ppermute | solution.py:753
  84.8 28.5 %all-to-all-start.2 = ((bf16[16,40,768]{2,1,0:T(8,128)(2,1)}), bf16[16,40,768]{2,1,0:T(8,128)(2,1)S(1)}, u32[]{:S(2)}, u32[]{:S(2)}) async-start(bf16[16,40,768]{2,1,0:T(8,128)(2,1)} %bitcast.41), calls=%async_computation.2 | async-start | bytes 1966080 | tf_op jit(solution)/shard_map/all_to_all | solution.py:782
  90.5 27.9 %copy-start.1 = (bf16[1,320,1536]{2,1,0:T(8,128)(2,1)S(1)}, bf16[1,320,1536]{2,1,0:T(8,128)(2,1)}, u32[]{:S(2)}) copy-start(bf16[1,320,1536]{2,1,0:T(8,128)(2,1)} %get-tuple-element.78.refs_0_) | copy-start | bytes 2949124
  94.6 37.0 %collective-permute-start.12 = (bf16[2,320,768]{2,1,0:T(8,128)(2,1)}, bf16[2,320,768]{2,1,0:T(8,128)(2,1)}, u32[]{:S(2)}, u32[]{:S(2)}) collective-permute-start(bf16[2,320,768]{2,1,0:T(8,128)(2,1)} %get-tuple-element.77), channel_id=1, source_target_pairs={{0,1},{1,0},{2,3},{3,2},{4,5},{5,4},{6,7},{7,6},{8,9},{9,8},{10,11... | collective-permute-start | bytes 2949128 | tf_op jit(solution)/shard_map/ppermute | solution.py:758
  101.1 3.8 %collective-permute-start.10 = (bf16[1,320,768]{2,1,0:T(8,128)(2,1)S(1)}, bf16[1,320,768]{2,1,0:T(8,128)(2,1)S(1)}, u32[]{:S(2)}, u32[]{:S(2)}) collective-permute-start(bf16[1,320,768]{2,1,0:T(8,128)(2,1)S(1)} %get-tuple-element.73), channel_id=1, source_target_pairs={{0,16},{16,0},{1,17},{17,1},{2,18},{18,2},{3,19},{19,3},{4,20},{20... | collective-permute-start | bytes 1474568 | tf_op jit(solution)/shard_map/ppermute | solution.py:753
  103.4 2.2 %collective-permute-start.11 = (bf16[1,320,768]{2,1,0:T(8,128)(2,1)S(1)}, bf16[1,320,768]{2,1,0:T(8,128)(2,1)S(1)}, u32[]{:S(2)}, u32[]{:S(2)}) collective-permute-start(bf16[1,320,768]{2,1,0:T(8,128)(2,1)S(1)} %get-tuple-element.74), channel_id=1, source_target_pairs={{0,16},{16,0},{1,17},{17,1},{2,18},{18,2},{3,19},{19,3},{4,20},{20... | collective-permute-start | bytes 1474568 | tf_op jit(solution)/shard_map/ppermute | solution.py:753
  113.2 29.6 %all-to-all-start.3 = ((bf16[16,40,768]{2,1,0:T(8,128)(2,1)}), bf16[16,40,768]{2,1,0:T(8,128)(2,1)}, u32[]{:S(2)}, u32[]{:S(2)}) async-start(bf16[16,40,768]{2,1,0:T(8,128)(2,1)} %bitcast.42), calls=%async_computation.3 | async-start | bytes 1966080 | tf_op jit(solution)/shard_map/all_to_all | solution.py:782
  122.7 13.7 %copy-start.2 = (bf16[1,320,1536]{2,1,0:T(8,128)(2,1)S(1)}, bf16[1,320,1536]{2,1,0:T(8,128)(2,1)}, u32[]{:S(2)}) copy-start(bf16[1,320,1536]{2,1,0:T(8,128)(2,1)} %get-tuple-element.78.refs_0_) | copy-start | bytes 2949124
  131.6 11.3 %copy-start = (bf16[128,3072]{1,0:T(8,128)(2,1)S(1)}, bf16[128,3072]{1,0:T(8,128)(2,1)}, u32[]{:S(2)}) copy-start(bf16[128,3072]{1,0:T(8,128)(2,1)} %cotangent.3) | copy-start | bytes 2359300
  131.6 4.8 %collective-permute-start.13 = (bf16[2,320,768]{2,1,0:T(8,128)(2,1)}, bf16[2,320,768]{2,1,0:T(8,128)(2,1)S(1)}, u32[]{:S(2)}, u32[]{:S(2)}) collective-permute-start(bf16[2,320,768]{2,1,0:T(8,128)(2,1)} %collective-permute-done.12.refs_2_), channel_id=1, source_target_pairs={{0,16},{16,0},{1,17},{17,1},{2,18},{18,2},{3,19},{19,3},{4,20},{20... | collective-permute-start | bytes 2949128 | tf_op jit(solution)/shard_map/ppermute | solution.py:753
  148.3 3.0 %collective-permute-start.14 = (bf16[2,2,128,768]{3,2,1,0:T(8,128)(2,1)}, bf16[2,2,128,768]{3,2,1,0:T(8,128)(2,1)S(1)}, u32[]{:S(2)}, u32[]{:S(2)}) collective-permute-start(bf16[2,2,128,768]{3,2,1,0:T(8,128)(2,1)} %get-tuple-element.89), channel_id=1, source_target_pairs={{0,16},{16,0},{1,17},{17,1},{2,18},{18,2},{3,19},{19,3},{4,20},{20... | collective-permute-start | bytes 2359304 | tf_op jit(solution)/shard_map/ppermute | solution.py:753
  148.6 2.0 %collective-permute-start.15 = (f32[128,128]{1,0:T(8,128)S(1)}, f32[128,128]{1,0:T(8,128)S(1)}, u32[]{:S(2)}, u32[]{:S(2)}) collective-permute-start(f32[128,128]{1,0:T(8,128)S(1)} %get-tuple-element.94), channel_id=1, source_target_pairs={{0,16},{16,0},{1,17},{17,1},{2,18},{18,2},{3,19},{19,3},{4,20},{20... | collective-permute-start | bytes 196616 | tf_op jit(solution)/shard_map/ppermute | solution.py:753
  (8 other events, 8.7 us)
